TPU v7x, 32 devices: a whole 2x2x4 slice. The times are simulated.
32 devices in a mesh: grp: 2 (over core), seq: 4 (over z), mdl: 4 (over y, x).
Axes of the slice: x: 2, y: 2, z: 4, core: 2. Of those that a mesh axis runs over, the one named last changes fastest.
Arguments:
- queries: bfloat16 [512, 8, 2048], P(('grp', 'seq'), None, 'mdl'), may hold values from -7 to 7
- out_grads: bfloat16 [512, 8, 2048], P(('grp', 'seq'), None, 'mdl'), may hold values from -12 to 12
- owners: int32 [512], P(('grp', 'seq')), may hold values from 0 to 7, as said below
- src_keys: bfloat16 [8, 512, 2048], P(('grp', 'seq'), None, 'mdl'), may hold values from -7 to 7
- src_values: bfloat16 [8, 512, 2048], P(('grp', 'seq'), None, 'mdl'), may hold values from -6 to 6
- states: bfloat16 [8, 512, 2048], P(('grp', 'seq'), None, 'mdl'), may hold values from -0.59765625 to 0.59765625
- kv_weight: bfloat16 [2048, 2, 2048], P(('grp', 'seq'), None, 'mdl'), may hold values from -0.125 to 0.125
- src_lengths: int32 [8], P(('grp', 'seq')), may hold values from 128 to 512, as said below
Outputs:
- query_grads: bfloat16 [512, 8, 2048], P(('grp', 'seq'), None, 'mdl')
- state_grads: bfloat16 [8, 512, 2048], P(('grp', 'seq'), None, 'mdl')
- weight_grads: float32 [2048, 2, 2048], P(('grp', 'seq'), None, 'mdl')
Inputs may be any that keep to these rules, and one draw needn't show every extreme that they name: `owners`: the 64 targets of each index of grp and seq (an aligned block) name any one source at most 16 times; one source, the same for every block, is named exactly 16 times by every block. `src_lengths`: each length is a multiple of 128; the largest is 512.
All inputs are finite; a program needn't handle non-finite values.
Results may differ from a plain program's by a relative error of at most 0.012.
Values may be sent and summed in bfloat16 or wider, within the bound.
No kernel may reach another device: no remote copies, remote signals or barrier semaphores. Data moves between devices by JAX's collectives and lax.ppermute only.
A program may use at most 64 MiB of HBM per device.

v0:
```python
import jax
import jax.numpy as jnp
from jax import lax
from jax.sharding import PartitionSpec as P

HEAD_DIM = 64


def block_grads(query_block, grad_block, key_local, value_local, key_valid):
    score_scale = key_local.shape[-1] ** (-0.5)
    scores = (
        jnp.einsum("rhe,khe->hrk", query_block, key_local, preferred_element_type=jnp.float32)
        * score_scale
    )
    scores = jnp.where(key_valid[None, None, :], scores, -1e30)
    row_peak = jnp.max(scores, axis=-1, keepdims=True)
    exp_terms = jnp.exp(scores - row_peak)
    attn_probs = exp_terms / jnp.sum(exp_terms, axis=-1, keepdims=True)
    probs_b = attn_probs.astype(jnp.bfloat16)
    context = jnp.einsum("hrk,khe->rhe", probs_b, value_local, preferred_element_type=jnp.float32)
    row_delta = jnp.sum(grad_block.astype(jnp.float32) * context, axis=-1)
    prob_grad = jnp.einsum(
        "rhe,khe->hrk", grad_block, value_local, preferred_element_type=jnp.float32
    )
    score_grad = (attn_probs * (prob_grad - row_delta.T[:, :, None]) * score_scale).astype(
        jnp.bfloat16
    )
    query_grad = jnp.einsum(
        "hrk,khe->rhe", score_grad, key_local, preferred_element_type=jnp.float32
    ).astype(jnp.bfloat16)
    key_grad = jnp.einsum(
        "hrk,rhe->khe", score_grad, query_block, preferred_element_type=jnp.float32
    )
    value_grad = jnp.einsum("hrk,rhe->khe", probs_b, grad_block, preferred_element_type=jnp.float32)
    return (query_grad, key_grad, value_grad)


def on_device(queries, out_grads, owners, src_keys, src_values, states, kv_weight, src_lengths):
    peer_count = lax.axis_size(("grp", "seq"))
    tgt_dev, tgt_len, inner_dev = queries.shape
    per_peer = max(2, 2 * tgt_dev // peer_count)
    slot_count = peer_count * per_peer
    row_width = tgt_len * inner_dev
    head_dim = HEAD_DIM
    local_heads = inner_dev // head_dim
    src_len = src_keys.shape[1]
    member = (owners[:, None] == jnp.arange(peer_count, dtype=jnp.int32)[None, :]).astype(jnp.int32)
    earlier = jnp.cumsum(member, axis=0) - member
    rank_own = jnp.sum(earlier * member, axis=1)
    slot_of = owners * per_peer + rank_own
    selector = (jnp.arange(slot_count, dtype=jnp.int32)[:, None] == slot_of[None, :]).astype(
        jnp.bfloat16
    )
    send_query = jnp.dot(
        selector, queries.reshape(tgt_dev, row_width), preferred_element_type=jnp.float32
    ).astype(jnp.bfloat16)
    send_grad = jnp.dot(
        selector, out_grads.reshape(tgt_dev, row_width), preferred_element_type=jnp.float32
    ).astype(jnp.bfloat16)
    got_query, got_grad = (
        lax.all_to_all(send_query, ("grp", "seq"), split_axis=0, concat_axis=0, tiled=True),
        lax.all_to_all(send_grad, ("grp", "seq"), split_axis=0, concat_axis=0, tiled=True),
    )
    total_rows = slot_count * tgt_len
    block_rows = 512
    block_count = total_rows // block_rows
    query_rows = got_query.reshape(block_count, block_rows, local_heads, head_dim)
    grad_rows = got_grad.reshape(block_count, block_rows, local_heads, head_dim)
    key_local = src_keys[0].reshape(src_len, local_heads, head_dim)
    value_local = src_values[0].reshape(src_len, local_heads, head_dim)
    key_valid = jnp.arange(src_len, dtype=jnp.int32) < src_lengths[0]

    def attend_step(totals, block_pair):
        query_grad, key_grad, value_grad = block_grads(
            block_pair[0], block_pair[1], key_local, value_local, key_valid
        )
        return ((totals[0] + key_grad, totals[1] + value_grad), query_grad)

    zero_grads = jnp.zeros((src_len, local_heads, head_dim), jnp.float32)
    (key_total, value_total), query_blocks = lax.scan(
        attend_step, (zero_grads, zero_grads), (query_rows, grad_rows)
    )
    back_rows = query_blocks.reshape(slot_count, row_width)
    returned = lax.all_to_all(back_rows, ("grp", "seq"), split_axis=0, concat_axis=0, tiled=True)
    query_out = lax.dot_general(
        selector, returned, (((0,), (0,)), ((), ())), preferred_element_type=jnp.float32
    )
    query_out = query_out.astype(jnp.bfloat16).reshape(tgt_dev, tgt_len, inner_dev)
    key_bf = key_total.reshape(src_len, inner_dev).astype(jnp.bfloat16)
    value_bf = value_total.reshape(src_len, inner_dev).astype(jnp.bfloat16)
    key_all, value_all = (
        lax.all_gather(key_bf, "mdl", axis=1, tiled=True),
        lax.all_gather(value_bf, "mdl", axis=1, tiled=True),
    )
    weight_piece = lax.all_gather(kv_weight, ("grp", "seq"), axis=0, tiled=True)
    key_cols = key_all
    value_cols = value_all
    total = jnp.dot(key_cols, weight_piece[:, 0, :], preferred_element_type=jnp.float32)
    state_sum = total + jnp.dot(
        value_cols, weight_piece[:, 1, :], preferred_element_type=jnp.float32
    )
    state_out = state_sum.astype(jnp.bfloat16).reshape(1, src_len, kv_weight.shape[2])
    flat_states = states.reshape(src_len, states.shape[2])
    key_cols = key_all
    value_cols = value_all
    grad_key = lax.dot_general(
        key_cols, flat_states, (((0,), (0,)), ((), ())), preferred_element_type=jnp.float32
    )
    grad_value = lax.dot_general(
        value_cols, flat_states, (((0,), (0,)), ((), ())), preferred_element_type=jnp.float32
    )
    weight_out = lax.psum_scatter(
        jnp.stack([grad_key, grad_value], axis=1), ("grp", "seq"), scatter_dimension=0, tiled=True
    )
    return (query_out, state_out, weight_out)


def solution(mesh):
    in_specs = (
        P(("grp", "seq"), None, "mdl"),
        P(("grp", "seq"), None, "mdl"),
        P(("grp", "seq")),
        P(("grp", "seq"), None, "mdl"),
        P(("grp", "seq"), None, "mdl"),
        P(("grp", "seq"), None, "mdl"),
        P(("grp", "seq"), None, "mdl"),
        P(("grp", "seq")),
    )
    out_specs = (
        P(("grp", "seq"), None, "mdl"),
        P(("grp", "seq"), None, "mdl"),
        P(("grp", "seq"), None, "mdl"),
    )
    return jax.shard_map(
        on_device, mesh=mesh, in_specs=in_specs, out_specs=out_specs, check_vma=False
    )
```

profile of v0, /device:TPU:0, one launch (start us, length us, event | category | flops | bytes accessed | tf_op | source)
XLA Modules:
  0.0 461.6 jit_solution(14571675646012147014)
XLA Ops:
  7.2 0.8 fusion.52
  8.0 0.1 reduce_window_sum.11
  8.1 0.8 select_reduce_fusion
  8.9 0.7 multiply_add_fusion
  9.6 1.2 copy.36
  10.8 1.4 convolution_convert_fusion.2
  12.2 6.3 %all-to-all-start = ((bf16[8,16,4096]{2,1,0:T(8,128)(2,1)}), bf16[8,16,4096]{2,1,0:T(8,128)(2,1)S(1)}, u32[]{:S(2)}, u32[]{:S(2)}) async-start(bf16[8,16,4096]{2,1,0:T(8,128)(2,1)} %bitcast), calls=%async_computation | async-start | bytes 2097152 | tf_op jit(solution)/shard_map/all_to_all | solution.py:61
  18.5 0.2 copy.37
  18.7 1.4 convolution_convert_fusion.1
  20.1 24.5 %all-to-all-done = bf16[8,16,4096]{2,1,0:T(8,128)(2,1)S(1)} async-done(((bf16[8,16,4096]{2,1,0:T(8,128)(2,1)}), bf16[8,16,4096]{2,1,0:T(8,128)(2,1)S(1)}, u32[]{:S(2)}, u32[]{:S(2)}) %all-to-all-start) | async-done | bytes 1048608 | tf_op jit(solution)/shard_map/all_to_all | solution.py:61
  44.7 4.2 all-to-all-start.1
  48.9 0.0 all-gather.8.cloned.1.call-start
  49.0 1.3 copy.24
  50.2 2.0 copy.25
  52.3 3.3 reshape.48
  55.5 3.3 copy.26
  58.9 16.2 %all-to-all-done.1 = bf16[8,16,4096]{2,1,0:T(8,128)(2,1)} async-done(((bf16[8,16,4096]{2,1,0:T(8,128)(2,1)}), bf16[8,16,4096]{2,1,0:T(8,128)(2,1)}, u32[]{:S(2)}, u32[]{:S(2)}) %all-to-all-start.1) | async-done | bytes 1048608 | tf_op jit(solution)/shard_map/all_to_all | solution.py:62
  75.0 4.3 reshape.50
  79.3 2.5 copy.27
  81.8 57.5 %while.15 = (s32[]{:T(128)}, f32[512,8,64]{0,2,1:T(8,128)S(1)}, f32[512,8,64]{0,2,1:T(8,128)}, bf16[2,512,8,64]{1,3,2,0:T(8,128)(2,1)}, bf16[2,512,8,64]{1,3,2,0...) while((s32[]{:T(128)}, f32[512,8,64]{0,2,1:T(8,128)S(1)}, ...), condition=%wide.region_6.7_spmd.clone, body=%wide.region_2.6_spmd.clone.sunk | while | flops 1635775488 | bytes 145836400 | solution.py:80
  81.8 0.7 iota_compare_fusion.7
  82.5 7.6 %fusion.104 = (f32[8,512]{1,0:T(8,128)S(1)}, f32[8,512,512]{1,2,0:T(8,128)}) fusion(pred[512]{0:T(512)(128)(4,1)S(1)} %iota_compare_fusion.7, bf16[512,8,64]{0,2,1:T(8,128)(2,1)S(1)} %get-tuple-element.209, bf16[2,512,8,64]{1,3,2,0:T(8,128)(2,1)} %get-tuple-element.208, s32[]{:T(128)} %get-tuple-element.193), kind=kOutput, calls=%fused_computation.64.clone.1 | convolution fusion | flops 276824576 | bytes 9454592 | tf_op jit(solution)/shard_map/while/body/eval_jaxpr/sub | solution.py:17
  90.1 4.8 %fusion.105 = bf16[8,512,512]{1,2,0:T(8,128)(2,1)S(1)} fusion(f32[8,512,512]{1,2,0:T(8,128)} %get-tuple-element.180, f32[8,512]{1,0:T(8,128)S(1)} %get-tuple-element.181), kind=kLoop, calls=%fused_computation.10.clone.1 | loop fusion | flops 4194304 | bytes 12599296 | tf_op jit(solution)/shard_map/while/body/eval_jaxpr/convert_element_type | solution.py:19
  94.9 2.0 copy-done.1
  96.9 0.8 fusion.106
  97.7 3.4 multiply_convert_fusion.2
  101.1 3.9 fusion.107
  105.1 0.8 fusion.109
  105.9 1.0 copy-done.9
  106.9 0.7 copy-done.2
  107.6 2.4 fusion.108
  110.0 0.6 iota_compare_fusion.7
  110.6 7.6 %fusion.104 = (f32[8,512]{1,0:T(8,128)S(1)}, f32[8,512,512]{1,2,0:T(8,128)}) fusion(pred[512]{0:T(512)(128)(4,1)S(1)} %iota_compare_fusion.7, bf16[512,8,64]{0,2,1:T(8,128)(2,1)S(1)} %get-tuple-element.209, bf16[2,512,8,64]{1,3,2,0:T(8,128)(2,1)} %get-tuple-element.208, s32[]{:T(128)} %get-tuple-element.193), kind=kOutput, calls=%fused_computation.64.clone.1 | convolution fusion | flops 276824576 | bytes 9454592 | tf_op jit(solution)/shard_map/while/body/eval_jaxpr/sub | solution.py:17
  118.2 4.8 %fusion.105 = bf16[8,512,512]{1,2,0:T(8,128)(2,1)S(1)} fusion(f32[8,512,512]{1,2,0:T(8,128)} %get-tuple-element.180, f32[8,512]{1,0:T(8,128)S(1)} %get-tuple-element.181), kind=kLoop, calls=%fused_computation.10.clone.1 | loop fusion | flops 4194304 | bytes 12599296 | tf_op jit(solution)/shard_map/while/body/eval_jaxpr/convert_element_type | solution.py:19
  123.0 2.0 copy-done.1
  125.0 0.8 fusion.106
  125.8 3.4 multiply_convert_fusion.2
  129.2 3.9 fusion.107
  133.2 0.8 fusion.109
  134.0 1.0 copy-done.9
  135.0 0.7 copy-done.2
  135.8 3.6 fusion.108
  139.3 2.1 convert_element_type.49
  141.5 0.0 all-gather.8.cloned.1.call-update
  141.5 0.0 all-gather.4.cloned.1.call-start
  141.5 0.9 convert_element_type.47
  142.4 0.2 all-gather.6.cloned.1.call-start
  142.7 0.9 copy.29
  143.6 0.0 reduce-scatter.2.cloned.1.call-start
  143.6 31.9 %all-gather.8.cloned.1.call-done = bf16[512,2048]{0,1:T(8,128)(2,1)} async-done(((bf16[512,512]{0,1:T(8,128)(2,1)}), bf16[512,2048]{0,1:T(8,128)(2,1)}) %all-gather.8.cloned.1.call-update) | async-done | bytes 2097168 | tf_op jit(solution)/shard_map/all_gather | solution.py:93
  175.5 4.8 %convolution_bitcast_fusion.3 = f32[2048,1,512]{2,0,1:T(8,128)} fusion(bf16[512,2048]{0,1:T(8,128)(2,1)} %all-gather.8.cloned.1.call-done, bf16[1,512,512]{2,1,0:T(8,128)(2,1)S(1)} %copy-done), kind=kOutput, calls=%fused_computation.45 | convolution fusion | flops 1073741824 | bytes 6815744 | tf_op jit(solution)/shard_map/dot_general | solution.py:109
  180.3 32.9 %all-gather.4.cloned.1.call-done = bf16[512,2048]{0,1:T(8,128)(2,1)} async-done(((bf16[512,512]{0,1:T(8,128)(2,1)}), bf16[512,2048]{0,1:T(8,128)(2,1)}) %all-gather.4.cloned.1.call-update) | async-done | bytes 2097168 | tf_op jit(solution)/shard_map/all_gather | solution.py:92
  213.3 3.0 convolution_bitcast_fusion.4
  216.3 4.2 pad_maximum_fusion
  220.5 2.7 copy.28
  223.2 2.5 all_to_all.24
  225.7 55.0 %all_to_all.30 = bf16[8,16,4096]{2,1,0:T(8,128)(2,1)S(1)} all-to-all(bf16[8,16,4096]{2,1,0:T(8,128)(2,1)} %all_to_all.24), channel_id=1, replica_groups=mesh['grp'=2,'seq'=4,'mdl'=4] {'grp','seq'}, dimensions={0} | all-to-all | bytes 2097152 | tf_op jit(solution)/shard_map/all_to_all | solution.py:84
  280.6 0.4 convolution_convert_fusion.3
  281.0 1.0 copy.38
  282.0 2.3 all-gather.6.cloned.1.call-done
  284.3 3.0 fusion.42
  287.3 3.7 fusion.46
  291.0 161.0 %reduce-scatter.2.cloned.1.call-done = f32[256,2,512]{2,0,1:T(8,128)} async-done(((f32[2048,2,512]{2,0,1:T(8,128)}), f32[256,2,512]{2,0,1:T(8,128)}) %reduce-scatter.2.cloned.1.call-update) | async-done | bytes 1048592 | tf_op jit(solution)/shard_map/reduce_scatter | solution.py:112
  452.0 3.0 copy.30
  (46 shorter events, 0.1 us)
Async XLA Ops:
  7.2 168.3 %copy-start = (bf16[1,512,512]{2,1,0:T(8,128)(2,1)S(1)}, bf16[1,512,512]{2,1,0:T(8,128)(2,1)}, u32[]{:S(2)}) copy-start(bf16[1,512,512]{2,1,0:T(8,128)(2,1)} %param.15) | copy-start | bytes 1572868
  7.2 11.4 %copy-start.10 = (bf16[64,8,512]{2,1,0:T(8,128)(2,1)S(1)}, bf16[64,8,512]{2,1,0:T(8,128)(2,1)}, u32[]{:S(2)}) copy-start(bf16[64,8,512]{2,1,0:T(8,128)(2,1)} %param.11) | copy-start | bytes 1572868
  12.2 32.4 %all-to-all-start = ((bf16[8,16,4096]{2,1,0:T(8,128)(2,1)}), bf16[8,16,4096]{2,1,0:T(8,128)(2,1)S(1)}, u32[]{:S(2)}, u32[]{:S(2)}) async-start(bf16[8,16,4096]{2,1,0:T(8,128)(2,1)} %bitcast), calls=%async_computation | async-start | bytes 2097152 | tf_op jit(solution)/shard_map/all_to_all | solution.py:61
  44.7 30.4 %all-to-all-start.1 = ((bf16[8,16,4096]{2,1,0:T(8,128)(2,1)}), bf16[8,16,4096]{2,1,0:T(8,128)(2,1)}, u32[]{:S(2)}, u32[]{:S(2)}) async-start(bf16[8,16,4096]{2,1,0:T(8,128)(2,1)} %bitcast.2), calls=%async_computation.1 | async-start | bytes 2097152 | tf_op jit(solution)/shard_map/all_to_all | solution.py:62
  48.9 126.6 %all-gather.8.cloned.1.call-start = ((), (), s32[]{:S(2)}) async-start(), calls=%async_computation.6 | async-start | bytes 2621440 | tf_op jit(solution)/shard_map/all_gather | solution.py:93
  90.1 7.6 %slice-start = ((s8[8388608]{0:T(1024)(128)(4,1)}), s8[4194304]{0:T(1024)(128)(4,1)S(1)}, s32[]{:S(2)}) async-start(s8[8388608]{0:T(1024)(128)(4,1)} %bitcast.133), calls=%async_computation.8 | async-start | bytes 8388608 | tf_op jit(solution)/shard_map/while
  90.1 6.8 %copy-start.4 = (bf16[512,8,64]{0,2,1:T(8,128)(2,1)S(1)}, bf16[512,8,64]{0,2,1:T(8,128)(2,1)}, u32[]{:S(2)}) copy-start(bf16[512,8,64]{0,2,1:T(8,128)(2,1)} %get-tuple-element.211) | copy-start | bytes 1572868 | tf_op jit(solution)/shard_map/while
  90.1 7.6 %slice-start.1 = ((s8[8388608]{0:T(1024)(128)(4,1)}), s8[4194304]{0:T(1024)(128)(4,1)S(1)}, s32[]{:S(2)}) async-start(s8[8388608]{0:T(1024)(128)(4,1)} %bitcast.133), calls=%async_computation.9 | async-start | bytes 8388608 | tf_op jit(solution)/shard_map/while
  94.9 2.0 copy-start.1
  101.1 4.0 copy-start.3
  101.1 4.0 copy-start.8
  105.0 2.6 copy-start.2
  105.9 1.0 copy-start.9
  118.2 7.6 %slice-start = ((s8[8388608]{0:T(1024)(128)(4,1)}), s8[4194304]{0:T(1024)(128)(4,1)S(1)}, s32[]{:S(2)}) async-start(s8[8388608]{0:T(1024)(128)(4,1)} %bitcast.133), calls=%async_computation.8 | async-start | bytes 8388608 | tf_op jit(solution)/shard_map/while
  118.2 6.8 %copy-start.4 = (bf16[512,8,64]{0,2,1:T(8,128)(2,1)S(1)}, bf16[512,8,64]{0,2,1:T(8,128)(2,1)}, u32[]{:S(2)}) copy-start(bf16[512,8,64]{0,2,1:T(8,128)(2,1)} %get-tuple-element.211) | copy-start | bytes 1572868 | tf_op jit(solution)/shard_map/while
  118.2 7.6 %slice-start.1 = ((s8[8388608]{0:T(1024)(128)(4,1)}), s8[4194304]{0:T(1024)(128)(4,1)S(1)}, s32[]{:S(2)}) async-start(s8[8388608]{0:T(1024)(128)(4,1)} %bitcast.133), calls=%async_computation.9 | async-start | bytes 8388608 | tf_op jit(solution)/shard_map/while
  123.0 2.0 copy-start.1
  129.2 4.0 copy-start.3
  129.2 4.0 copy-start.8
  133.2 2.6 copy-start.2
  134.0 1.0 copy-start.9
  139.3 3.3 copy-start.11
  141.5 71.8 %all-gather.4.cloned.1.call-start = ((), (), s32[]{:S(2)}) async-start(), calls=%async_computation.4 | async-start | bytes 2621440 | tf_op jit(solution)/shard_map/all_gather | solution.py:92
  142.4 141.9 %all-gather.6.cloned.1.call-start = ((), (), s32[]{:S(2)}) async-start(), calls=%async_computation.5 | async-start | bytes 4718592 | tf_op jit(solution)/shard_map/all_gather | solution.py:95
  143.6 308.5 %reduce-scatter.2.cloned.1.call-start = ((), (), s32[]{:S(2)}) async-start(), calls=%async_computation.7 | async-start | bytes 9437184 | tf_op jit(solution)/shard_map/reduce_scatter | solution.py:112
  213.3 3.0 copy-start.6
  225.7 58.6 %copy-start.7 = (bf16[512,2048]{0,1:T(8,128)(2,1)S(1)}, bf16[512,2048]{0,1:T(8,128)(2,1)}, u32[]{:S(2)}) copy-start(bf16[512,2048]{0,1:T(8,128)(2,1)} %all-gather.8.cloned.1.call-done) | copy-start | bytes 6291460
  284.3 3.0 copy-start.5
Sparse Core Ops, SparseCore 0:
  141.6 33.8 all-gather.7
  177.9 35.2 all-gather.3
  214.9 69.3 all-gather.5
  286.4 165.5 reduce-scatter.1
where the time goes:
time: 462 us
  waiting for transfers between devices  269 us (58%)
  matrix products  56.6 us (12%)
  blocking collectives  55 us (12%)
  local copies, waits for them, and re-layouts  35.5 us (8%)
  other arithmetic  20.6 us (4%)
  between operations  13.9 us (3%)
  starting transfers between devices  10.9 us (2%)
    reduce_scatter x1, waiting for transfers between devices, on_device(): lax.psum_scatter(jnp.stack([grad_key, grad_value], axis=1), ('grp', 'seq'...  161 us
    all_to_all x1, blocking collectives, on_device(): lax.all_to_all(back_rows, ('grp', 'seq'), split_axis=0, concat_axis=0, ti...  55 us
    all_gather x1, waiting for transfers between devices, on_device(): lax.all_gather(key_bf, 'mdl', axis=1, tiled=True)  32.9 us
    all_gather x1, waiting for transfers between devices, on_device(): lax.all_gather(value_bf, 'mdl', axis=1, tiled=True)  31.9 us
    all_to_all x1, waiting for transfers between devices, on_device(): lax.all_to_all(send_query, ('grp', 'seq'), split_axis=0, concat_axis=0, t...  24.5 us
    all_to_all x1, waiting for transfers between devices, on_device(): lax.all_to_all(send_grad, ('grp', 'seq'), split_axis=0, concat_axis=0, ti...  16.2 us
    unnamed x21, local copies, waits for them, and re-layouts  15.4 us
    sub x2, matrix products, block_grads(): exp_terms = jnp.exp(scores - row_peak)  15.2 us
  transfers between devices with their start and end apart: 6, of which 6 were waited for; matrix products, arithmetic and copies ran while one was open for 8% of the time, Pallas kernels for 0%

commit v1 on v0

--- a/solution.py
+++ b/solution.py
@@ -1,9 +1,333 @@
+import functools
+
 import jax
 import jax.numpy as jnp
 from jax import lax
+from jax.experimental import pallas as pl
+from jax.experimental.pallas import tpu as pltpu
 from jax.sharding import PartitionSpec as P
 
 HEAD_DIM = 64
+LANES = 128
+PEERS = ("grp", "seq")
+BF16 = jnp.bfloat16
+F32 = jnp.float32
+VMEM_BYTES = 40 * 1024 * 1024
+
+VMEM_SPEC = pl.BlockSpec(memory_space=pltpu.VMEM)
+SMEM_SPEC = pl.BlockSpec(memory_space=pltpu.SMEM)
+NT = (((1,), (1,)), ((), ()))
+TN = (((0,), (0,)), ((), ()))
+
+
+def cost(flops, bytes_accessed, transcendentals=0):
+    return pl.CostEstimate(
+        flops=flops, bytes_accessed=bytes_accessed, transcendentals=transcendentals
+    )
+
+
+def pack_kernel(peers, per_peer, chunks, me_ref, owners_ref, q_ref, g_ref, *refs):
+    table_ref, out_refs = refs[0], refs[1 : 1 + chunks * peers]
+    both_ref, count_ref = refs[-2:]
+    targets, rows, width = q_ref.shape
+    both = jnp.concatenate([q_ref[...].astype(F32), g_ref[...].astype(F32)], axis=1)
+    both_ref[:targets] = both.astype(BF16)
+    both_ref[targets] = jnp.zeros((2 * rows, width), BF16)
+    me = me_ref[0]
+
+    def clear_count(i, _):
+        count_ref[i] = 0
+        return 0
+
+    def clear_slot(i, _):
+        table_ref[i] = targets
+        return 0
+
+    def place(t, _):
+        distance = owners_ref[t] ^ me
+        rank = count_ref[distance]
+        table_ref[distance * per_peer + rank] = t
+        count_ref[distance] = rank + 1
+        return 0
+
+    lax.fori_loop(0, peers, clear_count, 0)
+    lax.fori_loop(0, peers * per_peer, clear_slot, 0)
+    lax.fori_loop(0, targets, place, 0)
+    groups = width // (chunks * LANES)
+    for d in range(peers):
+
+        def move(slot, _, d=d):
+            t = table_ref[d * per_peer + slot]
+            for c in range(chunks):
+                for a in range(groups):
+                    lane = (a * chunks + c) * LANES
+                    out_refs[c * peers + d][slot, :, a * LANES : (a + 1) * LANES] = both_ref[
+                        t, :, lane : lane + LANES
+                    ]
+            return 0
+
+        lax.fori_loop(0, per_peer, move, 0, unroll=4)
+
+
+def pack(me, owners, queries, out_grads, peers, per_peer, chunks):
+    targets, rows, width = queries.shape
+    block = jax.ShapeDtypeStruct((per_peer, 2 * rows, width // chunks), BF16)
+    outs = pl.pallas_call(
+        functools.partial(pack_kernel, peers, per_peer, chunks),
+        out_shape=[jax.ShapeDtypeStruct((peers * per_peer,), jnp.int32)]
+        + [block] * (chunks * peers),
+        in_specs=[SMEM_SPEC, SMEM_SPEC, VMEM_SPEC, VMEM_SPEC],
+        out_specs=[SMEM_SPEC] + [VMEM_SPEC] * (chunks * peers),
+        scratch_shapes=[
+            pltpu.VMEM((targets + 1, 2 * rows, width), BF16),
+            pltpu.SMEM((peers,), jnp.int32),
+        ],
+        compiler_params=pltpu.CompilerParams(vmem_limit_bytes=VMEM_BYTES),
+        cost_estimate=cost(0, 3 << 20),
+        name="pack_targets",
+    )(me, owners, queries, out_grads)
+    return outs[0], [outs[1 + c * peers : 1 + (c + 1) * peers] for c in range(chunks)]
+
+
+def unpack_kernel(peers, per_peer, chunks, table_ref, *refs):
+    in_refs, out_ref, rows_ref = refs[: chunks * peers], refs[-2], refs[-1]
+    targets, rows, width = out_ref.shape
+    groups = width // (chunks * LANES)
+    for c in range(chunks):
+        for d in range(peers):
+            block = in_refs[c * peers + d][...].astype(F32)
+            block = block.reshape(per_peer, rows, width // chunks)
+            for a in range(groups):
+                lane = (a * chunks + c) * LANES
+                rows_ref[d * per_peer : (d + 1) * per_peer, :, lane : lane + LANES] = block[
+                    :, :, a * LANES : (a + 1) * LANES
+                ]
+
+    def move(slot, _):
+        t = table_ref[slot]
+
+        @pl.when(t < targets)
+        def _():
+            out_ref[t] = rows_ref[slot].astype(BF16)
+
+        return 0
+
+    lax.fori_loop(0, peers * per_peer, move, 0)
+
+
+def unpack(table, blocks, targets, rows, width, peers, per_peer):
+    chunks = len(blocks)
+    return pl.pallas_call(
+        functools.partial(unpack_kernel, peers, per_peer, chunks),
+        out_shape=jax.ShapeDtypeStruct((targets, rows, width), BF16),
+        in_specs=[SMEM_SPEC] + [VMEM_SPEC] * (chunks * peers),
+        out_specs=VMEM_SPEC,
+        scratch_shapes=[pltpu.VMEM((peers * per_peer, rows, width), F32)],
+        compiler_params=pltpu.CompilerParams(vmem_limit_bytes=VMEM_BYTES),
+        cost_estimate=cost(0, 3 << 20),
+        name="unpack_query_grads",
+    )(table, *[b for part in blocks for b in part])
+
+
+def attend_kernel(peers, chunk, chunks, len_ref, k_ref, v_ref, *refs):
+    in_refs = refs[:peers]
+    groups = k_ref.shape[1] // (chunks * LANES)
+    kv_refs = refs[peers : peers + groups]
+    out_refs = refs[peers + groups : 2 * peers + groups]
+    q_s, g_s, o_s, kt_s, kg_s, vg_s = refs[2 * peers + groups :]
+    src_len = k_ref.shape[0]
+    per_peer, double, width = in_refs[0].shape
+    rows = double // 2
+    block_rows = per_peer * rows
+    total_rows = peers * block_rows
+    tile = min(256, total_rows)
+    scale = HEAD_DIM**-0.5
+    for d in range(peers):
+        both = in_refs[d][...].astype(F32)
+        at = slice(d * block_rows, (d + 1) * block_rows)
+        q_s[at] = (both[:, :rows] * scale).reshape(block_rows, width).astype(BF16)
+        g_s[at] = both[:, rows:].reshape(block_rows, width).astype(BF16)
+    valid = lax.broadcasted_iota(jnp.int32, (src_len, 1), 0) < len_ref[0]
+    lane_head = lax.broadcasted_iota(jnp.int32, (1, LANES), 1) // HEAD_DIM
+    for a in range(groups):
+        lane = (a * chunks + chunk) * LANES
+        mine = slice(a * LANES, (a + 1) * LANES)
+        kt_s[...] = (k_ref[:, lane : lane + LANES].astype(F32) * scale).T.astype(BF16)
+        kg_s[...] = jnp.zeros_like(kg_s)
+        vg_s[...] = jnp.zeros_like(vg_s)
+
+        def step(i, _, lane=lane, mine=mine):
+            at = pl.ds(pl.multiple_of(i * tile, tile), tile)
+            q_pair, g_pair = q_s[at, mine], g_s[at, mine]
+            k_pair, v_pair = k_ref[:, lane : lane + LANES], v_ref[:, lane : lane + LANES]
+            parts = []
+            for h in range(LANES // HEAD_DIM):
+                q_h = jnp.where(lane_head == h, q_pair, jnp.zeros_like(q_pair))
+                g_h = jnp.where(lane_head == h, g_pair, jnp.zeros_like(g_pair))
+                scores = lax.dot_general(k_pair, q_h, NT, preferred_element_type=F32)
+                scores = jnp.where(valid, scores, -1e30)
+                prob_grad = lax.dot_general(v_pair, g_h, NT, preferred_element_type=F32)
+                peak = jnp.max(scores, axis=0, keepdims=True)
+                terms = jnp.exp(scores - peak)
+                probs = terms * (1.0 / jnp.sum(terms, axis=0, keepdims=True))
+                row_delta = jnp.sum(probs * prob_grad, axis=0, keepdims=True)
+                score_grad = (probs * (prob_grad - row_delta)).astype(BF16)
+                vg_s[...] += jnp.dot(probs.astype(BF16), g_h, preferred_element_type=F32)
+                kg_s[...] += jnp.dot(score_grad, q_h, preferred_element_type=F32)
+                parts.append(
+                    jnp.dot(
+                        kt_s[h * HEAD_DIM : (h + 1) * HEAD_DIM],
+                        score_grad,
+                        preferred_element_type=F32,
+                    )
+                )
+            o_s[at, mine] = jnp.concatenate(parts, axis=0).T.astype(BF16)
+            return 0
+
+        lax.fori_loop(0, total_rows // tile, step, 0)
+        kv_refs[a][:, :LANES] = kg_s[...].astype(BF16)
+        kv_refs[a][:, LANES:] = vg_s[...].astype(BF16)
+    for d in range(peers):
+        out_refs[d][...] = o_s[d * block_rows : (d + 1) * block_rows]
+
+
+def attend(length, keys, values, blocks, chunk, chunks):
+    peers = len(blocks)
+    src_len, width = keys.shape
+    per_peer, double, part = blocks[0].shape
+    block_rows = per_peer * double // 2
+    total_rows = peers * block_rows
+    groups = part // LANES
+    heads = part // HEAD_DIM
+    outs = pl.pallas_call(
+        functools.partial(attend_kernel, peers, chunk, chunks),
+        out_shape=[jax.ShapeDtypeStruct((src_len, 2 * LANES), BF16)] * groups
+        + [jax.ShapeDtypeStruct((block_rows, part), BF16)] * peers,
+        in_specs=[SMEM_SPEC] + [VMEM_SPEC] * (2 + peers),
+        out_specs=[VMEM_SPEC] * (groups + peers),
+        scratch_shapes=[
+            pltpu.VMEM((total_rows, part), BF16),
+            pltpu.VMEM((total_rows, part), BF16),
+            pltpu.VMEM((total_rows, part), BF16),
+            pltpu.VMEM((LANES, src_len), BF16),
+            pltpu.VMEM((src_len, LANES), F32),
+            pltpu.VMEM((src_len, LANES), F32),
+        ],
+        compiler_params=pltpu.CompilerParams(vmem_limit_bytes=VMEM_BYTES),
+        cost_estimate=cost(
+            40 * total_rows * src_len * HEAD_DIM * heads, 4 << 20, total_rows * src_len * heads
+        ),
+        name="attend",
+    )(length, keys, values, *blocks)
+    return outs[:groups], outs[groups:]
+
+
+def weight_kernel(place_ref, states_ref, *refs):
+    in_refs, own_ref, sib_ref = refs[:-2], refs[-2], refs[-1]
+    states = states_ref[...]
+    groups = 2
+    for e in range(len(in_refs) // groups):
+        for a in range(groups):
+            piece = lax.dot_general(
+                in_refs[e * groups + a][...], states, TN, preferred_element_type=F32
+            )
+            index = e * groups + a
+            away, seq = place_ref[2 * index], place_ref[2 * index + 1]
+
+            @pl.when(away == 0)
+            def _(piece=piece, seq=seq):
+                own_ref[seq] = piece
+
+            @pl.when(away != 0)
+            def _(piece=piece, seq=seq):
+                sib_ref[seq] = piece.astype(BF16)
+
+
+def weight_parts(place, states, blocks, seq_size):
+    src_len, width = states.shape
+    tall = blocks[0].shape[1]
+    shape = (seq_size, tall, width)
+    return pl.pallas_call(
+        weight_kernel,
+        out_shape=[jax.ShapeDtypeStruct(shape, F32), jax.ShapeDtypeStruct(shape, BF16)],
+        in_specs=[SMEM_SPEC] + [VMEM_SPEC] * (1 + len(blocks)),
+        out_specs=[VMEM_SPEC] * 2,
+        compiler_params=pltpu.CompilerParams(vmem_limit_bytes=VMEM_BYTES),
+        cost_estimate=cost(2 * len(blocks) * src_len * tall * width, 6 << 20),
+        name="weight_parts",
+    )(place, states, *blocks)
+
+
+def state_kernel(chunks, order_ref, w_ref, *refs):
+    in_refs, out_ref, total_ref = refs[:-2], refs[-2], refs[-1]
+    total_ref[...] = jnp.zeros_like(total_ref)
+    per_chunk = len(in_refs) // chunks
+    for c in range(chunks):
+        at = slice(c * LANES, (c + 1) * LANES)
+        for index in range(per_chunk):
+            piece = order_ref[index]
+            weight = jnp.concatenate([w_ref[piece, 0, at], w_ref[piece, 1, at]], axis=0)
+            total_ref[...] += jnp.dot(
+                in_refs[c * per_chunk + index][...], weight, preferred_element_type=F32
+            )
+    out_ref[...] = total_ref[...].astype(BF16)
+
+
+def state_grads(order, weights, blocks, chunks):
+    src_len, width = blocks[0].shape[0], weights.shape[-1]
+    return pl.pallas_call(
+        functools.partial(state_kernel, chunks),
+        out_shape=jax.ShapeDtypeStruct((src_len, width), BF16),
+        in_specs=[SMEM_SPEC] + [VMEM_SPEC] * (1 + len(blocks)),
+        out_specs=VMEM_SPEC,
+        scratch_shapes=[pltpu.VMEM((src_len, width), F32)],
+        compiler_params=pltpu.CompilerParams(vmem_limit_bytes=VMEM_BYTES),
+        cost_estimate=cost(2 * len(blocks) * src_len * 2 * LANES * width, 8 << 20),
+        name="state_grads",
+    )(order, weights, *blocks)
+
+
+def swap(x, axes, size, distance):
+    return lax.ppermute(x, axes, [(i, i ^ distance) for i in range(size)])
+
+
+def exchange(blocks):
+    peers = len(blocks)
+    far_first = sorted(range(1, peers), key=lambda d: -(d % (peers // 2)))
+    got = {d: swap(blocks[d], PEERS, peers, d) for d in far_first}
+    return [blocks[0]] + [got[d] for d in range(1, peers)]
+
+
+def gather_mdl(pair):
+    near = [swap(b, "mdl", 4, 1) for b in pair]
+    over = [swap(b, "mdl", 4, 2) for b in pair]
+    across = [swap(near[0], "mdl", 4, 2), swap(over[1], "mdl", 4, 1)]
+    return list(pair) + near + over + across
+
+
+def scatter_line(own, sib, seq_size):
+    place = lax.axis_index("seq")
+    got = swap(sib, "grp", 2, 1)
+
+    def piece(index):
+        index = jnp.clip(index, 0, seq_size - 1)
+        mine = lax.dynamic_index_in_dim(own, index, 0, keepdims=False)
+        other = lax.dynamic_index_in_dim(got, index, 0, keepdims=False)
+        return mine + other.astype(F32)
+
+    right = left = None
+    last = seq_size - 1
+    for t in range(last):
+        send_right, send_left = piece(last - t + place), piece(t + place - last)
+        if t > 0:
+            send_right, send_left = send_right + right.astype(F32), send_left + left.astype(F32)
+        right = lax.ppermute(
+            send_right.astype(BF16), "seq", [(z, z + 1) for z in range(t + 1)]
+        )
+        left = lax.ppermute(
+            send_left.astype(BF16), "seq", [(last - z, last - z - 1) for z in range(t + 1)]
+        )
+    return piece(place) + right.astype(F32) + left.astype(F32)
 
 
 def block_grads(query_block, grad_block, key_local, value_local, key_valid):
@@ -35,7 +359,7 @@
     return (query_grad, key_grad, value_grad)
 
 
-def on_device(queries, out_grads, owners, src_keys, src_values, states, kv_weight, src_lengths):
+def any_mesh(queries, out_grads, owners, src_keys, src_values, states, kv_weight, src_lengths):
     peer_count = lax.axis_size(("grp", "seq"))
     tgt_dev, tgt_len, inner_dev = queries.shape
     per_peer = max(2, 2 * tgt_dev // peer_count)
@@ -115,22 +439,50 @@
     return (query_out, state_out, weight_out)
 
 
+def on_device(queries, out_grads, owners, src_keys, src_values, states, kv_weight, src_lengths):
+    seq_size = lax.axis_size("seq")
+    peers = lax.axis_size(PEERS)
+    targets, rows, width = queries.shape
+    per_peer = max(2, 2 * targets // peers)
+    src_len = src_keys.shape[1]
+    chunks = 2
+    groups = width // (chunks * LANES)
+    me = lax.axis_index(PEERS).astype(jnp.int32)
+    mdl = lax.axis_index("mdl").astype(jnp.int32)
+    grp = lax.axis_index("grp").astype(jnp.int32)
+    table, sends = pack(me[None], owners, queries, out_grads, peers, per_peer, chunks)
+    keys, values = src_keys[0], src_values[0]
+    flat_states = states[0]
+    tall = jnp.transpose(kv_weight, (1, 0, 2))
+
+    source = mdl ^ (jnp.arange(4 * groups, dtype=jnp.int32) // groups)
+    order = source * groups + jnp.arange(4 * groups, dtype=jnp.int32) % groups
+    place = jnp.stack([(order // seq_size) ^ grp, order % seq_size], axis=1).reshape(-1)
+
+    got = [exchange(sends[c]) for c in range(chunks)]
+    gathered, back, sums = [], [], []
+    for c in range(chunks):
+        pair, query_blocks = attend(src_lengths, keys, values, got[c], c, chunks)
+        back.append(query_blocks)
+        gathered.append(gather_mdl(pair))
+    tall, _ = lax.optimization_barrier((tall, got[1][1]))
+    weights = lax.all_gather(tall, PEERS, axis=0)
+    for c in range(chunks):
+        own, sib = weight_parts(place, flat_states, gathered[c], seq_size)
+        sums.append(scatter_line(own, sib, seq_size))
+    returned = [exchange(b) for b in back]
+    state_out = state_grads(order, weights, [b for part in gathered for b in part], chunks)
+    query_out = unpack(table, returned, targets, rows, width, peers, per_peer)
+    weight_out = jnp.concatenate(
+        [s.reshape(2, LANES, width).transpose(1, 0, 2) for s in sums], axis=0
+    )
+    return (query_out, state_out.reshape(1, src_len, width), weight_out)
+
+
 def solution(mesh):
-    in_specs = (
-        P(("grp", "seq"), None, "mdl"),
-        P(("grp", "seq"), None, "mdl"),
-        P(("grp", "seq")),
-        P(("grp", "seq"), None, "mdl"),
-        P(("grp", "seq"), None, "mdl"),
-        P(("grp", "seq"), None, "mdl"),
-        P(("grp", "seq"), None, "mdl"),
-        P(("grp", "seq")),
-    )
-    out_specs = (
-        P(("grp", "seq"), None, "mdl"),
-        P(("grp", "seq"), None, "mdl"),
-        P(("grp", "seq"), None, "mdl"),
-    )
+    spec = P(PEERS, None, "mdl")
+    in_specs = (spec, spec, P(PEERS), spec, spec, spec, spec, P(PEERS))
+    tuned = (mesh.shape["grp"], mesh.shape["seq"], mesh.shape["mdl"]) == (2, 4, 4)
     return jax.shard_map(
-        on_device, mesh=mesh, in_specs=in_specs, out_specs=out_specs, check_vma=False
-    )
+        on_device if tuned else any_mesh, mesh=mesh, in_specs=in_specs, out_specs=(spec, spec, spec), check_vma=False
+    )

time: 462 us -> 281 us (0.61)
  waiting for transfers between devices: 269 us -> 30 us
  starting transfers between devices: 10.9 us -> 126 us
  matrix products: 56.6 us -> 0 us
  blocking collectives: 55 us -> 0 us
  Pallas kernels: 0 us -> 48.2 us
    reduce_scatter x1 -> x0, waiting for transfers between devices: 161 us -> none  [on_device(): lax.psum_scatter(jnp.stack([grad_key, grad_value], axis=1), ('grp', 'seq'...]
    ppermute x0 -> x54, starting transfers between devices: none -> 126 us  [the longest x42 100 us: swap(): return lax.ppermute(x, axes, [(i, i ^ distance) for i in range(size)])]
    all_gather x3 -> x1, waiting for transfers between devices: 67.1 us -> 0.01 us  [on_device(): weights = lax.all_gather(tall, PEERS, axis=0)]
    all_to_all x1 -> x0, blocking collectives: 55 us -> none  [on_device(): lax.all_to_all(back_rows, ('grp', 'seq'), split_axis=0, concat_axis=0, ti...]
    pallas_call x0 -> x7, Pallas kernels: none -> 48.2 us  [the longest x2 27 us: attend(): pl.pallas_call(functools.partial(attend_kernel, peers, chunk, chunks), ou...]
    dot_general x17 -> x0, matrix products: 41.4 us -> none  [the longest x2 7.87 us: block_grads(): jnp.einsum('hrk,rhe->khe', score_grad, query_block, preferred_element_typ...]
    all_to_all x2 -> x0, waiting for transfers between devices: 40.7 us -> none  [the longest x1 24.5 us: on_device(): lax.all_to_all(send_query, ('grp', 'seq'), split_axis=0, concat_axis=0, t...]
    ppermute x0 -> x54, waiting for transfers between devices: none -> 30 us  [the longest x42 29.1 us: swap(): return lax.ppermute(x, axes, [(i, i ^ distance) for i in range(size)])]
  transfers between devices with their start and end apart: 6 -> 55, of which waited for: 6 -> 11; matrix products, arithmetic and copies ran while one was open for 8% -> 8% of each run, Pallas kernels for 0% -> 14%
where the time goes in v1:
time: 281 us; the launch traced here: 279 us
  starting transfers between devices  126 us (45%)
  Pallas kernels  48.2 us (17%)
  local copies, waits for them, and re-layouts  38.8 us (14%)
  waiting for transfers between devices  30 us (11%)
  other arithmetic  20.7 us (7%)
  between operations  15.1 us (5%)
    ppermute x42, starting transfers between devices, swap(): return lax.ppermute(x, axes, [(i, i ^ distance) for i in range(size)])  100 us
    unnamed x119, local copies, waits for them, and re-layouts  37.9 us
    ppermute x42, waiting for transfers between devices, swap(): return lax.ppermute(x, axes, [(i, i ^ distance) for i in range(size)])  29.1 us
    pallas_call x2, Pallas kernels, attend(): pl.pallas_call(functools.partial(attend_kernel, peers, chunk, chunks), ou...  27 us
    ppermute x6, starting transfers between devices, scatter_line(): lax.ppermute(send_right.astype(BF16), 'seq', [(z, z + 1) for z in range(t...  17.9 us
    convert_element_type x6, other arithmetic, scatter_line(): send_right.astype(BF16)  12.6 us
    pallas_call x2, Pallas kernels, weight_parts(): pl.pallas_call(weight_kernel, out_shape=[jax.ShapeDtypeStruct(shape, F32)...  9.54 us
    ppermute x6, starting transfers between devices, scatter_line(): lax.ppermute(send_left.astype(BF16), 'seq', [(last - z, last - z - 1) for...  8.03 us
  transfers between devices with their start and end apart: 55, of which 11 were waited for; matrix products, arithmetic and copies ran while one was open for 8% of the time, Pallas kernels for 14%

profile of v1, /device:TPU:0, one launch (start us, length us, event | category | flops | bytes accessed | tf_op | source)
XLA Modules:
  0.0 279.3 jit_solution(18074873849589308146)
XLA Ops:
  10.0 3.5 %pack_targets.1 = (s32[128]{0:T(128)S(1)}, bf16[16,16,256]{2,1,0:T(8,128)(2,1)S(1)}, bf16[16,16,256]{2,1,0:T(8,128)(2,1)S(1)}, bf16[16,16,256]{2,1,0:T(8,128)(2,...) custom-call(s32[1]{0:T(128)} %bitcast.me_ref, ...), custom_call_target="tpu_custom_call" | custom-call | bytes 3145728 | tf_op jit(solution)/shard_map/pack_targets/pallas_call | solution.py:75
  13.5 3.1 %collective-permute-start.14 = (bf16[16,16,256]{2,1,0:T(8,128)(2,1)S(1)}, bf16[16,16,256]{2,1,0:T(8,128)(2,1)S(1)}, u32[]{:S(2)}, u32[]{:S(2)}) collective-permute-start(bf16[16,16,256]{2,1,0:T(8,128)(2,1)S(1)} %get-tuple-element.63), channel_id=1, source_target_pairs={{0,4},{4,0},{8,12},{12,8},{16,20},{20,16},{24,28},{28,24},{1,5},{5... | collective-permute-start | bytes 393224 | tf_op jit(solution)/shard_map/ppermute | solution.py:291
  16.6 1.9 copy.26
  18.5 1.6 collective-permute-done.14.refs_1_
  20.1 1.8 collective-permute-start
  21.9 2.6 collective-permute-start.1
  26.6 2.1 collective-permute-start.5
  28.6 7.7 %collective-permute-done.1.refs_2_ = bf16[16,16,256]{2,1,0:T(8,128)(2,1)S(1)} collective-permute-done((bf16[16,16,256]{2,1,0:T(8,128)(2,1)S(1)}, bf16[16,16,256]{2,1,0:T(8,128)(2,1)S(1)}, u32[]{:S(2)}, u32[]{:S(2)}) %collective-permute-start.1) | collective-permute-done | bytes 131104 | tf_op jit(solution)/shard_map/ppermute | solution.py:291
  36.3 21.6 %collective-permute-start.15 = (bf16[16,16,256]{2,1,0:T(8,128)(2,1)S(1)}, bf16[16,16,256]{2,1,0:T(8,128)(2,1)S(1)}, u32[]{:S(2)}, u32[]{:S(2)}) collective-permute-start(bf16[16,16,256]{2,1,0:T(8,128)(2,1)S(1)} %get-tuple-element.64), channel_id=1, source_target_pairs={{0,8},{4,12},{8,0},{12,4},{16,24},{20,28},{24,16},{28,20},{1,9},{5... | collective-permute-start | bytes 393224 | tf_op jit(solution)/shard_map/ppermute | solution.py:291
  59.3 20.5 %collective-permute-start.19 = (bf16[16,16,256]{2,1,0:T(8,128)(2,1)S(1)}, bf16[16,16,256]{2,1,0:T(8,128)(2,1)S(1)}, u32[]{:S(2)}, u32[]{:S(2)}) collective-permute-start(bf16[16,16,256]{2,1,0:T(8,128)(2,1)S(1)} %get-tuple-element.68), channel_id=1, source_target_pairs={{0,24},{4,28},{8,16},{12,20},{16,8},{20,12},{24,0},{28,4},{1,25},{... | collective-permute-start | bytes 393224 | tf_op jit(solution)/shard_map/ppermute | solution.py:291
  79.8 7.7 %collective-permute-done.15.refs_2_ = bf16[16,16,256]{2,1,0:T(8,128)(2,1)S(1)} collective-permute-done((bf16[16,16,256]{2,1,0:T(8,128)(2,1)S(1)}, bf16[16,16,256]{2,1,0:T(8,128)(2,1)S(1)}, u32[]{:S(2)}, u32[]{:S(2)}) %collective-permute-start.15) | collective-permute-done | bytes 131104 | tf_op jit(solution)/shard_map/ppermute | solution.py:291
  87.5 13.5 %attend.2 = (bf16[512,256]{1,0:T(8,128)(2,1)S(1)}, bf16[512,256]{1,0:T(8,128)(2,1)S(1)}, bf16[128,256]{1,0:T(8,128)(2,1)S(1)}, bf16[128,256]{1,0:T(8,128)(2,1)S(...) custom-call(s32[1]{0:T(128)S(6)} %copy.27.len_ref, ...), custom_call_target="tpu_custom_call" | custom-call | flops 5368709120 | bytes 4194304 | tf_op jit(solution)/shard_map/attend/pallas_call | solution.py:202
  101.7 1.5 collective-permute-start.28
  103.2 13.5 %attend.3 = (bf16[512,256]{1,0:T(8,128)(2,1)S(1)}, bf16[512,256]{1,0:T(8,128)(2,1)S(1)}, bf16[128,256]{1,0:T(8,128)(2,1)S(1)}, bf16[128,256]{1,0:T(8,128)(2,1)S(...) custom-call(s32[1]{0:T(128)S(6)} %copy.27.len_ref, ...), custom_call_target="tpu_custom_call" | custom-call | flops 5368709120 | bytes 4194304 | tf_op jit(solution)/shard_map/attend/pallas_call | solution.py:202
  121.0 1.5 collective-permute-start.37
  123.0 1.5 collective-permute-start.35
  124.5 1.5 collective-permute-start.36
  126.8 1.5 collective-permute-start.38
  130.3 2.9 %collective-permute-done.31.refs_5_ = bf16[512,256]{1,0:T(8,128)(2,1)} collective-permute-done((bf16[512,256]{1,0:T(8,128)(2,1)S(1)}, bf16[512,256]{1,0:T(8,128)(2,1)}, u32[]{:S(2)}, u32[]{:S(2)}) %collective-permute-start.31) | collective-permute-done | bytes 262176 | tf_op jit(solution)/shard_map/ppermute | solution.py:291
  133.2 1.5 collective-permute-start.29
  135.4 1.5 collective-permute-start.30
  136.9 1.8 collective-permute-done.36.refs_12_.refs_4_
  139.4 1.6 collective-permute-start.32
  140.9 3.4 %collective-permute-done.38.refs_14_.refs_6_ = bf16[512,256]{1,0:T(8,128)(2,1)S(1)} collective-permute-done((bf16[512,256]{1,0:T(8,128)(2,1)S(1)}, bf16[512,256]{1,0:T(8,128)(2,1)S(1)}, u32[]{:S(2)}, u32[]{:S(2)}) %collective-permute-start.38) | collective-permute-done | bytes 262176 | tf_op jit(solution)/shard_map/ppermute | solution.py:291
  145.0 1.5 collective-permute-start.33
  154.2 4.3 %weight_parts.3 = (f32[4,256,512]{2,1,0:T(8,128)S(1)}, bf16[4,256,512]{2,1,0:T(8,128)(2,1)}) custom-call(s32[16]{0:T(128)S(1)} %reshape.179.place_ref, bf16[512,512]{1,0:T(8,128)(2,1)S(1)} %bitcast.70, bf16[512,256]{1,0:T(8,128)(2,1)S(1)} %get-tuple-element.81.refs_8_.refs_0_, bf16[512,256]{1,0:T(8,128)(2,1)S(1)} %get-tuple-element.82.refs_9_.refs_1_, ...), custom_call_target="tpu_custom_call" | custom-call | flops 1073741824 | bytes 6291456 | tf_op jit(solution)/shard_map/weight_parts/pallas_call | solution.py:250
  158.5 5.3 %collective-permute-start.47 = (bf16[4,256,512]{2,1,0:T(8,128)(2,1)}, bf16[4,256,512]{2,1,0:T(8,128)(2,1)}, u32[]{:S(2)}, u32[]{:S(2)}) collective-permute-start(bf16[4,256,512]{2,1,0:T(8,128)(2,1)} %get-tuple-element.86), channel_id=1, source_target_pairs={{0,16},{16,0},{1,17},{17,1},{2,18},{18,2},{3,19},{19,3},{4,20},{20... | collective-permute-start | bytes 3145736 | tf_op jit(solution)/shard_map/ppermute | solution.py:291
  164.8 5.2 %weight_parts.2 = (f32[4,256,512]{2,1,0:T(8,128)S(1)}, bf16[4,256,512]{2,1,0:T(8,128)(2,1)}) custom-call(s32[16]{0:T(128)S(1)} %reshape.179.place_ref, bf16[512,512]{1,0:T(8,128)(2,1)S(1)} %bitcast.71, bf16[512,256]{1,0:T(8,128)(2,1)S(1)} %get-tuple-element.79.refs_0_, bf16[512,256]{1,0:T(8,128)(2,1)S(1)} %get-tuple-element.80.refs_1_, ...), custom_call_target="tpu_custom_call" | custom-call | flops 1073741824 | bytes 6291456 | tf_op jit(solution)/shard_map/weight_parts/pallas_call | solution.py:250
  170.0 1.3 copy-done
  171.4 2.2 fusion.12
  173.5 2.0 collective-permute-start.48
  175.5 2.0 fusion.10
  177.6 2.0 collective-permute-start.41
  179.6 1.4 collective-permute-start.51
  181.8 1.8 fusion.2
  183.7 5.1 %collective-permute-start.49 = (bf16[256,512]{1,0:T(8,128)(2,1)}, bf16[256,512]{1,0:T(8,128)(2,1)}, u32[]{:S(2)}, u32[]{:S(2)}) collective-permute-start(bf16[256,512]{1,0:T(8,128)(2,1)} %fusion.2), channel_id=1, source_target_pairs={{0,4},{4,8},{1,5},{5,9},{2,6},{6,10},{3,7},{7,11},{16,20},{20,24},... | collective-permute-start | bytes 786440 | tf_op jit(solution)/shard_map/ppermute | solution.py:324
  188.8 1.4 collective-permute-start.44
  190.1 2.0 fusion.7
  192.1 2.2 collective-permute-start.42
  194.4 4.3 %collective-permute-start.9 = (bf16[128,256]{1,0:T(8,128)(2,1)}, bf16[128,256]{1,0:T(8,128)(2,1)S(1)}, u32[]{:S(2)}, u32[]{:S(2)}) collective-permute-start(bf16[128,256]{1,0:T(8,128)(2,1)} %copy-done.56), channel_id=1, source_target_pairs={{0,12},{4,8},{8,4},{12,0},{16,28},{20,24},{24,20},{28,16},{1,13},{... | collective-permute-start | bytes 196616 | tf_op jit(solution)/shard_map/ppermute | solution.py:291
  198.7 2.2 fusion.3
  202.0 1.1 collective-permute-done.8.refs_2_
  203.1 1.4 collective-permute-start.11
  205.6 1.4 collective-permute-start.52
  206.9 2.3 fusion.8
  209.8 1.4 collective-permute-start.45
  211.2 4.7 %collective-permute-start.13 = (bf16[128,256]{1,0:T(8,128)(2,1)}, bf16[128,256]{1,0:T(8,128)(2,1)S(1)}, u32[]{:S(2)}, u32[]{:S(2)}) collective-permute-start(bf16[128,256]{1,0:T(8,128)(2,1)} %copy-done.52), channel_id=1, source_target_pairs={{0,28},{4,24},{8,20},{12,16},{16,12},{20,8},{24,4},{28,0},{1,29},{... | collective-permute-start | bytes 196616 | tf_op jit(solution)/shard_map/ppermute | solution.py:291
  215.9 3.3 %collective-permute-start.22 = (bf16[128,256]{1,0:T(8,128)(2,1)}, bf16[128,256]{1,0:T(8,128)(2,1)S(1)}, u32[]{:S(2)}, u32[]{:S(2)}) collective-permute-start(bf16[128,256]{1,0:T(8,128)(2,1)} %copy-done.54), channel_id=1, source_target_pairs={{0,8},{4,12},{8,0},{12,4},{16,24},{20,28},{24,16},{28,20},{1,9},{5... | collective-permute-start | bytes 196616 | tf_op jit(solution)/shard_map/ppermute | solution.py:291
  219.2 1.1 collective-permute-start.23
  220.3 1.9 fusion.1
  222.8 4.2 %collective-permute-start.24 = (bf16[128,256]{1,0:T(8,128)(2,1)}, bf16[128,256]{1,0:T(8,128)(2,1)S(1)}, u32[]{:S(2)}, u32[]{:S(2)}) collective-permute-start(bf16[128,256]{1,0:T(8,128)(2,1)} %copy-done.51), channel_id=1, source_target_pairs={{0,16},{4,20},{8,24},{12,28},{16,0},{20,4},{24,8},{28,12},{1,17},{... | collective-permute-start | bytes 196616 | tf_op jit(solution)/shard_map/ppermute | solution.py:291
  227.6 3.3 %collective-permute-start.25 = (bf16[128,256]{1,0:T(8,128)(2,1)}, bf16[128,256]{1,0:T(8,128)(2,1)S(1)}, u32[]{:S(2)}, u32[]{:S(2)}) collective-permute-start(bf16[128,256]{1,0:T(8,128)(2,1)} %copy-done.50), channel_id=1, source_target_pairs={{0,20},{4,16},{8,28},{12,24},{16,4},{20,0},{24,12},{28,8},{1,21},{... | collective-permute-start | bytes 196616 | tf_op jit(solution)/shard_map/ppermute | solution.py:291
  232.2 4.0 %collective-permute-start.50 = (bf16[256,512]{1,0:T(8,128)(2,1)}, bf16[256,512]{1,0:T(8,128)(2,1)}, u32[]{:S(2)}, u32[]{:S(2)}) collective-permute-start(bf16[256,512]{1,0:T(8,128)(2,1)} %get-tuple-element.91), channel_id=1, source_target_pairs={{0,4},{4,8},{8,12},{1,5},{5,9},{9,13},{2,6},{6,10},{10,14},{3,7},{... | collective-permute-start | bytes 786440 | tf_op jit(solution)/shard_map/ppermute | solution.py:324
  236.2 1.3 collective-permute-start.53
  237.5 2.0 fusion.6
  240.1 3.2 %collective-permute-start.27 = (bf16[128,256]{1,0:T(8,128)(2,1)}, bf16[128,256]{1,0:T(8,128)(2,1)}, u32[]{:S(2)}, u32[]{:S(2)}) collective-permute-start(bf16[128,256]{1,0:T(8,128)(2,1)} %get-tuple-element.77), channel_id=1, source_target_pairs={{0,28},{4,24},{8,20},{12,16},{16,12},{20,8},{24,4},{28,0},{1,29},{... | collective-permute-start | bytes 196616 | tf_op jit(solution)/shard_map/ppermute | solution.py:291
  243.9 2.6 collective-permute-start.43
  247.2 1.3 collective-permute-start.46
  256.9 3.8 %unpack_query_grads.1 = bf16[64,8,512]{2,1,0:T(8,128)(2,1)} custom-call(s32[128]{0:T(128)S(1)} %get-tuple-element.45.table_ref, bf16[128,256]{1,0:T(8,128)(2,1)S(1)} %get-tuple-element.54.refs_0_, bf16[128,256]{1,0:T(8,128)(2,1)S(1)} %copy-done.25, bf16[128,256]{1,0:T(8,128)(2,1)S(1)} %copy-done.27, bf16[128,256]{1,0:T(8,128)(2,1)S(1)} %copy-done.29, ...), custom_call_target="tpu_custom_call" | custom-call | bytes 3145728 | tf_op jit(solution)/shard_map/unpack_query_grads/pallas_call | solution.py:120
  260.7 1.3 fusion.4
  262.4 1.5 fusion.9
  264.4 1.4 pad_maximum_fusion
  265.8 2.2 copy-done.3
  268.0 4.4 %state_grads.1 = bf16[512,512]{1,0:T(8,128)(2,1)} custom-call(s32[8]{0:T(128)S(1)} %fusion.14.order_ref, bf16[8,2,256,512]{3,2,1,0:T(8,128)(2,1)S(1)} %bitcast.65, bf16[512,256]{1,0:T(8,128)(2,1)S(1)} %get-tuple-element.79.refs_0_, bf16[512,256]{1,0:T(8,128)(2,1)S(1)} %get-tuple-element.80.refs_1_, bf16[512,256]{1,0:T(8,128)(2,1)S(1)} %collective-permute-done.28.refs_2_, ...), custom_call_target="tpu_custom_call" | custom-call | flops 2147483648 | bytes 8388608 | tf_op jit(solution)/shard_map/state_grads/pallas_call | solution.py:278
  (191 shorter events, 41.9 us)
Async XLA Ops:
  7.2 258.6 %all-gather.3.cloned.1.call-start = ((), (), s32[]{:S(2)}) async-start(), calls=%async_computation | async-start | bytes 4718592 | tf_op jit(solution)/shard_map/all_gather | solution.py:469
  10.0 77.5 %copy-start.45 = (bf16[1,512,512]{2,1,0:T(8,128)(2,1)S(1)}, bf16[1,512,512]{2,1,0:T(8,128)(2,1)}, u32[]{:S(2)}) copy-start(bf16[1,512,512]{2,1,0:T(8,128)(2,1)} %param.11) | copy-start | bytes 1572868
  10.0 77.5 %copy-start.46 = (bf16[1,512,512]{2,1,0:T(8,128)(2,1)S(1)}, bf16[1,512,512]{2,1,0:T(8,128)(2,1)}, u32[]{:S(2)}) copy-start(bf16[1,512,512]{2,1,0:T(8,128)(2,1)} %param.12) | copy-start | bytes 1572868
  13.5 6.6 %collective-permute-start.14 = (bf16[16,16,256]{2,1,0:T(8,128)(2,1)S(1)}, bf16[16,16,256]{2,1,0:T(8,128)(2,1)S(1)}, u32[]{:S(2)}, u32[]{:S(2)}) collective-permute-start(bf16[16,16,256]{2,1,0:T(8,128)(2,1)S(1)} %get-tuple-element.63), channel_id=1, source_target_pairs={{0,4},{4,0},{8,12},{12,8},{16,20},{20,16},{24,28},{28,24},{1,5},{5... | collective-permute-start | bytes 393224 | tf_op jit(solution)/shard_map/ppermute | solution.py:291
  20.1 6.4 %collective-permute-start = (bf16[16,16,256]{2,1,0:T(8,128)(2,1)S(1)}, bf16[16,16,256]{2,1,0:T(8,128)(2,1)S(1)}, u32[]{:S(2)}, u32[]{:S(2)}) collective-permute-start(bf16[16,16,256]{2,1,0:T(8,128)(2,1)S(1)} %get-tuple-element.47), channel_id=1, source_target_pairs={{0,4},{4,0},{8,12},{12,8},{16,20},{20,16},{24,28},{28,24},{1,5},{5... | collective-permute-start | bytes 393224 | tf_op jit(solution)/shard_map/ppermute | solution.py:291
  21.9 14.4 %collective-permute-start.1 = (bf16[16,16,256]{2,1,0:T(8,128)(2,1)S(1)}, bf16[16,16,256]{2,1,0:T(8,128)(2,1)S(1)}, u32[]{:S(2)}, u32[]{:S(2)}) collective-permute-start(bf16[16,16,256]{2,1,0:T(8,128)(2,1)S(1)} %get-tuple-element.48), channel_id=1, source_target_pairs={{0,8},{4,12},{8,0},{12,4},{16,24},{20,28},{24,16},{28,20},{1,9},{5... | collective-permute-start | bytes 393224 | tf_op jit(solution)/shard_map/ppermute | solution.py:291
  24.5 11.8 %collective-permute-start.2 = (bf16[16,16,256]{2,1,0:T(8,128)(2,1)S(1)}, bf16[16,16,256]{2,1,0:T(8,128)(2,1)S(1)}, u32[]{:S(2)}, u32[]{:S(2)}) collective-permute-start(bf16[16,16,256]{2,1,0:T(8,128)(2,1)S(1)} %get-tuple-element.49), channel_id=1, source_target_pairs={{0,12},{4,8},{8,4},{12,0},{16,28},{20,24},{24,20},{28,16},{1,13},{... | collective-permute-start | bytes 393224 | tf_op jit(solution)/shard_map/ppermute | solution.py:291
  24.6 34.0 %collective-permute-start.3 = (bf16[16,16,256]{2,1,0:T(8,128)(2,1)S(1)}, bf16[16,16,256]{2,1,0:T(8,128)(2,1)S(1)}, u32[]{:S(2)}, u32[]{:S(2)}) collective-permute-start(bf16[16,16,256]{2,1,0:T(8,128)(2,1)S(1)} %get-tuple-element.50), channel_id=1, source_target_pairs={{0,16},{4,20},{8,24},{12,28},{16,0},{20,4},{24,8},{28,12},{1,17},{... | collective-permute-start | bytes 393224 | tf_op jit(solution)/shard_map/ppermute | solution.py:291
  24.6 34.1 %collective-permute-start.4 = (bf16[16,16,256]{2,1,0:T(8,128)(2,1)S(1)}, bf16[16,16,256]{2,1,0:T(8,128)(2,1)S(1)}, u32[]{:S(2)}, u32[]{:S(2)}) collective-permute-start(bf16[16,16,256]{2,1,0:T(8,128)(2,1)S(1)} %get-tuple-element.51), channel_id=1, source_target_pairs={{0,20},{4,16},{8,28},{12,24},{16,4},{20,0},{24,12},{28,8},{1,21},{... | collective-permute-start | bytes 393224 | tf_op jit(solution)/shard_map/ppermute | solution.py:291
  26.6 32.2 %collective-permute-start.5 = (bf16[16,16,256]{2,1,0:T(8,128)(2,1)S(1)}, bf16[16,16,256]{2,1,0:T(8,128)(2,1)S(1)}, u32[]{:S(2)}, u32[]{:S(2)}) collective-permute-start(bf16[16,16,256]{2,1,0:T(8,128)(2,1)S(1)} %get-tuple-element.52), channel_id=1, source_target_pairs={{0,24},{4,28},{8,16},{12,20},{16,8},{20,12},{24,0},{28,4},{1,25},{... | collective-permute-start | bytes 393224 | tf_op jit(solution)/shard_map/ppermute | solution.py:291
  36.3 23.0 %collective-permute-start.6 = (bf16[16,16,256]{2,1,0:T(8,128)(2,1)S(1)}, bf16[16,16,256]{2,1,0:T(8,128)(2,1)S(1)}, u32[]{:S(2)}, u32[]{:S(2)}) collective-permute-start(bf16[16,16,256]{2,1,0:T(8,128)(2,1)S(1)} %get-tuple-element.53), channel_id=1, source_target_pairs={{0,28},{4,24},{8,20},{12,16},{16,12},{20,8},{24,4},{28,0},{1,29},{... | collective-permute-start | bytes 393224 | tf_op jit(solution)/shard_map/ppermute | solution.py:291
  36.3 51.2 %collective-permute-start.15 = (bf16[16,16,256]{2,1,0:T(8,128)(2,1)S(1)}, bf16[16,16,256]{2,1,0:T(8,128)(2,1)S(1)}, u32[]{:S(2)}, u32[]{:S(2)}) collective-permute-start(bf16[16,16,256]{2,1,0:T(8,128)(2,1)S(1)} %get-tuple-element.64), channel_id=1, source_target_pairs={{0,8},{4,12},{8,0},{12,4},{16,24},{20,28},{24,16},{28,20},{1,9},{5... | collective-permute-start | bytes 393224 | tf_op jit(solution)/shard_map/ppermute | solution.py:291
  58.6 43.1 %collective-permute-start.16 = (bf16[16,16,256]{2,1,0:T(8,128)(2,1)S(1)}, bf16[16,16,256]{2,1,0:T(8,128)(2,1)S(1)}, u32[]{:S(2)}, u32[]{:S(2)}) collective-permute-start(bf16[16,16,256]{2,1,0:T(8,128)(2,1)S(1)} %get-tuple-element.65), channel_id=1, source_target_pairs={{0,12},{4,8},{8,4},{12,0},{16,28},{20,24},{24,20},{28,16},{1,13},{... | collective-permute-start | bytes 393224 | tf_op jit(solution)/shard_map/ppermute | solution.py:291
  58.6 44.6 %collective-permute-start.17 = (bf16[16,16,256]{2,1,0:T(8,128)(2,1)S(1)}, bf16[16,16,256]{2,1,0:T(8,128)(2,1)S(1)}, u32[]{:S(2)}, u32[]{:S(2)}) collective-permute-start(bf16[16,16,256]{2,1,0:T(8,128)(2,1)S(1)} %get-tuple-element.66), channel_id=1, source_target_pairs={{0,16},{4,20},{8,24},{12,28},{16,0},{20,4},{24,8},{28,12},{1,17},{... | collective-permute-start | bytes 393224 | tf_op jit(solution)/shard_map/ppermute | solution.py:291
  58.7 44.5 %collective-permute-start.18 = (bf16[16,16,256]{2,1,0:T(8,128)(2,1)S(1)}, bf16[16,16,256]{2,1,0:T(8,128)(2,1)S(1)}, u32[]{:S(2)}, u32[]{:S(2)}) collective-permute-start(bf16[16,16,256]{2,1,0:T(8,128)(2,1)S(1)} %get-tuple-element.67), channel_id=1, source_target_pairs={{0,20},{4,16},{8,28},{12,24},{16,4},{20,0},{24,12},{28,8},{1,21},{... | collective-permute-start | bytes 393224 | tf_op jit(solution)/shard_map/ppermute | solution.py:291
  59.3 43.9 %collective-permute-start.19 = (bf16[16,16,256]{2,1,0:T(8,128)(2,1)S(1)}, bf16[16,16,256]{2,1,0:T(8,128)(2,1)S(1)}, u32[]{:S(2)}, u32[]{:S(2)}) collective-permute-start(bf16[16,16,256]{2,1,0:T(8,128)(2,1)S(1)} %get-tuple-element.68), channel_id=1, source_target_pairs={{0,24},{4,28},{8,16},{12,20},{16,8},{20,12},{24,0},{28,4},{1,25},{... | collective-permute-start | bytes 393224 | tf_op jit(solution)/shard_map/ppermute | solution.py:291
  87.5 15.7 %collective-permute-start.20 = (bf16[16,16,256]{2,1,0:T(8,128)(2,1)S(1)}, bf16[16,16,256]{2,1,0:T(8,128)(2,1)S(1)}, u32[]{:S(2)}, u32[]{:S(2)}) collective-permute-start(bf16[16,16,256]{2,1,0:T(8,128)(2,1)S(1)} %get-tuple-element.69), channel_id=1, source_target_pairs={{0,28},{4,24},{8,20},{12,16},{16,12},{20,8},{24,4},{28,0},{1,29},{... | collective-permute-start | bytes 393224 | tf_op jit(solution)/shard_map/ppermute | solution.py:291
  101.7 15.0 %copy-start.52 = (bf16[128,256]{1,0:T(8,128)(2,1)}, bf16[128,256]{1,0:T(8,128)(2,1)S(1)}, u32[]{:S(2)}) copy-start(bf16[128,256]{1,0:T(8,128)(2,1)S(1)} %get-tuple-element.61) | copy-start | bytes 196612
  101.7 15.0 %copy-start.56 = (bf16[128,256]{1,0:T(8,128)(2,1)}, bf16[128,256]{1,0:T(8,128)(2,1)S(1)}, u32[]{:S(2)}) copy-start(bf16[128,256]{1,0:T(8,128)(2,1)S(1)} %get-tuple-element.57) | copy-start | bytes 196612
  101.7 15.0 %copy-start.57 = (bf16[128,256]{1,0:T(8,128)(2,1)}, bf16[128,256]{1,0:T(8,128)(2,1)S(1)}, u32[]{:S(2)}) copy-start(bf16[128,256]{1,0:T(8,128)(2,1)S(1)} %get-tuple-element.56) | copy-start | bytes 196612
  101.7 22.8 %collective-permute-start.28 = (bf16[512,256]{1,0:T(8,128)(2,1)S(1)}, bf16[512,256]{1,0:T(8,128)(2,1)S(1)}, u32[]{:S(2)}, u32[]{:S(2)}) collective-permute-start(bf16[512,256]{1,0:T(8,128)(2,1)S(1)} %get-tuple-element.79.refs_0_), channel_id=1, source_target_pairs={{0,1},{1,0},{2,3},{3,2},{4,5},{5,4},{6,7},{7,6},{8,9},{9,8},{10,11... | collective-permute-start | bytes 786440 | tf_op jit(solution)/shard_map/ppermute | solution.py:291
  120.4 6.4 %collective-permute-start.34 = (bf16[512,256]{1,0:T(8,128)(2,1)S(1)}, bf16[512,256]{1,0:T(8,128)(2,1)S(1)}, u32[]{:S(2)}, u32[]{:S(2)}) collective-permute-start(bf16[512,256]{1,0:T(8,128)(2,1)S(1)} %get-tuple-element.81.refs_8_.refs_0_), channel_id=1, source_target_pairs={{0,1},{1,0},{2,3},{3,2},{4,5},{5,4},{6,7},{7,6},{8,9},{9,8},{10,11... | collective-permute-start | bytes 786440 | tf_op jit(solution)/shard_map/ppermute | solution.py:291
  121.0 8.1 %collective-permute-start.37 = (bf16[512,256]{1,0:T(8,128)(2,1)S(1)}, bf16[512,256]{1,0:T(8,128)(2,1)S(1)}, u32[]{:S(2)}, u32[]{:S(2)}) collective-permute-start(bf16[512,256]{1,0:T(8,128)(2,1)S(1)} %get-tuple-element.82.refs_9_.refs_1_), channel_id=1, source_target_pairs={{0,2},{1,3},{2,0},{3,1},{4,6},{5,7},{6,4},{7,5},{8,10},{9,11},{10,... | collective-permute-start | bytes 786440 | tf_op jit(solution)/shard_map/ppermute | solution.py:291
  122.5 10.7 %collective-permute-start.31 = (bf16[512,256]{1,0:T(8,128)(2,1)S(1)}, bf16[512,256]{1,0:T(8,128)(2,1)}, u32[]{:S(2)}, u32[]{:S(2)}) collective-permute-start(bf16[512,256]{1,0:T(8,128)(2,1)S(1)} %get-tuple-element.80.refs_1_), channel_id=1, source_target_pairs={{0,2},{1,3},{2,0},{3,1},{4,6},{5,7},{6,4},{7,5},{8,10},{9,11},{10,... | collective-permute-start | bytes 786440 | tf_op jit(solution)/shard_map/ppermute | solution.py:291
  123.0 11.7 %collective-permute-start.35 = (bf16[512,256]{1,0:T(8,128)(2,1)S(1)}, bf16[512,256]{1,0:T(8,128)(2,1)S(1)}, u32[]{:S(2)}, u32[]{:S(2)}) collective-permute-start(bf16[512,256]{1,0:T(8,128)(2,1)S(1)} %get-tuple-element.82.refs_9_.refs_1_), channel_id=1, source_target_pairs={{0,1},{1,0},{2,3},{3,2},{4,5},{5,4},{6,7},{7,6},{8,9},{9,8},{10,11... | collective-permute-start | bytes 786440 | tf_op jit(solution)/shard_map/ppermute | solution.py:291
  124.5 14.2 %collective-permute-start.36 = (bf16[512,256]{1,0:T(8,128)(2,1)S(1)}, bf16[512,256]{1,0:T(8,128)(2,1)S(1)}, u32[]{:S(2)}, u32[]{:S(2)}) collective-permute-start(bf16[512,256]{1,0:T(8,128)(2,1)S(1)} %get-tuple-element.81.refs_8_.refs_0_), channel_id=1, source_target_pairs={{0,2},{1,3},{2,0},{3,1},{4,6},{5,7},{6,4},{7,5},{8,10},{9,11},{10,... | collective-permute-start | bytes 786440 | tf_op jit(solution)/shard_map/ppermute | solution.py:291
  126.8 17.5 %collective-permute-start.38 = (bf16[512,256]{1,0:T(8,128)(2,1)S(1)}, bf16[512,256]{1,0:T(8,128)(2,1)S(1)}, u32[]{:S(2)}, u32[]{:S(2)}) collective-permute-start(bf16[512,256]{1,0:T(8,128)(2,1)S(1)} %collective-permute-done.34.refs_10_.refs_2_), channel_id=1, source_target_pairs={{0,2},{1,3},{2,0},{3,1},{4,6},{5,7},{6,4},{7,5},{8,10},{9,11},{10,... | collective-permute-start | bytes 786440 | tf_op jit(solution)/shard_map/ppermute | solution.py:291
  129.0 17.7 %collective-permute-start.39 = (bf16[512,256]{1,0:T(8,128)(2,1)S(1)}, bf16[512,256]{1,0:T(8,128)(2,1)S(1)}, u32[]{:S(2)}, u32[]{:S(2)}) collective-permute-start(bf16[512,256]{1,0:T(8,128)(2,1)S(1)} %collective-permute-done.37.refs_13_.refs_5_), channel_id=1, source_target_pairs={{0,1},{1,0},{2,3},{3,2},{4,5},{5,4},{6,7},{7,6},{8,9},{9,8},{10,11... | collective-permute-start | bytes 786440 | tf_op jit(solution)/shard_map/ppermute | solution.py:291
  133.2 30.6 %collective-permute-start.29 = (bf16[512,256]{1,0:T(8,128)(2,1)S(1)}, bf16[512,256]{1,0:T(8,128)(2,1)}, u32[]{:S(2)}, u32[]{:S(2)}) collective-permute-start(bf16[512,256]{1,0:T(8,128)(2,1)S(1)} %get-tuple-element.80.refs_1_), channel_id=1, source_target_pairs={{0,1},{1,0},{2,3},{3,2},{4,5},{5,4},{6,7},{7,6},{8,9},{9,8},{10,11... | collective-permute-start | bytes 786440 | tf_op jit(solution)/shard_map/ppermute | solution.py:291
  135.4 28.3 %collective-permute-start.30 = (bf16[512,256]{1,0:T(8,128)(2,1)S(1)}, bf16[512,256]{1,0:T(8,128)(2,1)}, u32[]{:S(2)}, u32[]{:S(2)}) collective-permute-start(bf16[512,256]{1,0:T(8,128)(2,1)S(1)} %get-tuple-element.79.refs_0_), channel_id=1, source_target_pairs={{0,2},{1,3},{2,0},{3,1},{4,6},{5,7},{6,4},{7,5},{8,10},{9,11},{10,... | collective-permute-start | bytes 786440 | tf_op jit(solution)/shard_map/ppermute | solution.py:291
  139.4 24.4 %collective-permute-start.32 = (bf16[512,256]{1,0:T(8,128)(2,1)S(1)}, bf16[512,256]{1,0:T(8,128)(2,1)}, u32[]{:S(2)}, u32[]{:S(2)}) collective-permute-start(bf16[512,256]{1,0:T(8,128)(2,1)S(1)} %collective-permute-done.28.refs_2_), channel_id=1, source_target_pairs={{0,2},{1,3},{2,0},{3,1},{4,6},{5,7},{6,4},{7,5},{8,10},{9,11},{10,... | collective-permute-start | bytes 786440 | tf_op jit(solution)/shard_map/ppermute | solution.py:291
  145.0 18.8 %collective-permute-start.33 = (bf16[512,256]{1,0:T(8,128)(2,1)}, bf16[512,256]{1,0:T(8,128)(2,1)}, u32[]{:S(2)}, u32[]{:S(2)}) collective-permute-start(bf16[512,256]{1,0:T(8,128)(2,1)} %collective-permute-done.31.refs_5_), channel_id=1, source_target_pairs={{0,1},{1,0},{2,3},{3,2},{4,5},{5,4},{6,7},{7,6},{8,9},{9,8},{10,11... | collective-permute-start | bytes 786440 | tf_op jit(solution)/shard_map/ppermute | solution.py:291
  158.5 12.9 %collective-permute-start.47 = (bf16[4,256,512]{2,1,0:T(8,128)(2,1)}, bf16[4,256,512]{2,1,0:T(8,128)(2,1)}, u32[]{:S(2)}, u32[]{:S(2)}) collective-permute-start(bf16[4,256,512]{2,1,0:T(8,128)(2,1)} %get-tuple-element.86), channel_id=1, source_target_pairs={{0,16},{16,0},{1,17},{17,1},{2,18},{18,2},{3,19},{19,3},{4,20},{20... | collective-permute-start | bytes 3145736 | tf_op jit(solution)/shard_map/ppermute | solution.py:291
  171.4 4.2 %collective-permute-start.40 = (bf16[4,256,512]{2,1,0:T(8,128)(2,1)}, bf16[4,256,512]{2,1,0:T(8,128)(2,1)}, u32[]{:S(2)}, u32[]{:S(2)}) collective-permute-start(bf16[4,256,512]{2,1,0:T(8,128)(2,1)} %get-tuple-element.84), channel_id=1, source_target_pairs={{0,16},{16,0},{1,17},{17,1},{2,18},{18,2},{3,19},{19,3},{4,20},{20... | collective-permute-start | bytes 3145736 | tf_op jit(solution)/shard_map/ppermute | solution.py:291
  171.4 4.2 %copy-start.1 = (f32[4,256,512]{2,1,0:T(8,128)S(1)}, f32[4,256,512]{2,1,0:T(8,128)}, u32[]{:S(2)}) copy-start(f32[4,256,512]{2,1,0:T(8,128)} %copy-done) | copy-start | bytes 6291460
  173.5 8.3 %collective-permute-start.48 = (bf16[256,512]{1,0:T(8,128)(2,1)}, bf16[256,512]{1,0:T(8,128)(2,1)}, u32[]{:S(2)}, u32[]{:S(2)}) collective-permute-start(bf16[256,512]{1,0:T(8,128)(2,1)} %get-tuple-element.93), channel_id=1, source_target_pairs={{0,4},{1,5},{2,6},{3,7},{16,20},{17,21},{18,22},{19,23}} | collective-permute-start | bytes 786440 | tf_op jit(solution)/shard_map/ppermute | solution.py:324
  177.6 12.6 %collective-permute-start.41 = (bf16[256,512]{1,0:T(8,128)(2,1)}, bf16[256,512]{1,0:T(8,128)(2,1)}, u32[]{:S(2)}, u32[]{:S(2)}) collective-permute-start(bf16[256,512]{1,0:T(8,128)(2,1)} %get-tuple-element.89), channel_id=1, source_target_pairs={{0,4},{1,5},{2,6},{3,7},{16,20},{17,21},{18,22},{19,23}} | collective-permute-start | bytes 786440 | tf_op jit(solution)/shard_map/ppermute | solution.py:324
  179.6 14.8 %collective-permute-start.51 = (bf16[256,512]{1,0:T(8,128)(2,1)}, bf16[256,512]{1,0:T(8,128)(2,1)}, u32[]{:S(2)}, u32[]{:S(2)}) collective-permute-start(bf16[256,512]{1,0:T(8,128)(2,1)} %get-tuple-element.94), channel_id=1, source_target_pairs={{12,8},{13,9},{14,10},{15,11},{28,24},{29,25},{30,26},{31,27}} | collective-permute-start | bytes 786440 | tf_op jit(solution)/shard_map/ppermute | solution.py:327
  183.7 10.7 %collective-permute-start.49 = (bf16[256,512]{1,0:T(8,128)(2,1)}, bf16[256,512]{1,0:T(8,128)(2,1)}, u32[]{:S(2)}, u32[]{:S(2)}) collective-permute-start(bf16[256,512]{1,0:T(8,128)(2,1)} %fusion.2), channel_id=1, source_target_pairs={{0,4},{4,8},{1,5},{5,9},{2,6},{6,10},{3,7},{7,11},{16,20},{20,24},... | collective-permute-start | bytes 786440 | tf_op jit(solution)/shard_map/ppermute | solution.py:324
  188.8 15.8 %collective-permute-start.44 = (bf16[256,512]{1,0:T(8,128)(2,1)}, bf16[256,512]{1,0:T(8,128)(2,1)}, u32[]{:S(2)}, u32[]{:S(2)}) collective-permute-start(bf16[256,512]{1,0:T(8,128)(2,1)} %get-tuple-element.90), channel_id=1, source_target_pairs={{12,8},{13,9},{14,10},{15,11},{28,24},{29,25},{30,26},{31,27}} | collective-permute-start | bytes 786440 | tf_op jit(solution)/shard_map/ppermute | solution.py:327
  192.1 13.4 %collective-permute-start.42 = (bf16[256,512]{1,0:T(8,128)(2,1)}, bf16[256,512]{1,0:T(8,128)(2,1)}, u32[]{:S(2)}, u32[]{:S(2)}) collective-permute-start(bf16[256,512]{1,0:T(8,128)(2,1)} %fusion.7), channel_id=1, source_target_pairs={{0,4},{4,8},{1,5},{5,9},{2,6},{6,10},{3,7},{7,11},{16,20},{20,24},... | collective-permute-start | bytes 786440 | tf_op jit(solution)/shard_map/ppermute | solution.py:324
  194.3 12.6 %copy-start.2 = (f32[4,256,512]{2,1,0:T(8,128)S(1)}, f32[4,256,512]{2,1,0:T(8,128)}, u32[]{:S(2)}) copy-start(f32[4,256,512]{2,1,0:T(8,128)} %copy-done) | copy-start | bytes 6291460
  194.3 7.7 %collective-permute-start.7 = (bf16[128,256]{1,0:T(8,128)(2,1)}, bf16[128,256]{1,0:T(8,128)(2,1)S(1)}, u32[]{:S(2)}, u32[]{:S(2)}) collective-permute-start(bf16[128,256]{1,0:T(8,128)(2,1)} %copy-done.58), channel_id=1, source_target_pairs={{0,4},{4,0},{8,12},{12,8},{16,20},{20,16},{24,28},{28,24},{1,5},{5... | collective-permute-start | bytes 196616 | tf_op jit(solution)/shard_map/ppermute | solution.py:291
  194.3 8.8 %collective-permute-start.8 = (bf16[128,256]{1,0:T(8,128)(2,1)}, bf16[128,256]{1,0:T(8,128)(2,1)S(1)}, u32[]{:S(2)}, u32[]{:S(2)}) collective-permute-start(bf16[128,256]{1,0:T(8,128)(2,1)} %copy-done.57), channel_id=1, source_target_pairs={{0,8},{4,12},{8,0},{12,4},{16,24},{20,28},{24,16},{28,20},{1,9},{5... | collective-permute-start | bytes 196616 | tf_op jit(solution)/shard_map/ppermute | solution.py:291
  194.4 14.8 %collective-permute-start.9 = (bf16[128,256]{1,0:T(8,128)(2,1)}, bf16[128,256]{1,0:T(8,128)(2,1)S(1)}, u32[]{:S(2)}, u32[]{:S(2)}) collective-permute-start(bf16[128,256]{1,0:T(8,128)(2,1)} %copy-done.56), channel_id=1, source_target_pairs={{0,12},{4,8},{8,4},{12,0},{16,28},{20,24},{24,20},{28,16},{1,13},{... | collective-permute-start | bytes 196616 | tf_op jit(solution)/shard_map/ppermute | solution.py:291
  202.0 7.2 %copy-start.24 = (bf16[128,256]{1,0:T(8,128)(2,1)}, bf16[128,256]{1,0:T(8,128)(2,1)S(1)}, u32[]{:S(2)}) copy-start(bf16[128,256]{1,0:T(8,128)(2,1)S(1)} %collective-permute-done.7.refs_1_) | copy-start | bytes 196612
  202.0 9.2 %collective-permute-start.10 = (bf16[128,256]{1,0:T(8,128)(2,1)}, bf16[128,256]{1,0:T(8,128)(2,1)}, u32[]{:S(2)}, u32[]{:S(2)}) collective-permute-start(bf16[128,256]{1,0:T(8,128)(2,1)} %get-tuple-element.58), channel_id=1, source_target_pairs={{0,16},{4,20},{8,24},{12,28},{16,0},{20,4},{24,8},{28,12},{1,17},{... | collective-permute-start | bytes 196616 | tf_op jit(solution)/shard_map/ppermute | solution.py:291
  203.1 6.1 %copy-start.26 = (bf16[128,256]{1,0:T(8,128)(2,1)}, bf16[128,256]{1,0:T(8,128)(2,1)S(1)}, u32[]{:S(2)}) copy-start(bf16[128,256]{1,0:T(8,128)(2,1)S(1)} %collective-permute-done.8.refs_2_) | copy-start | bytes 196612
  203.1 12.8 %collective-permute-start.11 = (bf16[128,256]{1,0:T(8,128)(2,1)}, bf16[128,256]{1,0:T(8,128)(2,1)}, u32[]{:S(2)}, u32[]{:S(2)}) collective-permute-start(bf16[128,256]{1,0:T(8,128)(2,1)} %get-tuple-element.59), channel_id=1, source_target_pairs={{0,20},{4,16},{8,28},{12,24},{16,4},{20,0},{24,12},{28,8},{1,21},{... | collective-permute-start | bytes 196616 | tf_op jit(solution)/shard_map/ppermute | solution.py:291
  204.5 11.4 %collective-permute-start.12 = (bf16[128,256]{1,0:T(8,128)(2,1)}, bf16[128,256]{1,0:T(8,128)(2,1)}, u32[]{:S(2)}, u32[]{:S(2)}) collective-permute-start(bf16[128,256]{1,0:T(8,128)(2,1)} %get-tuple-element.60), channel_id=1, source_target_pairs={{0,24},{4,28},{8,16},{12,20},{16,8},{20,12},{24,0},{28,4},{1,25},{... | collective-permute-start | bytes 196616 | tf_op jit(solution)/shard_map/ppermute | solution.py:291
  205.6 13.7 %collective-permute-start.52 = (bf16[256,512]{1,0:T(8,128)(2,1)}, bf16[256,512]{1,0:T(8,128)(2,1)}, u32[]{:S(2)}, u32[]{:S(2)}) collective-permute-start(bf16[256,512]{1,0:T(8,128)(2,1)} %get-tuple-element.92), channel_id=1, source_target_pairs={{12,8},{8,4},{13,9},{9,5},{14,10},{10,6},{15,11},{11,7},{28,24},{2... | collective-permute-start | bytes 786440 | tf_op jit(solution)/shard_map/ppermute | solution.py:327
  209.8 26.4 %collective-permute-start.45 = (bf16[256,512]{1,0:T(8,128)(2,1)}, bf16[256,512]{1,0:T(8,128)(2,1)}, u32[]{:S(2)}, u32[]{:S(2)}) collective-permute-start(bf16[256,512]{1,0:T(8,128)(2,1)} %get-tuple-element.88), channel_id=1, source_target_pairs={{12,8},{8,4},{13,9},{9,5},{14,10},{10,6},{15,11},{11,7},{28,24},{2... | collective-permute-start | bytes 786440 | tf_op jit(solution)/shard_map/ppermute | solution.py:327
  211.2 11.0 %collective-permute-start.13 = (bf16[128,256]{1,0:T(8,128)(2,1)}, bf16[128,256]{1,0:T(8,128)(2,1)S(1)}, u32[]{:S(2)}, u32[]{:S(2)}) collective-permute-start(bf16[128,256]{1,0:T(8,128)(2,1)} %copy-done.52), channel_id=1, source_target_pairs={{0,28},{4,24},{8,20},{12,16},{16,12},{20,8},{24,4},{28,0},{1,29},{... | collective-permute-start | bytes 196616 | tf_op jit(solution)/shard_map/ppermute | solution.py:291
  215.9 11.1 %collective-permute-start.21 = (bf16[128,256]{1,0:T(8,128)(2,1)}, bf16[128,256]{1,0:T(8,128)(2,1)S(1)}, u32[]{:S(2)}, u32[]{:S(2)}) collective-permute-start(bf16[128,256]{1,0:T(8,128)(2,1)} %copy-done.55), channel_id=1, source_target_pairs={{0,4},{4,0},{8,12},{12,8},{16,20},{20,16},{24,28},{28,24},{1,5},{5... | collective-permute-start | bytes 196616 | tf_op jit(solution)/shard_map/ppermute | solution.py:291
  215.9 15.1 %collective-permute-start.22 = (bf16[128,256]{1,0:T(8,128)(2,1)}, bf16[128,256]{1,0:T(8,128)(2,1)S(1)}, u32[]{:S(2)}, u32[]{:S(2)}) collective-permute-start(bf16[128,256]{1,0:T(8,128)(2,1)} %copy-done.54), channel_id=1, source_target_pairs={{0,8},{4,12},{8,0},{12,4},{16,24},{20,28},{24,16},{28,20},{1,9},{5... | collective-permute-start | bytes 196616 | tf_op jit(solution)/shard_map/ppermute | solution.py:291
  219.2 12.4 %collective-permute-start.23 = (bf16[128,256]{1,0:T(8,128)(2,1)}, bf16[128,256]{1,0:T(8,128)(2,1)S(1)}, u32[]{:S(2)}, u32[]{:S(2)}) collective-permute-start(bf16[128,256]{1,0:T(8,128)(2,1)} %copy-done.53), channel_id=1, source_target_pairs={{0,12},{4,8},{8,4},{12,0},{16,28},{20,24},{24,20},{28,16},{1,13},{... | collective-permute-start | bytes 196616 | tf_op jit(solution)/shard_map/ppermute | solution.py:291
  222.8 16.7 %collective-permute-start.24 = (bf16[128,256]{1,0:T(8,128)(2,1)}, bf16[128,256]{1,0:T(8,128)(2,1)S(1)}, u32[]{:S(2)}, u32[]{:S(2)}) collective-permute-start(bf16[128,256]{1,0:T(8,128)(2,1)} %copy-done.51), channel_id=1, source_target_pairs={{0,16},{4,20},{8,24},{12,28},{16,0},{20,4},{24,8},{28,12},{1,17},{... | collective-permute-start | bytes 196616 | tf_op jit(solution)/shard_map/ppermute | solution.py:291
  227.6 15.7 %collective-permute-start.25 = (bf16[128,256]{1,0:T(8,128)(2,1)}, bf16[128,256]{1,0:T(8,128)(2,1)S(1)}, u32[]{:S(2)}, u32[]{:S(2)}) collective-permute-start(bf16[128,256]{1,0:T(8,128)(2,1)} %copy-done.50), channel_id=1, source_target_pairs={{0,20},{4,16},{8,28},{12,24},{16,4},{20,0},{24,12},{28,8},{1,21},{... | collective-permute-start | bytes 196616 | tf_op jit(solution)/shard_map/ppermute | solution.py:291
  231.6 15.0 %collective-permute-start.26 = (bf16[128,256]{1,0:T(8,128)(2,1)}, bf16[128,256]{1,0:T(8,128)(2,1)S(1)}, u32[]{:S(2)}, u32[]{:S(2)}) collective-permute-start(bf16[128,256]{1,0:T(8,128)(2,1)} %copy-done.49), channel_id=1, source_target_pairs={{0,24},{4,28},{8,16},{12,20},{16,8},{20,12},{24,0},{28,4},{1,25},{... | collective-permute-start | bytes 196616 | tf_op jit(solution)/shard_map/ppermute | solution.py:291
  232.2 28.5 %collective-permute-start.50 = (bf16[256,512]{1,0:T(8,128)(2,1)}, bf16[256,512]{1,0:T(8,128)(2,1)}, u32[]{:S(2)}, u32[]{:S(2)}) collective-permute-start(bf16[256,512]{1,0:T(8,128)(2,1)} %get-tuple-element.91), channel_id=1, source_target_pairs={{0,4},{4,8},{8,12},{1,5},{5,9},{9,13},{2,6},{6,10},{10,14},{3,7},{... | collective-permute-start | bytes 786440 | tf_op jit(solution)/shard_map/ppermute | solution.py:324
  236.2 24.5 %collective-permute-start.53 = (bf16[256,512]{1,0:T(8,128)(2,1)}, bf16[256,512]{1,0:T(8,128)(2,1)}, u32[]{:S(2)}, u32[]{:S(2)}) collective-permute-start(bf16[256,512]{1,0:T(8,128)(2,1)} %fusion.1), channel_id=1, source_target_pairs={{12,8},{8,4},{4,0},{13,9},{9,5},{5,1},{14,10},{10,6},{6,2},{15,11}... | collective-permute-start | bytes 786440 | tf_op jit(solution)/shard_map/ppermute | solution.py:327
  240.1 8.4 %collective-permute-start.27 = (bf16[128,256]{1,0:T(8,128)(2,1)}, bf16[128,256]{1,0:T(8,128)(2,1)}, u32[]{:S(2)}, u32[]{:S(2)}) collective-permute-start(bf16[128,256]{1,0:T(8,128)(2,1)} %get-tuple-element.77), channel_id=1, source_target_pairs={{0,28},{4,24},{8,20},{12,16},{16,12},{20,8},{24,4},{28,0},{1,29},{... | collective-permute-start | bytes 196616 | tf_op jit(solution)/shard_map/ppermute | solution.py:291
  243.9 18.5 %collective-permute-start.43 = (bf16[256,512]{1,0:T(8,128)(2,1)}, bf16[256,512]{1,0:T(8,128)(2,1)}, u32[]{:S(2)}, u32[]{:S(2)}) collective-permute-start(bf16[256,512]{1,0:T(8,128)(2,1)} %get-tuple-element.87), channel_id=1, source_target_pairs={{0,4},{4,8},{8,12},{1,5},{5,9},{9,13},{2,6},{6,10},{10,14},{3,7},{... | collective-permute-start | bytes 786440 | tf_op jit(solution)/shard_map/ppermute | solution.py:324
  247.2 15.2 %collective-permute-start.46 = (bf16[256,512]{1,0:T(8,128)(2,1)}, bf16[256,512]{1,0:T(8,128)(2,1)}, u32[]{:S(2)}, u32[]{:S(2)}) collective-permute-start(bf16[256,512]{1,0:T(8,128)(2,1)} %fusion.6), channel_id=1, source_target_pairs={{12,8},{8,4},{4,0},{13,9},{9,5},{5,1},{14,10},{10,6},{6,2},{15,11}... | collective-permute-start | bytes 786440 | tf_op jit(solution)/shard_map/ppermute | solution.py:327
  (50 other events, 56.5 us)
Sparse Core Ops, SparseCore 0:
  20.2 82.5 all-gather.2

commit v2 on v1

--- a/solution.py
+++ b/solution.py
@@ -8,13 +8,16 @@
 from jax.sharding import PartitionSpec as P
 
 HEAD_DIM = 64
+CHUNKS = 2
 LANES = 128
 PEERS = ("grp", "seq")
 BF16 = jnp.bfloat16
 F32 = jnp.float32
-VMEM_BYTES = 40 * 1024 * 1024
+VMEM_BYTES = 16 * 1024 * 1024
+ATTEND_BYTES = 24 * 1024 * 1024
 
 VMEM_SPEC = pl.BlockSpec(memory_space=pltpu.VMEM)
+ANY_SPEC = pl.BlockSpec(memory_space=pl.ANY)
 SMEM_SPEC = pl.BlockSpec(memory_space=pltpu.SMEM)
 NT = (((1,), (1,)), ((), ()))
 TN = (((0,), (0,)), ((), ()))
@@ -26,13 +29,21 @@
     )
 
 
-def pack_kernel(peers, per_peer, chunks, me_ref, owners_ref, q_ref, g_ref, *refs):
-    table_ref, out_refs = refs[0], refs[1 : 1 + chunks * peers]
-    both_ref, count_ref = refs[-2:]
+def fetch(sources, targets, sems):
+    copies = []
+    for i, (source, target) in enumerate(zip(sources, targets)):
+        copies.append(pltpu.make_async_copy(source, target, sems.at[i]))
+        copies[-1].start()
+    return copies
+
+
+def pack_kernel(peers, per_peer, chunk, chunks, me_ref, owners_hbm, q_hbm, g_hbm, *refs):
+    both_ref, count_ref, owners_ref, q_ref, g_ref, sems = refs[-6:]
+    table_ref, out_refs = refs[-8 - peers // 2], refs[-7 - peers // 2 : -6]
     targets, rows, width = q_ref.shape
-    both = jnp.concatenate([q_ref[...].astype(F32), g_ref[...].astype(F32)], axis=1)
-    both_ref[:targets] = both.astype(BF16)
-    both_ref[targets] = jnp.zeros((2 * rows, width), BF16)
+    groups = width // (chunks * LANES)
+    copies = fetch([owners_hbm, q_hbm, g_hbm], [owners_ref, q_ref, g_ref], sems)
+    both_ref[targets] = jnp.zeros(both_ref.shape[1:], BF16)
     me = me_ref[0]
 
     def clear_count(i, _):
@@ -51,57 +62,111 @@
         return 0
 
     lax.fori_loop(0, peers, clear_count, 0)
-    lax.fori_loop(0, peers * per_peer, clear_slot, 0)
-    lax.fori_loop(0, targets, place, 0)
-    groups = width // (chunks * LANES)
-    for d in range(peers):
+    lax.fori_loop(0, peers * per_peer, clear_slot, 0, unroll=8)
+    copies[0].wait()
+    lax.fori_loop(0, targets, place, 0, unroll=8)
+    copies[1].wait()
+    copies[2].wait()
+    for a in range(groups):
+        lane = (a * chunks + chunk) * LANES
+        both = jnp.concatenate(
+            [
+                q_ref[:, :, lane : lane + LANES].astype(F32),
+                g_ref[:, :, lane : lane + LANES].astype(F32),
+            ],
+            axis=1,
+        )
+        both_ref[:targets, :, a * LANES : (a + 1) * LANES] = both.astype(BF16)
+    half = peers // 2
+    for d in range(half):
 
         def move(slot, _, d=d):
-            t = table_ref[d * per_peer + slot]
-            for c in range(chunks):
-                for a in range(groups):
-                    lane = (a * chunks + c) * LANES
-                    out_refs[c * peers + d][slot, :, a * LANES : (a + 1) * LANES] = both_ref[
-                        t, :, lane : lane + LANES
-                    ]
+            out_refs[d][slot] = both_ref[table_ref[d * per_peer + slot]]
+            out_refs[half][d, slot] = both_ref[table_ref[(half + d) * per_peer + slot]]
             return 0
 
         lax.fori_loop(0, per_peer, move, 0, unroll=4)
 
 
-def pack(me, owners, queries, out_grads, peers, per_peer, chunks):
+def pack(me, owners, queries, out_grads, peers, per_peer, chunk, chunks):
     targets, rows, width = queries.shape
-    block = jax.ShapeDtypeStruct((per_peer, 2 * rows, width // chunks), BF16)
+    part, half = width // chunks, peers // 2
+    block = (per_peer, 2 * rows, part)
     outs = pl.pallas_call(
-        functools.partial(pack_kernel, peers, per_peer, chunks),
+        functools.partial(pack_kernel, peers, per_peer, chunk, chunks),
         out_shape=[jax.ShapeDtypeStruct((peers * per_peer,), jnp.int32)]
-        + [block] * (chunks * peers),
-        in_specs=[SMEM_SPEC, SMEM_SPEC, VMEM_SPEC, VMEM_SPEC],
-        out_specs=[SMEM_SPEC] + [VMEM_SPEC] * (chunks * peers),
+        + [jax.ShapeDtypeStruct(block, BF16)] * half
+        + [jax.ShapeDtypeStruct((half,) + block, BF16)],
+        in_specs=[SMEM_SPEC, ANY_SPEC, ANY_SPEC, ANY_SPEC],
+        out_specs=[SMEM_SPEC] + [VMEM_SPEC] * (half + 1),
         scratch_shapes=[
-            pltpu.VMEM((targets + 1, 2 * rows, width), BF16),
+            pltpu.VMEM((targets + 1, 2 * rows, part), BF16),
             pltpu.SMEM((peers,), jnp.int32),
+            pltpu.SMEM((targets,), jnp.int32),
+            pltpu.VMEM(queries.shape, BF16),
+            pltpu.VMEM(queries.shape, BF16),
+            pltpu.SemaphoreType.DMA((3,)),
         ],
         compiler_params=pltpu.CompilerParams(vmem_limit_bytes=VMEM_BYTES),
         cost_estimate=cost(0, 3 << 20),
         name="pack_targets",
     )(me, owners, queries, out_grads)
-    return outs[0], [outs[1 + c * peers : 1 + (c + 1) * peers] for c in range(chunks)]
-
-
-def unpack_kernel(peers, per_peer, chunks, table_ref, *refs):
-    in_refs, out_ref, rows_ref = refs[: chunks * peers], refs[-2], refs[-1]
+    return outs[0], outs[1:-1], outs[-1]
+
+
+def hold_kernel(count, *refs):
+    for x_ref, out_ref in zip(refs[:count], refs[-count:]):
+        out_ref[...] = x_ref[...]
+
+
+def hold(arrays, earlier):
+    return pl.pallas_call(
+        functools.partial(hold_kernel, len(arrays)),
+        out_shape=[jax.ShapeDtypeStruct(x.shape, x.dtype) for x in arrays],
+        in_specs=[VMEM_SPEC] * (len(arrays) + len(earlier)),
+        out_specs=[VMEM_SPEC] * len(arrays),
+        compiler_params=pltpu.CompilerParams(vmem_limit_bytes=VMEM_BYTES),
+        cost_estimate=cost(0, 1 << 20),
+        name="hold",
+    )(*arrays, *earlier)
+
+
+def merge_kernel(half, *refs):
+    blocks, got_ref, out_refs = refs[:half], refs[half], refs[-half:]
+    for d in range(half):
+        out_refs[d][0] = blocks[d][...]
+        out_refs[d][1] = got_ref[d]
+
+
+def merge(blocks, got, earlier):
+    half = len(blocks)
+    return pl.pallas_call(
+        functools.partial(merge_kernel, half),
+        out_shape=[jax.ShapeDtypeStruct((2,) + blocks[0].shape, BF16)] * half,
+        in_specs=[VMEM_SPEC] * (half + 1 + len(earlier)),
+        out_specs=[VMEM_SPEC] * half,
+        compiler_params=pltpu.CompilerParams(vmem_limit_bytes=VMEM_BYTES),
+        cost_estimate=cost(0, 1 << 20),
+        name="merge",
+    )(*blocks, got, *earlier)
+
+
+def unpack_kernel(peers, per_peer, table_ref, *refs):
+    half = peers // 2
+    near_refs, over_ref, out_ref = refs[:half], refs[half], refs[half + 1]
+    near_s, over_s, rows_ref, sems = refs[half + 2 :]
     targets, rows, width = out_ref.shape
-    groups = width // (chunks * LANES)
-    for c in range(chunks):
-        for d in range(peers):
-            block = in_refs[c * peers + d][...].astype(F32)
-            block = block.reshape(per_peer, rows, width // chunks)
-            for a in range(groups):
-                lane = (a * chunks + c) * LANES
-                rows_ref[d * per_peer : (d + 1) * per_peer, :, lane : lane + LANES] = block[
-                    :, :, a * LANES : (a + 1) * LANES
-                ]
+    block_rows = per_peer * rows
+    copies = fetch(
+        list(near_refs) + [over_ref], [near_s.at[d] for d in range(half)] + [over_s], sems
+    )
+    for copy in copies:
+        copy.wait()
+    for d in range(peers):
+        block = near_s[d, :block_rows] if d < half else over_s[d - half]
+        rows_ref[d * per_peer : (d + 1) * per_peer] = block.astype(F32).reshape(
+            per_peer, rows, width
+        )
 
     def move(slot, _):
         t = table_ref[slot]
@@ -115,35 +180,41 @@
     lax.fori_loop(0, peers * per_peer, move, 0)
 
 
-def unpack(table, blocks, targets, rows, width, peers, per_peer):
-    chunks = len(blocks)
+def unpack(table, near, over, targets, rows, per_peer):
+    half, width = len(near), near[0].shape[1]
     return pl.pallas_call(
-        functools.partial(unpack_kernel, peers, per_peer, chunks),
+        functools.partial(unpack_kernel, 2 * half, per_peer),
         out_shape=jax.ShapeDtypeStruct((targets, rows, width), BF16),
-        in_specs=[SMEM_SPEC] + [VMEM_SPEC] * (chunks * peers),
+        in_specs=[SMEM_SPEC] + [ANY_SPEC] * (half + 1),
         out_specs=VMEM_SPEC,
-        scratch_shapes=[pltpu.VMEM((peers * per_peer, rows, width), F32)],
+        scratch_shapes=[
+            pltpu.VMEM((half,) + near[0].shape, BF16),
+            pltpu.VMEM(over.shape, BF16),
+            pltpu.VMEM((2 * half * per_peer, rows, width), F32),
+            pltpu.SemaphoreType.DMA((half + 1,)),
+        ],
         compiler_params=pltpu.CompilerParams(vmem_limit_bytes=VMEM_BYTES),
         cost_estimate=cost(0, 3 << 20),
         name="unpack_query_grads",
-    )(table, *[b for part in blocks for b in part])
-
-
-def attend_kernel(peers, chunk, chunks, len_ref, k_ref, v_ref, *refs):
-    in_refs = refs[:peers]
+    )(table, *near, over)
+
+
+def attend_kernel(peers, chunk, chunks, waits, len_ref, k_ref, v_ref, *refs):
+    half = peers // 2
+    in_refs, before_refs = refs[:half], refs[half : half + chunk]
     groups = k_ref.shape[1] // (chunks * LANES)
-    kv_refs = refs[peers : peers + groups]
-    out_refs = refs[peers + groups : 2 * peers + groups]
-    q_s, g_s, o_s, kt_s, kg_s, vg_s = refs[2 * peers + groups :]
+    outs = refs[half + chunk + waits : -6]
+    kv_ref, out_refs = outs[0], outs[1:]
+    q_s, g_s, o_s, kt_s, kg_s, vg_s = refs[-6:]
     src_len = k_ref.shape[0]
-    per_peer, double, width = in_refs[0].shape
+    _, per_peer, double, width = in_refs[0].shape
     rows = double // 2
     block_rows = per_peer * rows
     total_rows = peers * block_rows
     tile = min(256, total_rows)
     scale = HEAD_DIM**-0.5
     for d in range(peers):
-        both = in_refs[d][...].astype(F32)
+        both = in_refs[d // 2][d % 2].astype(F32)
         at = slice(d * block_rows, (d + 1) * block_rows)
         q_s[at] = (both[:, :rows] * scale).reshape(block_rows, width).astype(BF16)
         g_s[at] = both[:, rows:].reshape(block_rows, width).astype(BF16)
@@ -185,26 +256,37 @@
             return 0
 
         lax.fori_loop(0, total_rows // tile, step, 0)
-        kv_refs[a][:, :LANES] = kg_s[...].astype(BF16)
-        kv_refs[a][:, LANES:] = vg_s[...].astype(BF16)
-    for d in range(peers):
-        out_refs[d][...] = o_s[d * block_rows : (d + 1) * block_rows]
-
-
-def attend(length, keys, values, blocks, chunk, chunks):
-    peers = len(blocks)
+        kv_ref[a, :, :LANES] = kg_s[...].astype(BF16)
+        kv_ref[a, :, LANES:] = vg_s[...].astype(BF16)
+    if chunk < chunks - 1:
+        out_refs[0][...] = o_s[...]
+        return
+    for d in range(half):
+        at = slice(2 * d * block_rows, 2 * (d + 1) * block_rows)
+        for c, part_ref in enumerate((*before_refs, o_s)):
+            for a in range(groups):
+                lane = (a * chunks + c) * LANES
+                out_refs[d][:, lane : lane + LANES] = part_ref[at, a * LANES : (a + 1) * LANES]
+
+
+def attend(length, keys, values, blocks, before, earlier):
+    chunk, chunks = len(before), CHUNKS
+    half = len(blocks)
+    peers = 2 * half
     src_len, width = keys.shape
-    per_peer, double, part = blocks[0].shape
+    _, per_peer, double, part = blocks[0].shape
     block_rows = per_peer * double // 2
     total_rows = peers * block_rows
     groups = part // LANES
     heads = part // HEAD_DIM
+    query_shapes = [jax.ShapeDtypeStruct((total_rows, part), BF16)]
+    if chunk == chunks - 1:
+        query_shapes = [jax.ShapeDtypeStruct((2 * block_rows, width), BF16)] * half
     outs = pl.pallas_call(
-        functools.partial(attend_kernel, peers, chunk, chunks),
-        out_shape=[jax.ShapeDtypeStruct((src_len, 2 * LANES), BF16)] * groups
-        + [jax.ShapeDtypeStruct((block_rows, part), BF16)] * peers,
-        in_specs=[SMEM_SPEC] + [VMEM_SPEC] * (2 + peers),
-        out_specs=[VMEM_SPEC] * (groups + peers),
+        functools.partial(attend_kernel, peers, chunk, chunks, len(earlier)),
+        out_shape=[jax.ShapeDtypeStruct((groups, src_len, 2 * LANES), BF16)] + query_shapes,
+        in_specs=[SMEM_SPEC] + [VMEM_SPEC] * (2 + half + chunk + len(earlier)),
+        out_specs=[VMEM_SPEC] * (1 + len(query_shapes)),
         scratch_shapes=[
             pltpu.VMEM((total_rows, part), BF16),
             pltpu.VMEM((total_rows, part), BF16),
@@ -213,76 +295,123 @@
             pltpu.VMEM((src_len, LANES), F32),
             pltpu.VMEM((src_len, LANES), F32),
         ],
-        compiler_params=pltpu.CompilerParams(vmem_limit_bytes=VMEM_BYTES),
+        compiler_params=pltpu.CompilerParams(vmem_limit_bytes=ATTEND_BYTES),
         cost_estimate=cost(
             40 * total_rows * src_len * HEAD_DIM * heads, 4 << 20, total_rows * src_len * heads
         ),
         name="attend",
-    )(length, keys, values, *blocks)
-    return outs[:groups], outs[groups:]
-
-
-def weight_kernel(place_ref, states_ref, *refs):
-    in_refs, own_ref, sib_ref = refs[:-2], refs[-2], refs[-1]
-    states = states_ref[...]
-    groups = 2
-    for e in range(len(in_refs) // groups):
-        for a in range(groups):
-            piece = lax.dot_general(
-                in_refs[e * groups + a][...], states, TN, preferred_element_type=F32
-            )
-            index = e * groups + a
-            away, seq = place_ref[2 * index], place_ref[2 * index + 1]
-
-            @pl.when(away == 0)
-            def _(piece=piece, seq=seq):
-                own_ref[seq] = piece
-
-            @pl.when(away != 0)
-            def _(piece=piece, seq=seq):
-                sib_ref[seq] = piece.astype(BF16)
-
-
-def weight_parts(place, states, blocks, seq_size):
+    )(length, keys, values, *blocks, *before, *earlier)
+    return outs[0], outs[1:]
+
+
+def weight_kernel(blocks, place_ref, states_ref, *refs):
+    own_ref, sib_ref, states_s, pairs_s, across_s, sems = refs[-6:]
+    targets = [states_s] + [pairs_s.at[e] for e in range(3)] + [across_s.at[a] for a in range(2)]
+    copies = fetch([states_ref] + list(refs[:blocks]), targets, sems)
+    copies[0].wait()
+    states = states_s[...]
+    for index in range(8):
+        e, a = index // 2, index % 2
+        if e < 3 and a == 0:
+            copies[1 + e].wait()
+        elif e == 3:
+            copies[4 + a].wait()
+        block = pairs_s[e, a] if e < 3 else across_s[a]
+        piece = lax.dot_general(block, states, TN, preferred_element_type=F32)
+        away, seq = place_ref[2 * index], place_ref[2 * index + 1]
+
+        @pl.when(away == 0)
+        def _(piece=piece, seq=seq):
+            own_ref[seq] = piece
+
+        @pl.when(away != 0)
+        def _(piece=piece, seq=seq):
+            sib_ref[seq] = piece.astype(BF16)
+
+
+def weight_parts(place, states, blocks, seq_size, earlier):
     src_len, width = states.shape
-    tall = blocks[0].shape[1]
+    tall = blocks[0].shape[2]
     shape = (seq_size, tall, width)
     return pl.pallas_call(
-        weight_kernel,
+        functools.partial(weight_kernel, len(blocks)),
         out_shape=[jax.ShapeDtypeStruct(shape, F32), jax.ShapeDtypeStruct(shape, BF16)],
-        in_specs=[SMEM_SPEC] + [VMEM_SPEC] * (1 + len(blocks)),
+        in_specs=[SMEM_SPEC] + [ANY_SPEC] * (1 + len(blocks) + len(earlier)),
         out_specs=[VMEM_SPEC] * 2,
+        scratch_shapes=[
+            pltpu.VMEM((src_len, width), BF16),
+            pltpu.VMEM((3, 2, src_len, tall), BF16),
+            pltpu.VMEM((2, src_len, tall), BF16),
+            pltpu.SemaphoreType.DMA((1 + len(blocks),)),
+        ],
         compiler_params=pltpu.CompilerParams(vmem_limit_bytes=VMEM_BYTES),
-        cost_estimate=cost(2 * len(blocks) * src_len * tall * width, 6 << 20),
+        cost_estimate=cost(16 * src_len * tall * width, 6 << 20),
         name="weight_parts",
-    )(place, states, *blocks)
+    )(place, states, *blocks, *earlier)
+
+
+def combine_kernel(chunks, seq_ref, *refs):
+    parts, outs = refs[: 2 * chunks], refs[2 * chunks :]
+    for d in range(len(outs)):
+        index = seq_ref[0] ^ d
+        for c in range(chunks):
+            total = parts[2 * c][index] + parts[2 * c + 1][index].astype(F32)
+            outs[d][c] = total.astype(outs[d].dtype)
+
+
+def combine(seq, parts):
+    pieces, tall, width = parts[0][0].shape
+    shape = (len(parts), tall, width)
+    return pl.pallas_call(
+        functools.partial(combine_kernel, len(parts)),
+        out_shape=[jax.ShapeDtypeStruct(shape, F32)]
+        + [jax.ShapeDtypeStruct(shape, BF16)] * (pieces - 1),
+        in_specs=[SMEM_SPEC] + [VMEM_SPEC] * (2 * len(parts)),
+        out_specs=[VMEM_SPEC] * pieces,
+        compiler_params=pltpu.CompilerParams(vmem_limit_bytes=VMEM_BYTES),
+        cost_estimate=cost(0, 6 << 20),
+        name="combine",
+    )(seq, *[x for part in parts for x in part])
 
 
 def state_kernel(chunks, order_ref, w_ref, *refs):
-    in_refs, out_ref, total_ref = refs[:-2], refs[-2], refs[-1]
+    in_refs, out_ref = refs[: 5 * chunks], refs[5 * chunks]
+    total_ref, w_s, pairs_s, across_s, sems = refs[5 * chunks + 1 :]
+    targets = []
+    for c in range(chunks):
+        targets += [pairs_s.at[c, e] for e in range(3)] + [across_s.at[c, a] for a in range(2)]
+    copies = fetch([w_ref] + list(in_refs), [w_s] + targets, sems)
+    for copy in copies:
+        copy.wait()
     total_ref[...] = jnp.zeros_like(total_ref)
-    per_chunk = len(in_refs) // chunks
     for c in range(chunks):
         at = slice(c * LANES, (c + 1) * LANES)
-        for index in range(per_chunk):
+        for index in range(8):
+            e, a = index // 2, index % 2
             piece = order_ref[index]
-            weight = jnp.concatenate([w_ref[piece, 0, at], w_ref[piece, 1, at]], axis=0)
-            total_ref[...] += jnp.dot(
-                in_refs[c * per_chunk + index][...], weight, preferred_element_type=F32
-            )
+            weight = jnp.concatenate([w_s[piece, 0, at], w_s[piece, 1, at]], axis=0)
+            block = pairs_s[c, e, a] if e < 3 else across_s[c, a]
+            total_ref[...] += jnp.dot(block, weight, preferred_element_type=F32)
     out_ref[...] = total_ref[...].astype(BF16)
 
 
 def state_grads(order, weights, blocks, chunks):
-    src_len, width = blocks[0].shape[0], weights.shape[-1]
+    src_len, tall = blocks[0].shape[1:]
+    width = weights.shape[-1]
     return pl.pallas_call(
         functools.partial(state_kernel, chunks),
         out_shape=jax.ShapeDtypeStruct((src_len, width), BF16),
-        in_specs=[SMEM_SPEC] + [VMEM_SPEC] * (1 + len(blocks)),
+        in_specs=[SMEM_SPEC] + [ANY_SPEC] * (1 + len(blocks)),
         out_specs=VMEM_SPEC,
-        scratch_shapes=[pltpu.VMEM((src_len, width), F32)],
-        compiler_params=pltpu.CompilerParams(vmem_limit_bytes=VMEM_BYTES),
-        cost_estimate=cost(2 * len(blocks) * src_len * 2 * LANES * width, 8 << 20),
+        scratch_shapes=[
+            pltpu.VMEM((src_len, width), F32),
+            pltpu.VMEM(weights.shape, BF16),
+            pltpu.VMEM((chunks, 3, 2, src_len, tall), BF16),
+            pltpu.VMEM((chunks, 2, src_len, tall), BF16),
+            pltpu.SemaphoreType.DMA((1 + len(blocks),)),
+        ],
+        compiler_params=pltpu.CompilerParams(vmem_limit_bytes=ATTEND_BYTES),
+        cost_estimate=cost(32 * src_len * 2 * LANES * width, 8 << 20),
         name="state_grads",
     )(order, weights, *blocks)
 
@@ -291,43 +420,35 @@
     return lax.ppermute(x, axes, [(i, i ^ distance) for i in range(size)])
 
 
-def exchange(blocks):
-    peers = len(blocks)
-    far_first = sorted(range(1, peers), key=lambda d: -(d % (peers // 2)))
-    got = {d: swap(blocks[d], PEERS, peers, d) for d in far_first}
-    return [blocks[0]] + [got[d] for d in range(1, peers)]
-
-
-def gather_mdl(pair):
-    near = [swap(b, "mdl", 4, 1) for b in pair]
-    over = [swap(b, "mdl", 4, 2) for b in pair]
-    across = [swap(near[0], "mdl", 4, 2), swap(over[1], "mdl", 4, 1)]
-    return list(pair) + near + over + across
-
-
-def scatter_line(own, sib, seq_size):
-    place = lax.axis_index("seq")
+def ring(x):
+    size = lax.axis_size("seq")
+    return lax.ppermute(x, "seq", [(z, (z + 1) % size) for z in range(size)])
+
+
+def exchange(blocks, sib, earlier):
+    half = len(blocks)
     got = swap(sib, "grp", 2, 1)
-
-    def piece(index):
-        index = jnp.clip(index, 0, seq_size - 1)
-        mine = lax.dynamic_index_in_dim(own, index, 0, keepdims=False)
-        other = lax.dynamic_index_in_dim(got, index, 0, keepdims=False)
-        return mine + other.astype(F32)
-
-    right = left = None
-    last = seq_size - 1
-    for t in range(last):
-        send_right, send_left = piece(last - t + place), piece(t + place - last)
-        if t > 0:
-            send_right, send_left = send_right + right.astype(F32), send_left + left.astype(F32)
-        right = lax.ppermute(
-            send_right.astype(BF16), "seq", [(z, z + 1) for z in range(t + 1)]
-        )
-        left = lax.ppermute(
-            send_left.astype(BF16), "seq", [(last - z, last - z - 1) for z in range(t + 1)]
-        )
-    return piece(place) + right.astype(F32) + left.astype(F32)
+    pairs = merge(blocks, got, earlier)
+    line = {d: swap(pairs[d], "seq", half, d) for d in range(half - 1, 0, -1)}
+    return [pairs[0]] + [line[d] for d in range(1, half)], pairs[1:]
+
+
+def send_back(pairs):
+    half, rows = len(pairs), pairs[0].shape[0] // 2
+    line = {d: swap(pairs[d], "seq", half, d) for d in range(half - 1, 0, -1)}
+    near = [pairs[0]] + [line[d] for d in range(1, half)]
+    return near, swap(jnp.stack([pair[rows:] for pair in near]), "grp", 2, 1)
+
+
+def gather_near(pair):
+    return [pair, swap(pair, "mdl", 4, 1), swap(pair, "mdl", 4, 2)]
+
+
+def gather_across(pair, near, over, earlier=()):
+    first, second = near[0], over[1]
+    if earlier:
+        first, second = hold([first, second], earlier)
+    return [pair, near, over, swap(first, "mdl", 4, 2), swap(second, "mdl", 4, 1)]
 
 
 def block_grads(query_block, grad_block, key_local, value_local, key_valid):
@@ -445,37 +566,64 @@
     targets, rows, width = queries.shape
     per_peer = max(2, 2 * targets // peers)
     src_len = src_keys.shape[1]
-    chunks = 2
+    chunks = CHUNKS
     groups = width // (chunks * LANES)
     me = lax.axis_index(PEERS).astype(jnp.int32)
     mdl = lax.axis_index("mdl").astype(jnp.int32)
     grp = lax.axis_index("grp").astype(jnp.int32)
-    table, sends = pack(me[None], owners, queries, out_grads, peers, per_peer, chunks)
     keys, values = src_keys[0], src_values[0]
     flat_states = states[0]
-    tall = jnp.transpose(kv_weight, (1, 0, 2))
-
     source = mdl ^ (jnp.arange(4 * groups, dtype=jnp.int32) // groups)
     order = source * groups + jnp.arange(4 * groups, dtype=jnp.int32) % groups
+    seq = lax.axis_index("seq").astype(jnp.int32)
+    distance = (seq - jnp.arange(seq_size, dtype=jnp.int32)) % seq_size
     place = jnp.stack([(order // seq_size) ^ grp, order % seq_size], axis=1).reshape(-1)
 
-    got = [exchange(sends[c]) for c in range(chunks)]
-    gathered, back, sums = [], [], []
+    lines = [kv_weight, ring(kv_weight)]
+    got, earlier = [], lines[1:]
     for c in range(chunks):
-        pair, query_blocks = attend(src_lengths, keys, values, got[c], c, chunks)
-        back.append(query_blocks)
-        gathered.append(gather_mdl(pair))
-    tall, _ = lax.optimization_barrier((tall, got[1][1]))
-    weights = lax.all_gather(tall, PEERS, axis=0)
+        table, blocks, sib = pack(
+            me[None], owners, queries, out_grads, peers, per_peer, c, chunks
+        )
+        arrived, sent = exchange(blocks, sib, earlier)
+        got.append(arrived)
+        earlier = arrived[1:]
+    gathered, before = [], []
     for c in range(chunks):
-        own, sib = weight_parts(place, flat_states, gathered[c], seq_size)
-        sums.append(scatter_line(own, sib, seq_size))
-    returned = [exchange(b) for b in back]
-    state_out = state_grads(order, weights, [b for part in gathered for b in part], chunks)
-    query_out = unpack(table, returned, targets, rows, width, peers, per_peer)
-    weight_out = jnp.concatenate(
-        [s.reshape(2, LANES, width).transpose(1, 0, 2) for s in sums], axis=0
-    )
+        last = c == chunks - 1
+        pair, query_blocks = attend(
+            src_lengths, keys, values, got[c], before, [pair] if last else sent
+        )
+        if last:
+            pair = hold([pair], gathered[0][1:] + lines[2:])[0]
+        else:
+            pair, held = hold([pair, lines[1]], got[c + 1][1:])
+            lines.append(ring(held))
+        before = before + list(query_blocks[:1])
+        gathered.append(gather_near(pair))
+    lines.append(ring(hold(lines[2:], [pair])[0]))
+    gathered = [gather_across(*part, [pair] if c == 0 else []) for c, part in enumerate(gathered)]
+    query_blocks = [query_blocks[0], *hold(query_blocks[1:], gathered[0][3:])]
+    near, over = send_back(query_blocks)
+    sums = []
+    for c in range(chunks):
+        own, sib = weight_parts(
+            place, flat_states, gathered[c], seq_size, near[1:] + sends if c else [pair]
+        )
+        keep, *sends = combine(seq[None], [(own, swap(sib, "grp", 2, 1))])
+        line = [swap(x, "seq", seq_size, d + 1) for d, x in enumerate(sends)]
+        sums.append(keep + sum(x.astype(F32) for x in line))
+    lines = lines + [swap(x, "grp", 2, 1) for x in lines]
+    weights = jnp.stack(lines).transpose(0, 2, 1, 3)
+    own_pieces, other_pieces = grp * seq_size + distance, (1 - grp) * seq_size + distance
+    piece_at = jnp.zeros((peers,), jnp.int32)
+    piece_at = piece_at.at[own_pieces].set(jnp.arange(seq_size, dtype=jnp.int32))
+    piece_at = piece_at.at[other_pieces].set(seq_size + jnp.arange(seq_size, dtype=jnp.int32))
+    state_out = state_grads(piece_at[order], weights, [b for part in gathered for b in part], chunks)
+    query_out = unpack(table, near, over, targets, rows, per_peer)
+    weight_sum = jnp.concatenate(sums, axis=0)
+    weight_out = weight_sum.reshape(chunks, 2, LANES, width).transpose(0, 2, 1, 3)
+    weight_out = weight_out.reshape(chunks * LANES, 2, width)
     return (query_out, state_out.reshape(1, src_len, width), weight_out)
 
 

time: 281 us -> 198 us (0.70)
  starting transfers between devices: 126 us -> 60.8 us
  waiting for transfers between devices: 30 us -> 71.7 us
  local copies, waits for them, and re-layouts: 38.8 us -> 17.1 us
  other arithmetic: 20.7 us -> 0.55 us
  between operations: 15.1 us -> 1.78 us
    ppermute x42 -> x32, starting transfers between devices: 100 us -> 50.5 us  [swap(): return lax.ppermute(x, axes, [(i, i ^ distance) for i in range(size)])]
    ppermute x42 -> x32, waiting for transfers between devices: 29.1 us -> 59.1 us  [swap(): return lax.ppermute(x, axes, [(i, i ^ distance) for i in range(size)])]
    unnamed x119 -> x30, local copies, waits for them, and re-layouts: 37.9 us -> 10.9 us
    convert_element_type x8 -> x0, other arithmetic: 16.4 us -> none  [the longest x6 12.6 us: scatter_line(): send_right.astype(BF16)]
    ppermute x12 -> x3, starting transfers between devices: 26 us -> 10.3 us  [ring(): return lax.ppermute(x, 'seq', [(z, (z + 1) % size) for z in range(size)])]
    ppermute x12 -> x3, waiting for transfers between devices: 0.92 us -> 12.6 us  [ring(): return lax.ppermute(x, 'seq', [(z, (z + 1) % size) for z in range(size)])]
    pallas_call x6 -> x16, Pallas kernels: 43.8 us -> 41.4 us  [the longest x2 25.9 us: attend(): pl.pallas_call(functools.partial(attend_kernel, peers, chunk, chunks, len...]
  transfers between devices with their start and end apart: 55 -> 35, of which waited for: 11 -> 14; matrix products, arithmetic and copies ran while one was open for 8% -> 4% of each run, Pallas kernels for 14% -> 23%
where the time goes in v2:
time: 198 us
  waiting for transfers between devices  71.7 us (36%)
  starting transfers between devices  60.8 us (31%)
  Pallas kernels  45.7 us (23%)
  local copies, waits for them, and re-layouts  17.1 us (9%)
    ppermute x32, waiting for transfers between devices, swap(): return lax.ppermute(x, axes, [(i, i ^ distance) for i in range(size)])  59.1 us
    ppermute x32, starting transfers between devices, swap(): return lax.ppermute(x, axes, [(i, i ^ distance) for i in range(size)])  50.5 us
    pallas_call x2, Pallas kernels, attend(): pl.pallas_call(functools.partial(attend_kernel, peers, chunk, chunks, len...  25.9 us
    ppermute x3, waiting for transfers between devices, ring(): return lax.ppermute(x, 'seq', [(z, (z + 1) % size) for z in range(size)])  12.6 us
    unnamed x30, local copies, waits for them, and re-layouts  10.9 us
    ppermute x3, starting transfers between devices, ring(): return lax.ppermute(x, 'seq', [(z, (z + 1) % size) for z in range(size)])  10.3 us
    pallas_call x2, Pallas kernels, weight_parts(): pl.pallas_call(functools.partial(weight_kernel, len(blocks)), out_shape=[...  7.25 us
    pallas_call x1, Pallas kernels, state_grads(): pl.pallas_call(functools.partial(state_kernel, chunks), out_shape=jax.Sha...  4.34 us
  transfers between devices with their start and end apart: 35, of which 14 were waited for; matrix products, arithmetic and copies ran while one was open for 4% of the time, Pallas kernels for 23%

profile of v2, /device:TPU:0, one launch (start us, length us, event | category | flops | bytes accessed | tf_op | source)
XLA Modules:
  0.0 197.6 jit_solution(7381710818367941153)
XLA Ops:
  0.7 2.0 copy.31
  2.6 3.0 %collective-permute-start.2 = (bf16[256,2,512]{2,0,1:T(8,128)(2,1)}, bf16[256,2,512]{2,0,1:T(8,128)(2,1)}, u32[]{:S(2)}, u32[]{:S(2)}) collective-permute-start(bf16[256,2,512]{2,0,1:T(8,128)(2,1)} %copy.31), channel_id=1, source_target_pairs={{0,4},{4,8},{8,12},{12,0},{1,5},{5,9},{9,13},{13,1},{2,6},{6,10},{... | collective-permute-start | bytes 1572872 | tf_op jit(solution)/shard_map/ppermute | solution.py:425
  5.7 1.0 copy-done.1
  6.7 1.0 copy-done.2
  7.7 0.7 copy-done.4
  8.4 2.0 %pack_targets.3 = (s32[128]{0:T(128)}, bf16[16,16,256]{2,1,0:T(8,128)(2,1)S(1)}, bf16[16,16,256]{2,1,0:T(8,128)(2,1)S(1)}, bf16[16,16,256]{2,1,0:T(8,128)(2,1)S(...) custom-call(s32[1]{0:T(128)} %bitcast.me_ref, s32[64]{0:T(128)S(1)} %copy-done.4, ...), custom_call_target="tpu_custom_call" | custom-call | bytes 3145728 | tf_op jit(solution)/shard_map/pack_targets/pallas_call | solution.py:95
  10.5 0.5 collective-permute-start.19
  11.0 2.0 %pack_targets.2 = (s32[128]{0:T(128)S(1)}, bf16[16,16,256]{2,1,0:T(8,128)(2,1)S(1)}, bf16[16,16,256]{2,1,0:T(8,128)(2,1)S(1)}, bf16[16,16,256]{2,1,0:T(8,128)(2,...) custom-call(s32[1]{0:T(128)} %bitcast.me_ref, s32[64]{0:T(128)S(1)} %copy-done.4, ...), custom_call_target="tpu_custom_call" | custom-call | bytes 3145728 | tf_op jit(solution)/shard_map/pack_targets/pallas_call | solution.py:95
  13.2 6.7 %collective-permute-done.2 = bf16[256,2,512]{2,0,1:T(8,128)(2,1)} collective-permute-done((bf16[256,2,512]{2,0,1:T(8,128)(2,1)}, bf16[256,2,512]{2,0,1:T(8,128)(2,1)}, u32[]{:S(2)}, u32[]{:S(2)}) %collective-permute-start.2) | collective-permute-done | bytes 524320 | tf_op jit(solution)/shard_map/ppermute | solution.py:425
  19.9 1.6 copy.32.refs_5_.refs_1_
  21.7 2.3 %collective-permute-start.4 = (bf16[2,16,16,256]{3,2,1,0:T(8,128)(2,1)S(1)}, bf16[2,16,16,256]{3,2,1,0:T(8,128)(2,1)S(1)}, u32[]{:S(2)}, u32[]{:S(2)}) collective-permute-start(bf16[2,16,16,256]{3,2,1,0:T(8,128)(2,1)S(1)} %get-tuple-element.60), channel_id=1, source_target_pairs={{0,8},{4,12},{8,0},{12,4},{1,9},{5,13},{9,1},{13,5},{2,10},{6,14},... | collective-permute-start | bytes 786440 | tf_op jit(solution)/shard_map/ppermute | solution.py:420
  24.0 2.1 %collective-permute-start.5 = (bf16[2,16,16,256]{3,2,1,0:T(8,128)(2,1)S(1)}, bf16[2,16,16,256]{3,2,1,0:T(8,128)(2,1)S(1)}, u32[]{:S(2)}, u32[]{:S(2)}) collective-permute-start(bf16[2,16,16,256]{3,2,1,0:T(8,128)(2,1)S(1)} %get-tuple-element.61), channel_id=1, source_target_pairs={{0,12},{4,8},{8,4},{12,0},{1,13},{5,9},{9,5},{13,1},{2,14},{6,10},... | collective-permute-start | bytes 786440 | tf_op jit(solution)/shard_map/ppermute | solution.py:420
  26.7 1.9 bitcast_dynamic-update-slice_fusion.7
  28.6 5.5 %collective-permute-done.3.refs_5_.refs_1_ = bf16[2,16,16,256]{3,2,1,0:T(8,128)(2,1)S(1)} collective-permute-done((bf16[2,16,16,256]{3,2,1,0:T(8,128)(2,1)S(1)}, bf16[2,16,16,256]{3,2,1,0:T(8,128)(2,1)S(1)}, u32[]{:S(2)}, u32[]{:S(2)}) %collective-permute-start.3) | collective-permute-done | bytes 262176 | tf_op jit(solution)/shard_map/ppermute | solution.py:420
  34.1 9.0 %collective-permute-done.4.refs_6_.refs_2_ = bf16[2,16,16,256]{3,2,1,0:T(8,128)(2,1)S(1)} collective-permute-done((bf16[2,16,16,256]{3,2,1,0:T(8,128)(2,1)S(1)}, bf16[2,16,16,256]{3,2,1,0:T(8,128)(2,1)S(1)}, u32[]{:S(2)}, u32[]{:S(2)}) %collective-permute-start.4) | collective-permute-done | bytes 262176 | tf_op jit(solution)/shard_map/ppermute | solution.py:420
  43.2 4.5 %collective-permute-start.6 = (bf16[2,16,16,256]{3,2,1,0:T(8,128)(2,1)S(1)}, bf16[2,16,16,256]{3,2,1,0:T(8,128)(2,1)S(1)}, u32[]{:S(2)}, u32[]{:S(2)}) collective-permute-start(bf16[2,16,16,256]{3,2,1,0:T(8,128)(2,1)S(1)} %get-tuple-element.63.refs_4_), channel_id=1, source_target_pairs={{0,4},{4,0},{8,12},{12,8},{1,5},{5,1},{9,13},{13,9},{2,6},{6,2},{1... | collective-permute-start | bytes 786440 | tf_op jit(solution)/shard_map/ppermute | solution.py:420
  47.9 2.3 %collective-permute-start.8 = (bf16[2,16,16,256]{3,2,1,0:T(8,128)(2,1)S(1)}, bf16[2,16,16,256]{3,2,1,0:T(8,128)(2,1)S(1)}, u32[]{:S(2)}, u32[]{:S(2)}) collective-permute-start(bf16[2,16,16,256]{3,2,1,0:T(8,128)(2,1)S(1)} %get-tuple-element.65.refs_6_), channel_id=1, source_target_pairs={{0,12},{4,8},{8,4},{12,0},{1,13},{5,9},{9,5},{13,1},{2,14},{6,10},... | collective-permute-start | bytes 786440 | tf_op jit(solution)/shard_map/ppermute | solution.py:420
  50.2 12.9 %attend.2 = (bf16[2,512,256]{2,1,0:T(8,128)(2,1)S(1)}, bf16[1024,256]{1,0:T(8,128)(2,1)S(1)}) custom-call(s32[1]{0:T(128)S(6)} %copy.51.len_ref, bf16[512,512]{1,0:T(8,128)(2,1)S(1)} %bitcast.52, bf16[512,512]{1,0:T(8,128)(2,1)S(1)} %bitcast.54, bf16[2,16,16,256]{3,2,1,0:T(8,128)(2,1)S(1)} %get-tuple-element.66.refs_0_, ...), custom_call_target="tpu_custom_call" | custom-call | flops 5368709120 | bytes 4194304 | tf_op jit(solution)/shard_map/attend/pallas_call | solution.py:285
  63.1 4.9 %collective-permute-done.7.refs_3_.refs_2_ = bf16[2,16,16,256]{3,2,1,0:T(8,128)(2,1)S(1)} collective-permute-done((bf16[2,16,16,256]{3,2,1,0:T(8,128)(2,1)S(1)}, bf16[2,16,16,256]{3,2,1,0:T(8,128)(2,1)S(1)}, u32[]{:S(2)}, u32[]{:S(2)}) %collective-permute-start.7) | collective-permute-done | bytes 262176 | tf_op jit(solution)/shard_map/ppermute | solution.py:420
  68.1 1.4 collective-permute-start.9
  69.7 0.6 scatter_custom_fusion
  70.3 0.6 scatter_fusion
  70.9 0.6 gather_fusion
  71.5 1.6 collective-permute-start.10
  73.2 7.2 %collective-permute-start.11 = (bf16[256,2,512]{2,0,1:T(8,128)(2,1)S(1)}, bf16[256,2,512]{2,0,1:T(8,128)(2,1)S(1)}, u32[]{:S(2)}, u32[]{:S(2)}) collective-permute-start(bf16[256,2,512]{2,0,1:T(8,128)(2,1)S(1)} %copy.34), channel_id=1, source_target_pairs={{0,4},{4,8},{8,12},{12,0},{1,5},{5,9},{9,13},{13,1},{2,6},{6,10},{... | collective-permute-start | bytes 1572872 | tf_op jit(solution)/shard_map/ppermute | solution.py:425
  80.4 0.9 copy-done.8
  81.4 1.0 copy-done.10
  82.4 13.0 %attend.3 = (bf16[2,512,256]{2,1,0:T(8,128)(2,1)S(1)}, bf16[256,512]{1,0:T(8,128)(2,1)S(1)}, bf16[256,512]{1,0:T(8,128)(2,1)S(1)}, bf16[256,512]{1,0:T(8,128)(2,1)S(1)}, bf16[256,512]{1,0:T(8,128)(2,1)S(1)}) custom-call(s32[1]{0:T(128)S(6)} %copy.51.len_ref, bf16[512,512]{1,0:T(8,128)(2,1)S(1)} %bitcast.53, bf16[512,512]{1,0:T(8,128)(2,1)S(1)} %bitcast.55, ...), custom_call_target="tpu_custom_call" | custom-call | flops 5368709120 | bytes 4194304 | tf_op jit(solution)/shard_map/attend/pallas_call | solution.py:285
  95.5 0.5 copy.35.refs_3_.refs_0_
  96.2 2.1 %collective-permute-start.12 = (bf16[512,256]{1,0:T(8,128)(2,1)S(1)}, bf16[512,256]{1,0:T(8,128)(2,1)S(1)}, u32[]{:S(2)}, u32[]{:S(2)}) collective-permute-start(bf16[512,256]{1,0:T(8,128)(2,1)S(1)} %get-tuple-element.76), channel_id=1, source_target_pairs={{0,2},{1,3},{2,0},{3,1},{4,6},{5,7},{6,4},{7,5},{8,10},{9,11},{10,... | collective-permute-start | bytes 786440 | tf_op jit(solution)/shard_map/ppermute | solution.py:420
  98.2 2.0 %collective-permute-start.13 = (bf16[512,256]{1,0:T(8,128)(2,1)S(1)}, bf16[512,256]{1,0:T(8,128)(2,1)S(1)}, u32[]{:S(2)}, u32[]{:S(2)}) collective-permute-start(bf16[512,256]{1,0:T(8,128)(2,1)S(1)} %get-tuple-element.77), channel_id=1, source_target_pairs={{0,1},{1,0},{2,3},{3,2},{4,5},{5,4},{6,7},{7,6},{8,9},{9,8},{10,11... | collective-permute-start | bytes 786440 | tf_op jit(solution)/shard_map/ppermute | solution.py:420
  100.3 1.1 bitcast_dynamic-update-slice_fusion.6
  101.5 1.4 collective-permute-start.24
  102.9 1.3 collective-permute-done.12.refs_3_
  104.2 0.5 collective-permute-done.13.refs_4_
  104.8 1.5 collective-permute-start.15
  106.3 3.7 %weight_parts.2 = (f32[4,256,512]{2,1,0:T(8,128)S(1)}, bf16[4,256,512]{2,1,0:T(8,128)(2,1)S(1)}) custom-call(s32[16]{0:T(128)S(1)} %reshape.220.place_ref, bf16[512,512]{1,0:T(8,128)(2,1)S(1)} %bitcast.50, bf16[2,512,256]{2,1,0:T(8,128)(2,1)S(1)} %get-tuple-element.69.refs_5_.refs_0_, bf16[2,512,256]{2,1,0:T(8,128)(2,1)S(1)} %collective-permute-done.9.refs_1_, ...), custom_call_target="tpu_custom_call" | custom-call | flops 1073741824 | bytes 6291456 | tf_op jit(solution)/shard_map/weight_parts/pallas_call | solution.py:336
  110.0 4.7 %collective-permute-done.16.refs_3_.refs_7_ = bf16[256,512]{1,0:T(8,128)(2,1)S(1)} collective-permute-done((bf16[256,512]{1,0:T(8,128)(2,1)S(1)}, bf16[256,512]{1,0:T(8,128)(2,1)S(1)}, u32[]{:S(2)}, u32[]{:S(2)}) %collective-permute-start.16) | collective-permute-done | bytes 262176 | tf_op jit(solution)/shard_map/ppermute | solution.py:420
  114.8 9.2 %collective-permute-start.14 = (bf16[256,512]{1,0:T(8,128)(2,1)S(1)}, bf16[256,512]{1,0:T(8,128)(2,1)S(1)}, u32[]{:S(2)}, u32[]{:S(2)}) collective-permute-start(bf16[256,512]{1,0:T(8,128)(2,1)S(1)} %get-tuple-element.78), channel_id=1, source_target_pairs={{0,4},{4,0},{8,12},{12,8},{1,5},{5,1},{9,13},{13,9},{2,6},{6,2},{1... | collective-permute-start | bytes 786440 | tf_op jit(solution)/shard_map/ppermute | solution.py:420
  124.0 2.3 %collective-permute-done.15.refs_2_.refs_6_ = bf16[256,512]{1,0:T(8,128)(2,1)S(1)} collective-permute-done((bf16[256,512]{1,0:T(8,128)(2,1)S(1)}, bf16[256,512]{1,0:T(8,128)(2,1)S(1)}, u32[]{:S(2)}, u32[]{:S(2)}) %collective-permute-start.15) | collective-permute-done | bytes 262176 | tf_op jit(solution)/shard_map/ppermute | solution.py:420
  126.3 2.7 %collective-permute-done.14.refs_1_.refs_5_ = bf16[256,512]{1,0:T(8,128)(2,1)S(1)} collective-permute-done((bf16[256,512]{1,0:T(8,128)(2,1)S(1)}, bf16[256,512]{1,0:T(8,128)(2,1)S(1)}, u32[]{:S(2)}, u32[]{:S(2)}) %collective-permute-start.14) | collective-permute-done | bytes 262176 | tf_op jit(solution)/shard_map/ppermute | solution.py:420
  129.1 1.6 collective-permute-start.25
  130.7 0.6 collective-permute-start.26
  131.4 5.9 %collective-permute-done.18 = bf16[256,2,512]{2,0,1:T(8,128)(2,1)S(1)} collective-permute-done((bf16[256,2,512]{2,0,1:T(8,128)(2,1)S(1)}, bf16[256,2,512]{2,0,1:T(8,128)(2,1)S(1)}, u32[]{:S(2)}, u32[]{:S(2)}) %collective-permute-start.18) | collective-permute-done | bytes 524320 | tf_op jit(solution)/shard_map/ppermute | solution.py:425
  137.3 0.6 collective-permute-start.21
  137.9 0.2 combine.2
  138.2 1.0 collective-permute-done.26.refs_9_.refs_4_
  139.2 3.5 %weight_parts.3 = (f32[4,256,512]{2,1,0:T(8,128)S(1)}, bf16[4,256,512]{2,1,0:T(8,128)(2,1)S(1)}) custom-call(s32[16]{0:T(128)S(1)} %reshape.220.place_ref, bf16[512,512]{1,0:T(8,128)(2,1)S(1)} %bitcast.51, bf16[2,512,256]{2,1,0:T(8,128)(2,1)S(1)} %hold.6.refs_2_.refs_1_.refs_5_.refs_0_, bf16[2,512,256]{2,1,0:T(8,128)(2,1)S(1)} %collective-permute-done.23.refs_6_.refs_1_, ...), custom_call_target="tpu_custom_call" | custom-call | flops 1073741824 | bytes 6291456 | tf_op jit(solution)/shard_map/weight_parts/pallas_call | solution.py:336
  142.8 0.6 collective-permute-start.31
  143.3 1.1 bitcast_dynamic-update-slice_fusion.3
  144.5 3.4 %unpack_query_grads.1 = bf16[64,8,512]{2,1,0:T(8,128)(2,1)} custom-call(s32[128]{0:T(128)S(1)} %get-tuple-element.48.table_ref, bf16[256,512]{1,0:T(8,128)(2,1)S(1)} %get-tuple-element.70.refs_0_, bf16[256,512]{1,0:T(8,128)(2,1)S(1)} %collective-permute-done.14.refs_1_.refs_5_, bf16[256,512]{1,0:T(8,128)(2,1)S(1)} %collective-permute-done.15.refs_2_.refs_6_, ...), custom_call_target="tpu_custom_call" | custom-call | bytes 3145728 | tf_op jit(solution)/shard_map/unpack_query_grads/pallas_call | solution.py:185
  148.0 1.3 collective-permute-start.30
  149.3 0.6 collective-permute-start.29
  149.9 2.6 %collective-permute-start.28 = (bf16[1,256,512]{2,1,0:T(8,128)(2,1)S(1)}, bf16[1,256,512]{2,1,0:T(8,128)(2,1)S(1)}, u32[]{:S(2)}, u32[]{:S(2)}) collective-permute-start(bf16[1,256,512]{2,1,0:T(8,128)(2,1)S(1)} %get-tuple-element.84.refs_8_), channel_id=1, source_target_pairs={{0,4},{4,0},{8,12},{12,8},{1,5},{5,1},{9,13},{13,9},{2,6},{6,2},{1... | collective-permute-start | bytes 786440 | tf_op jit(solution)/shard_map/ppermute | solution.py:420
  152.5 4.3 %state_grads.1 = bf16[512,512]{1,0:T(8,128)(2,1)} custom-call(s32[8]{0:T(128)S(1)} %gather_fusion, bf16[8,2,256,512]{3,2,1,0:T(8,128)(2,1)S(1)} %bitcast.49, bf16[2,512,256]{2,1,0:T(8,128)(2,1)S(1)} %get-tuple-element.69.refs_5_.refs_0_, bf16[2,512,256]{2,1,0:T(8,128)(2,1)S(1)} %collective-permute-done.9.refs_1_, ...), custom_call_target="tpu_custom_call" | custom-call | flops 2147483648 | bytes 8388608 | tf_op jit(solution)/shard_map/state_grads/pallas_call | solution.py:401
  156.8 0.2 combine.3
  157.0 1.3 collective-permute-start.34
  158.3 0.3 collective-permute-start.33
  158.6 0.6 collective-permute-done.30
  159.2 9.6 %collective-permute-start.32 = (bf16[1,256,512]{2,1,0:T(8,128)(2,1)S(1)}, bf16[1,256,512]{2,1,0:T(8,128)(2,1)S(1)}, u32[]{:S(2)}, u32[]{:S(2)}) collective-permute-start(bf16[1,256,512]{2,1,0:T(8,128)(2,1)S(1)} %get-tuple-element.90), channel_id=1, source_target_pairs={{0,4},{4,0},{8,12},{12,8},{1,5},{5,1},{9,13},{13,9},{2,6},{6,2},{1... | collective-permute-start | bytes 786440 | tf_op jit(solution)/shard_map/ppermute | solution.py:420
  168.8 16.3 %collective-permute-done.29 = bf16[1,256,512]{2,1,0:T(8,128)(2,1)S(1)} collective-permute-done((bf16[1,256,512]{2,1,0:T(8,128)(2,1)S(1)}, bf16[1,256,512]{2,1,0:T(8,128)(2,1)S(1)}, u32[]{:S(2)}, u32[]{:S(2)}) %collective-permute-start.29) | collective-permute-done | bytes 262176 | tf_op jit(solution)/shard_map/ppermute | solution.py:420
  185.1 0.2 add_add_fusion.1
  185.3 10.3 %collective-permute-done.33 = bf16[1,256,512]{2,1,0:T(8,128)(2,1)S(1)} collective-permute-done((bf16[1,256,512]{2,1,0:T(8,128)(2,1)S(1)}, bf16[1,256,512]{2,1,0:T(8,128)(2,1)S(1)}, u32[]{:S(2)}, u32[]{:S(2)}) %collective-permute-start.33) | collective-permute-done | bytes 262176 | tf_op jit(solution)/shard_map/ppermute | solution.py:420
  195.8 1.8 copy.41
  (83 shorter events, 2.1 us)
Async XLA Ops:
  0.6 49.5 %copy-start.5 = (bf16[1,512,512]{2,1,0:T(8,128)(2,1)S(1)}, bf16[1,512,512]{2,1,0:T(8,128)(2,1)}, u32[]{:S(2)}) copy-start(bf16[1,512,512]{2,1,0:T(8,128)(2,1)} %param.11) | copy-start | bytes 1572868
  0.6 49.5 %copy-start.6 = (bf16[1,512,512]{2,1,0:T(8,128)(2,1)S(1)}, bf16[1,512,512]{2,1,0:T(8,128)(2,1)}, u32[]{:S(2)}) copy-start(bf16[1,512,512]{2,1,0:T(8,128)(2,1)} %param.12) | copy-start | bytes 1572868
  2.6 17.3 %collective-permute-start.2 = (bf16[256,2,512]{2,0,1:T(8,128)(2,1)}, bf16[256,2,512]{2,0,1:T(8,128)(2,1)}, u32[]{:S(2)}, u32[]{:S(2)}) collective-permute-start(bf16[256,2,512]{2,0,1:T(8,128)(2,1)} %copy.31), channel_id=1, source_target_pairs={{0,4},{4,8},{8,12},{12,0},{1,5},{5,9},{9,13},{13,1},{2,6},{6,10},{... | collective-permute-start | bytes 1572872 | tf_op jit(solution)/shard_map/ppermute | solution.py:425
  5.6 1.0 copy-start.1
  6.7 1.0 copy-start.2
  7.7 0.7 copy-start.4
  10.4 11.1 %collective-permute-start.1 = (bf16[4,16,16,256]{3,2,1,0:T(8,128)(2,1)}, bf16[4,16,16,256]{3,2,1,0:T(8,128)(2,1)S(1)}, u32[]{:S(2)}, u32[]{:S(2)}) collective-permute-start(bf16[4,16,16,256]{3,2,1,0:T(8,128)(2,1)} %get-tuple-element.58), channel_id=1, source_target_pairs={{0,16},{16,0},{1,17},{17,1},{2,18},{18,2},{3,19},{19,3},{4,20},{20... | collective-permute-start | bytes 1572872 | tf_op jit(solution)/shard_map/ppermute | solution.py:420
  10.5 132.3 %collective-permute-start.19 = (bf16[256,2,512]{2,0,1:T(8,128)(2,1)}, bf16[256,2,512]{2,0,1:T(8,128)(2,1)}, u32[]{:S(2)}, u32[]{:S(2)}) collective-permute-start(bf16[256,2,512]{2,0,1:T(8,128)(2,1)} %copy.31), channel_id=1, source_target_pairs={{0,16},{16,0},{1,17},{17,1},{2,18},{18,2},{3,19},{19,3},{4,20},{20... | collective-permute-start | bytes 1572872 | tf_op jit(solution)/shard_map/ppermute | solution.py:420
  13.0 15.6 %collective-permute-start = (bf16[4,16,16,256]{3,2,1,0:T(8,128)(2,1)}, bf16[4,16,16,256]{3,2,1,0:T(8,128)(2,1)S(1)}, u32[]{:S(2)}, u32[]{:S(2)}) collective-permute-start(bf16[4,16,16,256]{3,2,1,0:T(8,128)(2,1)} %get-tuple-element.53), channel_id=1, source_target_pairs={{0,16},{16,0},{1,17},{17,1},{2,18},{18,2},{3,19},{19,3},{4,20},{20... | collective-permute-start | bytes 1572872 | tf_op jit(solution)/shard_map/ppermute | solution.py:420
  21.6 12.5 %collective-permute-start.3 = (bf16[2,16,16,256]{3,2,1,0:T(8,128)(2,1)S(1)}, bf16[2,16,16,256]{3,2,1,0:T(8,128)(2,1)S(1)}, u32[]{:S(2)}, u32[]{:S(2)}) collective-permute-start(bf16[2,16,16,256]{3,2,1,0:T(8,128)(2,1)S(1)} %get-tuple-element.59), channel_id=1, source_target_pairs={{0,4},{4,0},{8,12},{12,8},{1,5},{5,1},{9,13},{13,9},{2,6},{6,2},{1... | collective-permute-start | bytes 786440 | tf_op jit(solution)/shard_map/ppermute | solution.py:420
  21.7 21.4 %collective-permute-start.4 = (bf16[2,16,16,256]{3,2,1,0:T(8,128)(2,1)S(1)}, bf16[2,16,16,256]{3,2,1,0:T(8,128)(2,1)S(1)}, u32[]{:S(2)}, u32[]{:S(2)}) collective-permute-start(bf16[2,16,16,256]{3,2,1,0:T(8,128)(2,1)S(1)} %get-tuple-element.60), channel_id=1, source_target_pairs={{0,8},{4,12},{8,0},{12,4},{1,9},{5,13},{9,1},{13,5},{2,10},{6,14},... | collective-permute-start | bytes 786440 | tf_op jit(solution)/shard_map/ppermute | solution.py:420
  24.0 19.2 %collective-permute-start.5 = (bf16[2,16,16,256]{3,2,1,0:T(8,128)(2,1)S(1)}, bf16[2,16,16,256]{3,2,1,0:T(8,128)(2,1)S(1)}, u32[]{:S(2)}, u32[]{:S(2)}) collective-permute-start(bf16[2,16,16,256]{3,2,1,0:T(8,128)(2,1)S(1)} %get-tuple-element.61), channel_id=1, source_target_pairs={{0,12},{4,8},{8,4},{12,0},{1,13},{5,9},{9,5},{13,1},{2,14},{6,10},... | collective-permute-start | bytes 786440 | tf_op jit(solution)/shard_map/ppermute | solution.py:420
  43.2 19.9 %copy-start.7 = (bf16[2,16,16,256]{3,2,1,0:T(8,128)(2,1)}, bf16[2,16,16,256]{3,2,1,0:T(8,128)(2,1)S(1)}, u32[]{:S(2)}) copy-start(bf16[2,16,16,256]{3,2,1,0:T(8,128)(2,1)S(1)} %get-tuple-element.62.refs_0_) | copy-start | bytes 786436
  43.2 19.9 %collective-permute-start.6 = (bf16[2,16,16,256]{3,2,1,0:T(8,128)(2,1)S(1)}, bf16[2,16,16,256]{3,2,1,0:T(8,128)(2,1)S(1)}, u32[]{:S(2)}, u32[]{:S(2)}) collective-permute-start(bf16[2,16,16,256]{3,2,1,0:T(8,128)(2,1)S(1)} %get-tuple-element.63.refs_4_), channel_id=1, source_target_pairs={{0,4},{4,0},{8,12},{12,8},{1,5},{5,1},{9,13},{13,9},{2,6},{6,2},{1... | collective-permute-start | bytes 786440 | tf_op jit(solution)/shard_map/ppermute | solution.py:420
  47.7 20.3 %collective-permute-start.7 = (bf16[2,16,16,256]{3,2,1,0:T(8,128)(2,1)S(1)}, bf16[2,16,16,256]{3,2,1,0:T(8,128)(2,1)S(1)}, u32[]{:S(2)}, u32[]{:S(2)}) collective-permute-start(bf16[2,16,16,256]{3,2,1,0:T(8,128)(2,1)S(1)} %get-tuple-element.64.refs_5_), channel_id=1, source_target_pairs={{0,8},{4,12},{8,0},{12,4},{1,9},{5,13},{9,1},{13,5},{2,10},{6,14},... | collective-permute-start | bytes 786440 | tf_op jit(solution)/shard_map/ppermute | solution.py:420
  47.9 20.2 %collective-permute-start.8 = (bf16[2,16,16,256]{3,2,1,0:T(8,128)(2,1)S(1)}, bf16[2,16,16,256]{3,2,1,0:T(8,128)(2,1)S(1)}, u32[]{:S(2)}, u32[]{:S(2)}) collective-permute-start(bf16[2,16,16,256]{3,2,1,0:T(8,128)(2,1)S(1)} %get-tuple-element.65.refs_6_), channel_id=1, source_target_pairs={{0,12},{4,8},{8,4},{12,0},{1,13},{5,9},{9,5},{13,1},{2,14},{6,10},... | collective-permute-start | bytes 786440 | tf_op jit(solution)/shard_map/ppermute | solution.py:420
  63.1 5.0 %copy-start.9 = (bf16[1024,256]{1,0:T(8,128)(2,1)}, bf16[1024,256]{1,0:T(8,128)(2,1)S(1)}, u32[]{:S(2)}) copy-start(bf16[1024,256]{1,0:T(8,128)(2,1)S(1)} %get-tuple-element.67.refs_4_) | copy-start | bytes 1572868
  68.1 27.3 %collective-permute-start.9 = (bf16[2,512,256]{2,1,0:T(8,128)(2,1)S(1)}, bf16[2,512,256]{2,1,0:T(8,128)(2,1)S(1)}, u32[]{:S(2)}, u32[]{:S(2)}) collective-permute-start(bf16[2,512,256]{2,1,0:T(8,128)(2,1)S(1)} %get-tuple-element.69.refs_5_.refs_0_), channel_id=1, source_target_pairs={{0,1},{1,0},{2,3},{3,2},{4,5},{5,4},{6,7},{7,6},{8,9},{9,8},{10,11... | collective-permute-start | bytes 1572872 | tf_op jit(solution)/shard_map/ppermute | solution.py:420
  71.5 23.9 %collective-permute-start.10 = (bf16[2,512,256]{2,1,0:T(8,128)(2,1)S(1)}, bf16[2,512,256]{2,1,0:T(8,128)(2,1)S(1)}, u32[]{:S(2)}, u32[]{:S(2)}) collective-permute-start(bf16[2,512,256]{2,1,0:T(8,128)(2,1)S(1)} %get-tuple-element.69.refs_5_.refs_0_), channel_id=1, source_target_pairs={{0,2},{1,3},{2,0},{3,1},{4,6},{5,7},{6,4},{7,5},{8,10},{9,11},{10,... | collective-permute-start | bytes 1572872 | tf_op jit(solution)/shard_map/ppermute | solution.py:420
  73.2 22.3 %collective-permute-start.11 = (bf16[256,2,512]{2,0,1:T(8,128)(2,1)S(1)}, bf16[256,2,512]{2,0,1:T(8,128)(2,1)S(1)}, u32[]{:S(2)}, u32[]{:S(2)}) collective-permute-start(bf16[256,2,512]{2,0,1:T(8,128)(2,1)S(1)} %copy.34), channel_id=1, source_target_pairs={{0,4},{4,8},{8,12},{12,0},{1,5},{5,9},{9,13},{13,1},{2,6},{6,10},{... | collective-permute-start | bytes 1572872 | tf_op jit(solution)/shard_map/ppermute | solution.py:425
  80.4 0.9 copy-start.8
  81.4 1.0 copy-start.10
  95.4 4.8 %copy-start = (bf16[8,256,2,512]{3,1,2,0:T(8,128)(2,1)S(1)}, bf16[8,256,2,512]{3,1,2,0:T(8,128)(2,1)}, u32[]{:S(2)}) copy-start(bf16[8,256,2,512]{3,1,2,0:T(8,128)(2,1)} %bitcast_dynamic-update-slice_fusion.7) | copy-start | bytes 12582916
  96.1 10.2 %copy-start.3 = (bf16[1,512,512]{2,1,0:T(8,128)(2,1)S(1)}, bf16[1,512,512]{2,1,0:T(8,128)(2,1)}, u32[]{:S(2)}) copy-start(bf16[1,512,512]{2,1,0:T(8,128)(2,1)} %param.13) | copy-start | bytes 1572868
  96.2 8.0 %collective-permute-start.12 = (bf16[512,256]{1,0:T(8,128)(2,1)S(1)}, bf16[512,256]{1,0:T(8,128)(2,1)S(1)}, u32[]{:S(2)}, u32[]{:S(2)}) collective-permute-start(bf16[512,256]{1,0:T(8,128)(2,1)S(1)} %get-tuple-element.76), channel_id=1, source_target_pairs={{0,2},{1,3},{2,0},{3,1},{4,6},{5,7},{6,4},{7,5},{8,10},{9,11},{10,... | collective-permute-start | bytes 786440 | tf_op jit(solution)/shard_map/ppermute | solution.py:420
  98.2 6.4 %collective-permute-start.13 = (bf16[512,256]{1,0:T(8,128)(2,1)S(1)}, bf16[512,256]{1,0:T(8,128)(2,1)S(1)}, u32[]{:S(2)}, u32[]{:S(2)}) collective-permute-start(bf16[512,256]{1,0:T(8,128)(2,1)S(1)} %get-tuple-element.77), channel_id=1, source_target_pairs={{0,1},{1,0},{2,3},{3,2},{4,5},{5,4},{6,7},{7,6},{8,9},{9,8},{10,11... | collective-permute-start | bytes 786440 | tf_op jit(solution)/shard_map/ppermute | solution.py:420
  101.4 27.7 %collective-permute-start.23 = (bf16[2,512,256]{2,1,0:T(8,128)(2,1)S(1)}, bf16[2,512,256]{2,1,0:T(8,128)(2,1)S(1)}, u32[]{:S(2)}, u32[]{:S(2)}) collective-permute-start(bf16[2,512,256]{2,1,0:T(8,128)(2,1)S(1)} %hold.6.refs_2_.refs_1_.refs_5_.refs_0_), channel_id=1, source_target_pairs={{0,1},{1,0},{2,3},{3,2},{4,5},{5,4},{6,7},{7,6},{8,9},{9,8},{10,11... | collective-permute-start | bytes 1572872 | tf_op jit(solution)/shard_map/ppermute | solution.py:420
  101.5 29.2 %collective-permute-start.24 = (bf16[2,512,256]{2,1,0:T(8,128)(2,1)S(1)}, bf16[2,512,256]{2,1,0:T(8,128)(2,1)S(1)}, u32[]{:S(2)}, u32[]{:S(2)}) collective-permute-start(bf16[2,512,256]{2,1,0:T(8,128)(2,1)S(1)} %hold.6.refs_2_.refs_1_.refs_5_.refs_0_), channel_id=1, source_target_pairs={{0,2},{1,3},{2,0},{3,1},{4,6},{5,7},{6,4},{7,5},{8,10},{9,11},{10,... | collective-permute-start | bytes 1572872 | tf_op jit(solution)/shard_map/ppermute | solution.py:420
  104.7 10.1 %collective-permute-start.16 = (bf16[256,512]{1,0:T(8,128)(2,1)S(1)}, bf16[256,512]{1,0:T(8,128)(2,1)S(1)}, u32[]{:S(2)}, u32[]{:S(2)}) collective-permute-start(bf16[256,512]{1,0:T(8,128)(2,1)S(1)} %get-tuple-element.80), channel_id=1, source_target_pairs={{0,12},{4,8},{8,4},{12,0},{1,13},{5,9},{9,5},{13,1},{2,14},{6,10},... | collective-permute-start | bytes 786440 | tf_op jit(solution)/shard_map/ppermute | solution.py:420
  104.8 21.5 %collective-permute-start.15 = (bf16[256,512]{1,0:T(8,128)(2,1)S(1)}, bf16[256,512]{1,0:T(8,128)(2,1)S(1)}, u32[]{:S(2)}, u32[]{:S(2)}) collective-permute-start(bf16[256,512]{1,0:T(8,128)(2,1)S(1)} %get-tuple-element.79), channel_id=1, source_target_pairs={{0,8},{4,12},{8,0},{12,4},{1,9},{5,13},{9,1},{13,5},{2,10},{6,14},... | collective-permute-start | bytes 786440 | tf_op jit(solution)/shard_map/ppermute | solution.py:420
  114.8 14.3 %collective-permute-start.14 = (bf16[256,512]{1,0:T(8,128)(2,1)S(1)}, bf16[256,512]{1,0:T(8,128)(2,1)S(1)}, u32[]{:S(2)}, u32[]{:S(2)}) collective-permute-start(bf16[256,512]{1,0:T(8,128)(2,1)S(1)} %get-tuple-element.78), channel_id=1, source_target_pairs={{0,4},{4,0},{8,12},{12,8},{1,5},{5,1},{9,13},{13,9},{2,6},{6,2},{1... | collective-permute-start | bytes 786440 | tf_op jit(solution)/shard_map/ppermute | solution.py:420
  126.3 11.0 %collective-permute-start.18 = (bf16[256,2,512]{2,0,1:T(8,128)(2,1)S(1)}, bf16[256,2,512]{2,0,1:T(8,128)(2,1)S(1)}, u32[]{:S(2)}, u32[]{:S(2)}) collective-permute-start(bf16[256,2,512]{2,0,1:T(8,128)(2,1)S(1)} %copy.38), channel_id=1, source_target_pairs={{0,4},{4,8},{8,12},{12,0},{1,5},{5,9},{9,13},{13,1},{2,6},{6,10},{... | collective-permute-start | bytes 1572872 | tf_op jit(solution)/shard_map/ppermute | solution.py:425
  129.0 8.3 %collective-permute-start.27 = (bf16[4,256,512]{2,1,0:T(8,128)(2,1)S(1)}, bf16[4,256,512]{2,1,0:T(8,128)(2,1)S(1)}, u32[]{:S(2)}, u32[]{:S(2)}) collective-permute-start(bf16[4,256,512]{2,1,0:T(8,128)(2,1)S(1)} %get-tuple-element.82), channel_id=1, source_target_pairs={{0,16},{16,0},{1,17},{17,1},{2,18},{18,2},{3,19},{19,3},{4,20},{20... | collective-permute-start | bytes 3145736 | tf_op jit(solution)/shard_map/ppermute | solution.py:420
  129.1 9.0 %collective-permute-start.25 = (bf16[512,256]{1,0:T(8,128)(2,1)S(1)}, bf16[512,256]{1,0:T(8,128)(2,1)S(1)}, u32[]{:S(2)}, u32[]{:S(2)}) collective-permute-start(bf16[512,256]{1,0:T(8,128)(2,1)S(1)} %slice_bitcast_fusion.1), channel_id=1, source_target_pairs={{0,2},{1,3},{2,0},{3,1},{4,6},{5,7},{6,4},{7,5},{8,10},{9,11},{10,... | collective-permute-start | bytes 786440 | tf_op jit(solution)/shard_map/ppermute | solution.py:420
  130.7 8.5 %collective-permute-start.26 = (bf16[512,256]{1,0:T(8,128)(2,1)S(1)}, bf16[512,256]{1,0:T(8,128)(2,1)S(1)}, u32[]{:S(2)}, u32[]{:S(2)}) collective-permute-start(bf16[512,256]{1,0:T(8,128)(2,1)S(1)} %slice_bitcast_fusion), channel_id=1, source_target_pairs={{0,1},{1,0},{2,3},{3,2},{4,5},{5,4},{6,7},{7,6},{8,9},{9,8},{10,11... | collective-permute-start | bytes 786440 | tf_op jit(solution)/shard_map/ppermute | solution.py:420
  137.3 7.1 %collective-permute-start.20 = (bf16[256,2,512]{2,0,1:T(8,128)(2,1)}, bf16[256,2,512]{2,0,1:T(8,128)(2,1)S(1)}, u32[]{:S(2)}, u32[]{:S(2)}) collective-permute-start(bf16[256,2,512]{2,0,1:T(8,128)(2,1)} %collective-permute-done.2), channel_id=1, source_target_pairs={{0,16},{16,0},{1,17},{17,1},{2,18},{18,2},{3,19},{19,3},{4,20},{20... | collective-permute-start | bytes 1572872 | tf_op jit(solution)/shard_map/ppermute | solution.py:420
  137.3 7.1 %collective-permute-start.21 = (bf16[256,2,512]{2,0,1:T(8,128)(2,1)S(1)}, bf16[256,2,512]{2,0,1:T(8,128)(2,1)S(1)}, u32[]{:S(2)}, u32[]{:S(2)}) collective-permute-start(bf16[256,2,512]{2,0,1:T(8,128)(2,1)S(1)} %collective-permute-done.11), channel_id=1, source_target_pairs={{0,16},{16,0},{1,17},{17,1},{2,18},{18,2},{3,19},{19,3},{4,20},{20... | collective-permute-start | bytes 1572872 | tf_op jit(solution)/shard_map/ppermute | solution.py:420
  138.1 6.4 %collective-permute-start.17 = (bf16[4,128,512]{2,1,0:T(8,128)(2,1)S(1)}, bf16[4,128,512]{2,1,0:T(8,128)(2,1)S(1)}, u32[]{:S(2)}, u32[]{:S(2)}) collective-permute-start(bf16[4,128,512]{2,1,0:T(8,128)(2,1)S(1)} %pad_maximum_fusion.1), channel_id=1, source_target_pairs={{0,16},{16,0},{1,17},{17,1},{2,18},{18,2},{3,19},{19,3},{4,20},{20... | collective-permute-start | bytes 1572872 | tf_op jit(solution)/shard_map/ppermute | solution.py:420
  139.2 13.2 %collective-permute-start.22 = (bf16[256,2,512]{2,0,1:T(8,128)(2,1)S(1)}, bf16[256,2,512]{2,0,1:T(8,128)(2,1)S(1)}, u32[]{:S(2)}, u32[]{:S(2)}) collective-permute-start(bf16[256,2,512]{2,0,1:T(8,128)(2,1)S(1)} %collective-permute-done.18), channel_id=1, source_target_pairs={{0,16},{16,0},{1,17},{17,1},{2,18},{18,2},{3,19},{19,3},{4,20},{20... | collective-permute-start | bytes 1572872 | tf_op jit(solution)/shard_map/ppermute | solution.py:420
  142.8 14.1 %collective-permute-start.31 = (bf16[4,256,512]{2,1,0:T(8,128)(2,1)S(1)}, bf16[4,256,512]{2,1,0:T(8,128)(2,1)S(1)}, u32[]{:S(2)}, u32[]{:S(2)}) collective-permute-start(bf16[4,256,512]{2,1,0:T(8,128)(2,1)S(1)} %get-tuple-element.88), channel_id=1, source_target_pairs={{0,16},{16,0},{1,17},{17,1},{2,18},{18,2},{3,19},{19,3},{4,20},{20... | collective-permute-start | bytes 3145736 | tf_op jit(solution)/shard_map/ppermute | solution.py:420
  148.0 11.2 %collective-permute-start.30 = (bf16[1,256,512]{2,1,0:T(8,128)(2,1)S(1)}, bf16[1,256,512]{2,1,0:T(8,128)(2,1)S(1)}, u32[]{:S(2)}, u32[]{:S(2)}) collective-permute-start(bf16[1,256,512]{2,1,0:T(8,128)(2,1)S(1)} %get-tuple-element.86.refs_10_), channel_id=1, source_target_pairs={{0,12},{4,8},{8,4},{12,0},{1,13},{5,9},{9,5},{13,1},{2,14},{6,10},... | collective-permute-start | bytes 786440 | tf_op jit(solution)/shard_map/ppermute | solution.py:420
  149.3 35.9 %collective-permute-start.29 = (bf16[1,256,512]{2,1,0:T(8,128)(2,1)S(1)}, bf16[1,256,512]{2,1,0:T(8,128)(2,1)S(1)}, u32[]{:S(2)}, u32[]{:S(2)}) collective-permute-start(bf16[1,256,512]{2,1,0:T(8,128)(2,1)S(1)} %get-tuple-element.85.refs_9_), channel_id=1, source_target_pairs={{0,8},{4,12},{8,0},{12,4},{1,9},{5,13},{9,1},{13,5},{2,10},{6,14},... | collective-permute-start | bytes 786440 | tf_op jit(solution)/shard_map/ppermute | solution.py:420
  149.9 35.3 %collective-permute-start.28 = (bf16[1,256,512]{2,1,0:T(8,128)(2,1)S(1)}, bf16[1,256,512]{2,1,0:T(8,128)(2,1)S(1)}, u32[]{:S(2)}, u32[]{:S(2)}) collective-permute-start(bf16[1,256,512]{2,1,0:T(8,128)(2,1)S(1)} %get-tuple-element.84.refs_8_), channel_id=1, source_target_pairs={{0,4},{4,0},{8,12},{12,8},{1,5},{5,1},{9,13},{13,9},{2,6},{6,2},{1... | collective-permute-start | bytes 786440 | tf_op jit(solution)/shard_map/ppermute | solution.py:420
  157.0 28.3 %collective-permute-start.34 = (bf16[1,256,512]{2,1,0:T(8,128)(2,1)S(1)}, bf16[1,256,512]{2,1,0:T(8,128)(2,1)S(1)}, u32[]{:S(2)}, u32[]{:S(2)}) collective-permute-start(bf16[1,256,512]{2,1,0:T(8,128)(2,1)S(1)} %get-tuple-element.92), channel_id=1, source_target_pairs={{0,12},{4,8},{8,4},{12,0},{1,13},{5,9},{9,5},{13,1},{2,14},{6,10},... | collective-permute-start | bytes 786440 | tf_op jit(solution)/shard_map/ppermute | solution.py:420
  158.3 37.3 %collective-permute-start.33 = (bf16[1,256,512]{2,1,0:T(8,128)(2,1)S(1)}, bf16[1,256,512]{2,1,0:T(8,128)(2,1)S(1)}, u32[]{:S(2)}, u32[]{:S(2)}) collective-permute-start(bf16[1,256,512]{2,1,0:T(8,128)(2,1)S(1)} %get-tuple-element.91), channel_id=1, source_target_pairs={{0,8},{4,12},{8,0},{12,4},{1,9},{5,13},{9,1},{13,5},{2,10},{6,14},... | collective-permute-start | bytes 786440 | tf_op jit(solution)/shard_map/ppermute | solution.py:420
  159.2 36.4 %collective-permute-start.32 = (bf16[1,256,512]{2,1,0:T(8,128)(2,1)S(1)}, bf16[1,256,512]{2,1,0:T(8,128)(2,1)S(1)}, u32[]{:S(2)}, u32[]{:S(2)}) collective-permute-start(bf16[1,256,512]{2,1,0:T(8,128)(2,1)S(1)} %get-tuple-element.90), channel_id=1, source_target_pairs={{0,4},{4,0},{8,12},{12,8},{1,5},{5,1},{9,13},{13,9},{2,6},{6,2},{1... | collective-permute-start | bytes 786440 | tf_op jit(solution)/shard_map/ppermute | solution.py:420

commit v3 on v2

--- a/solution.py
+++ b/solution.py
@@ -17,6 +17,7 @@
 ATTEND_BYTES = 24 * 1024 * 1024
 
 VMEM_SPEC = pl.BlockSpec(memory_space=pltpu.VMEM)
+HBM_SPEC = pl.BlockSpec(memory_space=pltpu.HBM)
 ANY_SPEC = pl.BlockSpec(memory_space=pl.ANY)
 SMEM_SPEC = pl.BlockSpec(memory_space=pltpu.SMEM)
 NT = (((1,), (1,)), ((), ()))
@@ -39,7 +40,7 @@
 
 def pack_kernel(peers, per_peer, chunk, chunks, me_ref, owners_hbm, q_hbm, g_hbm, *refs):
     both_ref, count_ref, owners_ref, q_ref, g_ref, sems = refs[-6:]
-    table_ref, out_refs = refs[-8 - peers // 2], refs[-7 - peers // 2 : -6]
+    table_ref, out_refs = refs[-7 - peers], refs[-6 - peers : -6]
     targets, rows, width = q_ref.shape
     groups = width // (chunks * LANES)
     copies = fetch([owners_hbm, q_hbm, g_hbm], [owners_ref, q_ref, g_ref], sems)
@@ -82,7 +83,7 @@
 
         def move(slot, _, d=d):
             out_refs[d][slot] = both_ref[table_ref[d * per_peer + slot]]
-            out_refs[half][d, slot] = both_ref[table_ref[(half + d) * per_peer + slot]]
+            out_refs[half + d][slot] = both_ref[table_ref[(half + d) * per_peer + slot]]
             return 0
 
         lax.fori_loop(0, per_peer, move, 0, unroll=4)
@@ -95,10 +96,9 @@
     outs = pl.pallas_call(
         functools.partial(pack_kernel, peers, per_peer, chunk, chunks),
         out_shape=[jax.ShapeDtypeStruct((peers * per_peer,), jnp.int32)]
-        + [jax.ShapeDtypeStruct(block, BF16)] * half
-        + [jax.ShapeDtypeStruct((half,) + block, BF16)],
-        in_specs=[SMEM_SPEC, ANY_SPEC, ANY_SPEC, ANY_SPEC],
-        out_specs=[SMEM_SPEC] + [VMEM_SPEC] * (half + 1),
+        + [jax.ShapeDtypeStruct(block, BF16)] * peers,
+        in_specs=[SMEM_SPEC, HBM_SPEC, HBM_SPEC, HBM_SPEC],
+        out_specs=[SMEM_SPEC] + [VMEM_SPEC] * peers,
         scratch_shapes=[
             pltpu.VMEM((targets + 1, 2 * rows, part), BF16),
             pltpu.SMEM((peers,), jnp.int32),
@@ -111,7 +111,7 @@
         cost_estimate=cost(0, 3 << 20),
         name="pack_targets",
     )(me, owners, queries, out_grads)
-    return outs[0], outs[1:-1], outs[-1]
+    return outs[0], outs[1 : 1 + half], outs[1 + half :]
 
 
 def hold_kernel(count, *refs):
@@ -123,7 +123,7 @@
     return pl.pallas_call(
         functools.partial(hold_kernel, len(arrays)),
         out_shape=[jax.ShapeDtypeStruct(x.shape, x.dtype) for x in arrays],
-        in_specs=[VMEM_SPEC] * (len(arrays) + len(earlier)),
+        in_specs=[VMEM_SPEC] * len(arrays) + [ANY_SPEC] * len(earlier),
         out_specs=[VMEM_SPEC] * len(arrays),
         compiler_params=pltpu.CompilerParams(vmem_limit_bytes=VMEM_BYTES),
         cost_estimate=cost(0, 1 << 20),
@@ -131,11 +131,34 @@
     )(*arrays, *earlier)
 
 
+def token(arrays):
+    return sum(x.reshape(-1, x.shape[-1])[:1, :LANES].astype(F32) for x in arrays)
+
+
+def join_kernel(near0, near1, over0, over1, *refs):
+    first_ref, second_ref = refs[-2:]
+    first_ref[0], first_ref[1] = near0[0], near1[0]
+    second_ref[0], second_ref[1] = over0[1], over1[1]
+
+
+def join(near, over, earlier):
+    shape = jax.ShapeDtypeStruct(near[0].shape, BF16)
+    return pl.pallas_call(
+        join_kernel,
+        out_shape=[shape] * 2,
+        in_specs=[VMEM_SPEC] * 4 + [ANY_SPEC] * len(earlier),
+        out_specs=[VMEM_SPEC] * 2,
+        compiler_params=pltpu.CompilerParams(vmem_limit_bytes=VMEM_BYTES),
+        cost_estimate=cost(0, 1 << 20),
+        name="join",
+    )(*near, *over, *earlier)
+
+
 def merge_kernel(half, *refs):
-    blocks, got_ref, out_refs = refs[:half], refs[half], refs[-half:]
+    blocks, got_refs, out_refs = refs[:half], refs[half : 2 * half], refs[-half:]
     for d in range(half):
         out_refs[d][0] = blocks[d][...]
-        out_refs[d][1] = got_ref[d]
+        out_refs[d][1] = got_refs[d][...]
 
 
 def merge(blocks, got, earlier):
@@ -143,12 +166,12 @@
     return pl.pallas_call(
         functools.partial(merge_kernel, half),
         out_shape=[jax.ShapeDtypeStruct((2,) + blocks[0].shape, BF16)] * half,
-        in_specs=[VMEM_SPEC] * (half + 1 + len(earlier)),
+        in_specs=[VMEM_SPEC] * (2 * half) + [ANY_SPEC] * len(earlier),
         out_specs=[VMEM_SPEC] * half,
         compiler_params=pltpu.CompilerParams(vmem_limit_bytes=VMEM_BYTES),
         cost_estimate=cost(0, 1 << 20),
         name="merge",
-    )(*blocks, got, *earlier)
+    )(*blocks, *got, *earlier)
 
 
 def unpack_kernel(peers, per_peer, table_ref, *refs):
@@ -199,25 +222,31 @@
     )(table, *near, over)
 
 
-def attend_kernel(peers, chunk, chunks, waits, len_ref, k_ref, v_ref, *refs):
+def attend_kernel(peers, chunk, chunks, waits, len_ref, k_hbm, v_hbm, *refs):
     half = peers // 2
     in_refs, before_refs = refs[:half], refs[half : half + chunk]
-    groups = k_ref.shape[1] // (chunks * LANES)
-    outs = refs[half + chunk + waits : -6]
+    groups = k_hbm.shape[1] // (chunks * LANES)
+    outs = refs[half + chunk + waits : -9]
     kv_ref, out_refs = outs[0], outs[1:]
-    q_s, g_s, o_s, kt_s, kg_s, vg_s = refs[-6:]
+    q_s, g_s, o_s, kt_s, kg_s, vg_s, k_ref, v_ref, sems = refs[-9:]
     src_len = k_ref.shape[0]
-    _, per_peer, double, width = in_refs[0].shape
+    copies = fetch([k_hbm, v_hbm], [k_ref, v_ref], sems)
+    _, per_peer, double, _ = in_refs[0].shape
+    width = groups * LANES
     rows = double // 2
     block_rows = per_peer * rows
     total_rows = peers * block_rows
-    tile = min(256, total_rows)
+    tile = min(1024, total_rows)
     scale = HEAD_DIM**-0.5
     for d in range(peers):
-        both = in_refs[d // 2][d % 2].astype(F32)
         at = slice(d * block_rows, (d + 1) * block_rows)
-        q_s[at] = (both[:, :rows] * scale).reshape(block_rows, width).astype(BF16)
-        g_s[at] = both[:, rows:].reshape(block_rows, width).astype(BF16)
+        for a in range(groups):
+            lane, mine = (a * chunks + chunk) * LANES, slice(a * LANES, (a + 1) * LANES)
+            both = in_refs[d // 2][d % 2, :, :, lane : lane + LANES].astype(F32)
+            q_s[at, mine] = (both[:, :rows] * scale).reshape(block_rows, LANES).astype(BF16)
+            g_s[at, mine] = both[:, rows:].reshape(block_rows, LANES).astype(BF16)
+    for copy in copies:
+        copy.wait()
     valid = lax.broadcasted_iota(jnp.int32, (src_len, 1), 0) < len_ref[0]
     lane_head = lax.broadcasted_iota(jnp.int32, (1, LANES), 1) // HEAD_DIM
     for a in range(groups):
@@ -274,7 +303,8 @@
     half = len(blocks)
     peers = 2 * half
     src_len, width = keys.shape
-    _, per_peer, double, part = blocks[0].shape
+    _, per_peer, double, _ = blocks[0].shape
+    part = width // chunks
     block_rows = per_peer * double // 2
     total_rows = peers * block_rows
     groups = part // LANES
@@ -285,7 +315,7 @@
     outs = pl.pallas_call(
         functools.partial(attend_kernel, peers, chunk, chunks, len(earlier)),
         out_shape=[jax.ShapeDtypeStruct((groups, src_len, 2 * LANES), BF16)] + query_shapes,
-        in_specs=[SMEM_SPEC] + [VMEM_SPEC] * (2 + half + chunk + len(earlier)),
+        in_specs=[SMEM_SPEC, HBM_SPEC, HBM_SPEC] + [VMEM_SPEC] * (half + chunk + len(earlier)),
         out_specs=[VMEM_SPEC] * (1 + len(query_shapes)),
         scratch_shapes=[
             pltpu.VMEM((total_rows, part), BF16),
@@ -294,6 +324,9 @@
             pltpu.VMEM((LANES, src_len), BF16),
             pltpu.VMEM((src_len, LANES), F32),
             pltpu.VMEM((src_len, LANES), F32),
+            pltpu.VMEM(keys.shape, BF16),
+            pltpu.VMEM(values.shape, BF16),
+            pltpu.SemaphoreType.DMA((2,)),
         ],
         compiler_params=pltpu.CompilerParams(vmem_limit_bytes=ATTEND_BYTES),
         cost_estimate=cost(
@@ -304,116 +337,114 @@
     return outs[0], outs[1:]
 
 
-def weight_kernel(blocks, place_ref, states_ref, *refs):
-    own_ref, sib_ref, states_s, pairs_s, across_s, sems = refs[-6:]
-    targets = [states_s] + [pairs_s.at[e] for e in range(3)] + [across_s.at[a] for a in range(2)]
-    copies = fetch([states_ref] + list(refs[:blocks]), targets, sems)
+def weight_kernel(count, first, place_ref, states_ref, *refs):
+    own_ref, sib_ref, states_s, blocks_s, sems = refs[-5:]
+    copies = fetch(
+        [states_ref] + list(refs[:count]), [states_s] + [blocks_s.at[i] for i in range(count)], sems
+    )
     copies[0].wait()
     states = states_s[...]
-    for index in range(8):
-        e, a = index // 2, index % 2
-        if e < 3 and a == 0:
-            copies[1 + e].wait()
-        elif e == 3:
-            copies[4 + a].wait()
-        block = pairs_s[e, a] if e < 3 else across_s[a]
-        piece = lax.dot_general(block, states, TN, preferred_element_type=F32)
-        away, seq = place_ref[2 * index], place_ref[2 * index + 1]
-
-        @pl.when(away == 0)
-        def _(piece=piece, seq=seq):
-            own_ref[seq] = piece
-
-        @pl.when(away != 0)
-        def _(piece=piece, seq=seq):
-            sib_ref[seq] = piece.astype(BF16)
-
-
-def weight_parts(place, states, blocks, seq_size, earlier):
+    tall = blocks_s.shape[-1]
+    for i in range(count):
+        copies[1 + i].wait()
+        for k in range(2):
+            index, c = (2 * (i // 2) + k, i % 2) if first == 0 else (first + i, k)
+            piece = lax.dot_general(blocks_s[i, k], states, TN, preferred_element_type=F32)
+            away, seq = place_ref[2 * index], place_ref[2 * index + 1]
+            at = slice(c * tall, (c + 1) * tall)
+
+            @pl.when(away == 0)
+            def _(piece=piece, seq=seq, at=at):
+                own_ref[seq, at] = piece
+
+            @pl.when(away != 0)
+            def _(piece=piece, seq=seq, at=at):
+                sib_ref[seq, at] = piece.astype(BF16)
+
+
+def weight_parts(place, states, blocks, first, seq_size, totals=(), earlier=()):
     src_len, width = states.shape
-    tall = blocks[0].shape[2]
+    tall = 2 * blocks[0].shape[-1]
     shape = (seq_size, tall, width)
+    given = 2 + len(blocks)
     return pl.pallas_call(
-        functools.partial(weight_kernel, len(blocks)),
+        functools.partial(weight_kernel, len(blocks), first),
         out_shape=[jax.ShapeDtypeStruct(shape, F32), jax.ShapeDtypeStruct(shape, BF16)],
-        in_specs=[SMEM_SPEC] + [ANY_SPEC] * (1 + len(blocks) + len(earlier)),
+        in_specs=[SMEM_SPEC, HBM_SPEC]
+        + [ANY_SPEC] * len(blocks)
+        + [VMEM_SPEC] * len(totals)
+        + [ANY_SPEC] * len(earlier),
         out_specs=[VMEM_SPEC] * 2,
+        input_output_aliases={given + i: i for i in range(len(totals))},
         scratch_shapes=[
             pltpu.VMEM((src_len, width), BF16),
-            pltpu.VMEM((3, 2, src_len, tall), BF16),
-            pltpu.VMEM((2, src_len, tall), BF16),
+            pltpu.VMEM((len(blocks),) + blocks[0].shape, BF16),
             pltpu.SemaphoreType.DMA((1 + len(blocks),)),
         ],
         compiler_params=pltpu.CompilerParams(vmem_limit_bytes=VMEM_BYTES),
-        cost_estimate=cost(16 * src_len * tall * width, 6 << 20),
+        cost_estimate=cost(8 * len(blocks) * src_len * tall * width, 6 << 20),
         name="weight_parts",
-    )(place, states, *blocks, *earlier)
-
-
-def combine_kernel(chunks, seq_ref, *refs):
-    parts, outs = refs[: 2 * chunks], refs[2 * chunks :]
-    for d in range(len(outs)):
+    )(place, states, *blocks, *totals, *earlier)
+
+
+def combine_kernel(pieces, seq_ref, own_ref, got_ref, *refs):
+    for d, out_ref in enumerate(refs[-pieces:]):
         index = seq_ref[0] ^ d
-        for c in range(chunks):
-            total = parts[2 * c][index] + parts[2 * c + 1][index].astype(F32)
-            outs[d][c] = total.astype(outs[d].dtype)
-
-
-def combine(seq, parts):
-    pieces, tall, width = parts[0][0].shape
-    shape = (len(parts), tall, width)
+        total = own_ref[index] + got_ref[index].astype(F32)
+        out_ref[...] = total.astype(out_ref.dtype)
+
+
+def combine(seq, own, got, earlier):
+    pieces, *shape = own.shape
     return pl.pallas_call(
-        functools.partial(combine_kernel, len(parts)),
+        functools.partial(combine_kernel, pieces),
         out_shape=[jax.ShapeDtypeStruct(shape, F32)]
         + [jax.ShapeDtypeStruct(shape, BF16)] * (pieces - 1),
-        in_specs=[SMEM_SPEC] + [VMEM_SPEC] * (2 * len(parts)),
+        in_specs=[SMEM_SPEC] + [VMEM_SPEC] * 2 + [ANY_SPEC] * len(earlier),
         out_specs=[VMEM_SPEC] * pieces,
         compiler_params=pltpu.CompilerParams(vmem_limit_bytes=VMEM_BYTES),
         cost_estimate=cost(0, 6 << 20),
         name="combine",
-    )(seq, *[x for part in parts for x in part])
-
-
-def state_kernel(chunks, order_ref, w_ref, *refs):
-    in_refs, out_ref = refs[: 5 * chunks], refs[5 * chunks]
-    total_ref, w_s, pairs_s, across_s, sems = refs[5 * chunks + 1 :]
-    targets = []
-    for c in range(chunks):
-        targets += [pairs_s.at[c, e] for e in range(3)] + [across_s.at[c, a] for a in range(2)]
-    copies = fetch([w_ref] + list(in_refs), [w_s] + targets, sems)
+    )(seq, own, got, *earlier)
+
+
+def state_kernel(pieces, order_ref, *refs):
+    in_refs, out_ref = refs[: 8 + pieces], refs[8 + pieces]
+    total_ref, w_s, blocks_s, sems = refs[9 + pieces :]
+    targets = [blocks_s.at[i] for i in range(8)]
+    copies = fetch(in_refs, [w_s.at[i] for i in range(pieces)] + targets, sems)
     for copy in copies:
         copy.wait()
     total_ref[...] = jnp.zeros_like(total_ref)
-    for c in range(chunks):
-        at = slice(c * LANES, (c + 1) * LANES)
-        for index in range(8):
-            e, a = index // 2, index % 2
-            piece = order_ref[index]
+    for index in range(8):
+        e, a = index // 2, index % 2
+        piece = order_ref[index]
+        for c in range(2):
+            at = slice(c * LANES, (c + 1) * LANES)
             weight = jnp.concatenate([w_s[piece, 0, at], w_s[piece, 1, at]], axis=0)
-            block = pairs_s[c, e, a] if e < 3 else across_s[c, a]
+            block = blocks_s[2 * e + c, a] if e < 3 else blocks_s[6 + a, c]
             total_ref[...] += jnp.dot(block, weight, preferred_element_type=F32)
     out_ref[...] = total_ref[...].astype(BF16)
 
 
-def state_grads(order, weights, blocks, chunks):
-    src_len, tall = blocks[0].shape[1:]
-    width = weights.shape[-1]
+def state_grads(order, weights, blocks):
+    src_len = blocks[0].shape[1]
+    pieces, width = len(weights), weights[0].shape[-1]
     return pl.pallas_call(
-        functools.partial(state_kernel, chunks),
+        functools.partial(state_kernel, pieces),
         out_shape=jax.ShapeDtypeStruct((src_len, width), BF16),
-        in_specs=[SMEM_SPEC] + [ANY_SPEC] * (1 + len(blocks)),
+        in_specs=[SMEM_SPEC] + [ANY_SPEC] * (pieces + len(blocks)),
         out_specs=VMEM_SPEC,
         scratch_shapes=[
             pltpu.VMEM((src_len, width), F32),
-            pltpu.VMEM(weights.shape, BF16),
-            pltpu.VMEM((chunks, 3, 2, src_len, tall), BF16),
-            pltpu.VMEM((chunks, 2, src_len, tall), BF16),
-            pltpu.SemaphoreType.DMA((1 + len(blocks),)),
+            pltpu.VMEM((pieces,) + weights[0].shape, BF16),
+            pltpu.VMEM((len(blocks),) + blocks[0].shape, BF16),
+            pltpu.SemaphoreType.DMA((pieces + len(blocks),)),
         ],
         compiler_params=pltpu.CompilerParams(vmem_limit_bytes=ATTEND_BYTES),
         cost_estimate=cost(32 * src_len * 2 * LANES * width, 8 << 20),
         name="state_grads",
-    )(order, weights, *blocks)
+    )(order, *weights, *blocks)
 
 
 def swap(x, axes, size, distance):
@@ -427,7 +458,7 @@
 
 def exchange(blocks, sib, earlier):
     half = len(blocks)
-    got = swap(sib, "grp", 2, 1)
+    got = [swap(x, "grp", 2, 1) for x in sib]
     pairs = merge(blocks, got, earlier)
     line = {d: swap(pairs[d], "seq", half, d) for d in range(half - 1, 0, -1)}
     return [pairs[0]] + [line[d] for d in range(1, half)], pairs[1:]
@@ -438,17 +469,6 @@
     line = {d: swap(pairs[d], "seq", half, d) for d in range(half - 1, 0, -1)}
     near = [pairs[0]] + [line[d] for d in range(1, half)]
     return near, swap(jnp.stack([pair[rows:] for pair in near]), "grp", 2, 1)
-
-
-def gather_near(pair):
-    return [pair, swap(pair, "mdl", 4, 1), swap(pair, "mdl", 4, 2)]
-
-
-def gather_across(pair, near, over, earlier=()):
-    first, second = near[0], over[1]
-    if earlier:
-        first, second = hold([first, second], earlier)
-    return [pair, near, over, swap(first, "mdl", 4, 2), swap(second, "mdl", 4, 1)]
 
 
 def block_grads(query_block, grad_block, key_local, value_local, key_valid):
@@ -567,7 +587,7 @@
     per_peer = max(2, 2 * targets // peers)
     src_len = src_keys.shape[1]
     chunks = CHUNKS
-    groups = width // (chunks * LANES)
+    groups = 2
     me = lax.axis_index(PEERS).astype(jnp.int32)
     mdl = lax.axis_index("mdl").astype(jnp.int32)
     grp = lax.axis_index("grp").astype(jnp.int32)
@@ -576,54 +596,37 @@
     source = mdl ^ (jnp.arange(4 * groups, dtype=jnp.int32) // groups)
     order = source * groups + jnp.arange(4 * groups, dtype=jnp.int32) % groups
     seq = lax.axis_index("seq").astype(jnp.int32)
-    distance = (seq - jnp.arange(seq_size, dtype=jnp.int32)) % seq_size
+    weight_order = ((order // seq_size) ^ grp) * seq_size + (seq - order) % seq_size
     place = jnp.stack([(order // seq_size) ^ grp, order % seq_size], axis=1).reshape(-1)
 
-    lines = [kv_weight, ring(kv_weight)]
-    got, earlier = [], lines[1:]
-    for c in range(chunks):
-        table, blocks, sib = pack(
-            me[None], owners, queries, out_grads, peers, per_peer, c, chunks
-        )
-        arrived, sent = exchange(blocks, sib, earlier)
-        got.append(arrived)
-        earlier = arrived[1:]
-    gathered, before = [], []
-    for c in range(chunks):
-        last = c == chunks - 1
-        pair, query_blocks = attend(
-            src_lengths, keys, values, got[c], before, [pair] if last else sent
-        )
-        if last:
-            pair = hold([pair], gathered[0][1:] + lines[2:])[0]
-        else:
-            pair, held = hold([pair, lines[1]], got[c + 1][1:])
-            lines.append(ring(held))
-        before = before + list(query_blocks[:1])
-        gathered.append(gather_near(pair))
-    lines.append(ring(hold(lines[2:], [pair])[0]))
-    gathered = [gather_across(*part, [pair] if c == 0 else []) for c, part in enumerate(gathered)]
-    query_blocks = [query_blocks[0], *hold(query_blocks[1:], gathered[0][3:])]
-    near, over = send_back(query_blocks)
-    sums = []
-    for c in range(chunks):
-        own, sib = weight_parts(
-            place, flat_states, gathered[c], seq_size, near[1:] + sends if c else [pair]
-        )
-        keep, *sends = combine(seq[None], [(own, swap(sib, "grp", 2, 1))])
-        line = [swap(x, "seq", seq_size, d + 1) for d, x in enumerate(sends)]
-        sums.append(keep + sum(x.astype(F32) for x in line))
+    tall = jnp.transpose(kv_weight, (1, 0, 2))
+    lines = [tall, ring(tall)]
+    table, blocks, sib = pack(me[None], owners, queries, out_grads, peers, per_peer, 0, 1)
+    got, _ = exchange(blocks, sib, lines[1:])
+    lines.append(ring(hold(lines[1:], got[1:])[0]))
+    lines.append(ring(lines[2]))
+    first, before = attend(src_lengths, keys, values, got, [], [])
+    near, over = [swap(first, "mdl", 4, 1)], [swap(first, "mdl", 4, 2)]
+    second, query_blocks = attend(src_lengths, keys, values, got, before, [token(lines[2:3])])
+    back, other = send_back(query_blocks)
+    second = hold([second], [near[0], over[0], lines[3]])[0]
+    near.append(swap(second, "mdl", 4, 1))
+    over.append(swap(second, "mdl", 4, 2))
+    across = join(near, over, [])
+    across = [swap(across[0], "mdl", 4, 2), swap(across[1], "mdl", 4, 1)]
+    gathered = [first, second, *near, *over, *across]
+    totals = weight_parts(place, flat_states, gathered[:6], 0, seq_size, (), [])
+    own, sib = weight_parts(
+        place, flat_states, gathered[6:], 6, seq_size, totals, back[1:]
+    )
+    keep, *sends = combine(seq[None], own, swap(sib, "grp", 2, 1), [])
+    line = [swap(sends[d - 1], "seq", seq_size, d) for d in range(seq_size - 1, 0, -1)]
+    weight_sum = keep + sum(x.astype(F32) for x in line)
     lines = lines + [swap(x, "grp", 2, 1) for x in lines]
-    weights = jnp.stack(lines).transpose(0, 2, 1, 3)
-    own_pieces, other_pieces = grp * seq_size + distance, (1 - grp) * seq_size + distance
-    piece_at = jnp.zeros((peers,), jnp.int32)
-    piece_at = piece_at.at[own_pieces].set(jnp.arange(seq_size, dtype=jnp.int32))
-    piece_at = piece_at.at[other_pieces].set(seq_size + jnp.arange(seq_size, dtype=jnp.int32))
-    state_out = state_grads(piece_at[order], weights, [b for part in gathered for b in part], chunks)
-    query_out = unpack(table, near, over, targets, rows, per_peer)
-    weight_sum = jnp.concatenate(sums, axis=0)
-    weight_out = weight_sum.reshape(chunks, 2, LANES, width).transpose(0, 2, 1, 3)
-    weight_out = weight_out.reshape(chunks * LANES, 2, width)
+    state_out = state_grads(weight_order, lines, gathered)
+    query_out = unpack(table, back, other, targets, rows, per_peer)
+    weight_out = weight_sum.reshape(2, 2, LANES, width).transpose(0, 2, 1, 3)
+    weight_out = weight_out.reshape(2 * LANES, 2, width)
     return (query_out, state_out.reshape(1, src_len, width), weight_out)
 
 

time: 198 us -> 185 us (0.934)
  waiting for transfers between devices: 71.7 us -> 99.9 us
  starting transfers between devices: 60.8 us -> 40.8 us
  local copies, waits for them, and re-layouts: 17.1 us -> 5.86 us
  Pallas kernels: 45.7 us -> 36.1 us
    ppermute x32 -> x25, waiting for transfers between devices: 59.1 us -> 90.3 us  [swap(): return lax.ppermute(x, axes, [(i, i ^ distance) for i in range(size)])]
    ppermute x32 -> x25, starting transfers between devices: 50.5 us -> 21.4 us  [swap(): return lax.ppermute(x, axes, [(i, i ^ distance) for i in range(size)])]
    pallas_call x2, Pallas kernels: 25.9 us -> 16.4 us  [attend(): pl.pallas_call(functools.partial(attend_kernel, peers, chunk, chunks, len...]
    ppermute x3, starting transfers between devices: 10.3 us -> 19.4 us  [ring(): return lax.ppermute(x, 'seq', [(z, (z + 1) % size) for z in range(size)])]
    unnamed x30 -> x27, local copies, waits for them, and re-layouts: 10.9 us -> 3.88 us
    ppermute x3, waiting for transfers between devices: 12.6 us -> 9.61 us  [ring(): return lax.ppermute(x, 'seq', [(z, (z + 1) % size) for z in range(size)])]
    pallas_call x5, Pallas kernels: 11.9 us -> 14.2 us  [the longest x2 7.2 us: weight_parts(): pl.pallas_call(functools.partial(weight_kernel, len(blocks), first), out_...]
    pallas_call x2 -> x1, Pallas kernels: 4.03 us -> 1.91 us  [pack(): pl.pallas_call(functools.partial(pack_kernel, peers, per_peer, chunk, chu...]
  transfers between devices with their start and end apart: 35 -> 28, of which waited for: 14 -> 19; matrix products, arithmetic and copies ran while one was open for 4% -> 0% of each run, Pallas kernels for 23% -> 18%
where the time goes in v3:
time: 185 us
  waiting for transfers between devices  99.9 us (54%)
  starting transfers between devices  40.8 us (22%)
  Pallas kernels  36.1 us (20%)
  local copies, waits for them, and re-layouts  5.86 us (3%)
    ppermute x25, waiting for transfers between devices, swap(): return lax.ppermute(x, axes, [(i, i ^ distance) for i in range(size)])  90.3 us
    ppermute x25, starting transfers between devices, swap(): return lax.ppermute(x, axes, [(i, i ^ distance) for i in range(size)])  21.4 us
    ppermute x3, starting transfers between devices, ring(): return lax.ppermute(x, 'seq', [(z, (z + 1) % size) for z in range(size)])  19.4 us
    pallas_call x2, Pallas kernels, attend(): pl.pallas_call(functools.partial(attend_kernel, peers, chunk, chunks, len...  16.4 us
    ppermute x3, waiting for transfers between devices, ring(): return lax.ppermute(x, 'seq', [(z, (z + 1) % size) for z in range(size)])  9.61 us
    pallas_call x2, Pallas kernels, weight_parts(): pl.pallas_call(functools.partial(weight_kernel, len(blocks), first), out_...  7.2 us
    pallas_call x1, Pallas kernels, state_grads(): pl.pallas_call(functools.partial(state_kernel, pieces), out_shape=jax.Sha...  5.41 us
    unnamed x27, local copies, waits for them, and re-layouts  3.88 us
  transfers between devices with their start and end apart: 28, of which 19 were waited for; matrix products, arithmetic and copies ran while one was open for 0% of the time, Pallas kernels for 18%

profile of v3, /device:TPU:0, one launch (start us, length us, event | category | flops | bytes accessed | tf_op | source)
XLA Modules:
  0.0 184.8 jit_solution(16165755981584547949)
XLA Ops:
  0.6 1.1 copy.21
  1.7 3.1 %collective-permute-start.4 = (bf16[2,256,512]{2,1,0:T(8,128)(2,1)S(1)}, bf16[2,256,512]{2,1,0:T(8,128)(2,1)S(1)}, u32[]{:S(2)}, u32[]{:S(2)}) collective-permute-start(bf16[2,256,512]{2,1,0:T(8,128)(2,1)S(1)} %bitcast.22), channel_id=1, source_target_pairs={{0,4},{4,8},{8,12},{12,0},{1,5},{5,9},{9,13},{13,1},{2,6},{6,10},{... | collective-permute-start | bytes 1572872 | tf_op jit(solution)/shard_map/ppermute | solution.py:456
  4.8 1.0 copy-done.5
  5.8 1.0 copy-done.6
  6.9 0.7 copy-done.7
  7.5 1.9 %pack_targets.1 = (s32[128]{0:T(128)S(1)}, bf16[16,16,512]{2,1,0:T(8,128)(2,1)S(1)}, bf16[16,16,512]{2,1,0:T(8,128)(2,1)S(1)}, bf16[16,16,512]{2,1,0:T(8,128)(2,...) custom-call(s32[1]{0:T(128)} %bitcast.me_ref, ...), custom_call_target="tpu_custom_call" | custom-call | bytes 3145728 | tf_op jit(solution)/shard_map/pack_targets/pallas_call | solution.py:96
  9.5 0.1 collective-permute-start
  9.5 0.5 collective-permute-start.1
  10.0 0.1 collective-permute-start.2
  10.1 0.4 collective-permute-start.3
  10.5 0.5 collective-permute-done.refs_4_
  11.1 0.4 collective-permute-done.1.refs_5_
  11.4 0.4 collective-permute-done.2.refs_6_
  11.8 0.4 collective-permute-done.3.refs_7_
  12.2 6.6 %collective-permute-done.4.refs_8_.refs_0_.refs_1_ = bf16[2,256,512]{2,1,0:T(8,128)(2,1)S(1)} collective-permute-done((bf16[2,256,512]{2,1,0:T(8,128)(2,1)S(1)}, bf16[2,256,512]{2,1,0:T(8,128)(2,1)S(1)}, u32[]{:S(2)}, u32[]{:S(2)}) %collective-permute-start.4) | collective-permute-done | bytes 524320 | tf_op jit(solution)/shard_map/ppermute | solution.py:456
  18.8 0.1 merge.1
  18.9 0.1 collective-permute-start.5
  19.0 2.3 %collective-permute-start.6 = (bf16[2,16,16,512]{3,2,1,0:T(8,128)(2,1)S(1)}, bf16[2,16,16,512]{3,2,1,0:T(8,128)(2,1)S(1)}, u32[]{:S(2)}, u32[]{:S(2)}) collective-permute-start(bf16[2,16,16,512]{3,2,1,0:T(8,128)(2,1)S(1)} %get-tuple-element.44), channel_id=1, source_target_pairs={{0,8},{4,12},{8,0},{12,4},{1,9},{5,13},{9,1},{13,5},{2,10},{6,14},... | collective-permute-start | bytes 1572872 | tf_op jit(solution)/shard_map/ppermute | solution.py:451
  21.3 2.1 %collective-permute-start.7 = (bf16[2,16,16,512]{3,2,1,0:T(8,128)(2,1)S(1)}, bf16[2,16,16,512]{3,2,1,0:T(8,128)(2,1)S(1)}, u32[]{:S(2)}, u32[]{:S(2)}) collective-permute-start(bf16[2,16,16,512]{3,2,1,0:T(8,128)(2,1)S(1)} %get-tuple-element.45), channel_id=1, source_target_pairs={{0,12},{4,8},{8,4},{12,0},{1,13},{5,9},{9,5},{13,1},{2,14},{6,10},... | collective-permute-start | bytes 1572872 | tf_op jit(solution)/shard_map/ppermute | solution.py:451
  23.4 19.3 %collective-permute-done.5.refs_1_ = bf16[2,16,16,512]{3,2,1,0:T(8,128)(2,1)S(1)} collective-permute-done((bf16[2,16,16,512]{3,2,1,0:T(8,128)(2,1)S(1)}, bf16[2,16,16,512]{3,2,1,0:T(8,128)(2,1)S(1)}, u32[]{:S(2)}, u32[]{:S(2)}) %collective-permute-start.5) | collective-permute-done | bytes 524320 | tf_op jit(solution)/shard_map/ppermute | solution.py:451
  42.6 20.3 %collective-permute-done.6.refs_2_ = bf16[2,16,16,512]{3,2,1,0:T(8,128)(2,1)S(1)} collective-permute-done((bf16[2,16,16,512]{3,2,1,0:T(8,128)(2,1)S(1)}, bf16[2,16,16,512]{3,2,1,0:T(8,128)(2,1)S(1)}, u32[]{:S(2)}, u32[]{:S(2)}) %collective-permute-start.6) | collective-permute-done | bytes 524320 | tf_op jit(solution)/shard_map/ppermute | solution.py:451
  62.9 15.8 %collective-permute-start.8 = (bf16[2,256,512]{2,1,0:T(8,128)(2,1)S(1)}, bf16[2,256,512]{2,1,0:T(8,128)(2,1)S(1)}, u32[]{:S(2)}, u32[]{:S(2)}) collective-permute-start(bf16[2,256,512]{2,1,0:T(8,128)(2,1)S(1)} %hold.2), channel_id=1, source_target_pairs={{0,4},{4,8},{8,12},{12,0},{1,5},{5,9},{9,13},{13,1},{2,6},{6,10},{... | collective-permute-start | bytes 1572872 | tf_op jit(solution)/shard_map/ppermute | solution.py:456
  79.4 8.1 %attend.2 = (bf16[2,512,256]{2,1,0:T(8,128)(2,1)S(1)}, bf16[1024,256]{1,0:T(8,128)(2,1)S(1)}) custom-call(s32[1]{0:T(128)S(6)} %copy.24.len_ref, bf16[512,512]{1,0:T(8,128)(2,1)S(1)} %bitcast.28, bf16[512,512]{1,0:T(8,128)(2,1)S(1)} %bitcast.30, bf16[2,16,16,512]{3,2,1,0:T(8,128)(2,1)S(1)} %get-tuple-element.42.refs_0_, ...), custom_call_target="tpu_custom_call" | custom-call | flops 5368709120 | bytes 4194304 | tf_op jit(solution)/shard_map/attend/pallas_call | solution.py:315
  87.5 1.3 collective-permute-start.19
  88.9 1.5 collective-permute-start.18
  90.3 0.6 collective-permute-start.13
  90.9 8.2 %attend.3 = (bf16[2,512,256]{2,1,0:T(8,128)(2,1)S(1)}, bf16[256,512]{1,0:T(8,128)(2,1)S(1)}, bf16[256,512]{1,0:T(8,128)(2,1)S(1)}, bf16[256,512]{1,0:T(8,128)(2,1)S(1)}, bf16[256,512]{1,0:T(8,128)(2,1)S(1)}) custom-call(s32[1]{0:T(128)S(6)} %copy.24.len_ref, bf16[512,512]{1,0:T(8,128)(2,1)S(1)} %bitcast.29, bf16[512,512]{1,0:T(8,128)(2,1)S(1)} %bitcast.31, ...), custom_call_target="tpu_custom_call" | custom-call | flops 5368709120 | bytes 4194304 | tf_op jit(solution)/shard_map/attend/pallas_call | solution.py:315
  99.2 0.3 collective-permute-done.19.refs_2_.over0.refs_12_.refs_4_
  99.5 0.7 collective-permute-done.18.refs_1_.near0.refs_10_.refs_2_
  100.3 3.0 %collective-permute-done.13.refs_3_ = bf16[2,256,512]{2,1,0:T(8,128)(2,1)S(1)} collective-permute-done((bf16[2,256,512]{2,1,0:T(8,128)(2,1)S(1)}, bf16[2,256,512]{2,1,0:T(8,128)(2,1)S(1)}, u32[]{:S(2)}, u32[]{:S(2)}) %collective-permute-start.13) | collective-permute-done | bytes 524320 | tf_op jit(solution)/shard_map/ppermute | solution.py:456
  103.4 0.6 collective-permute-start.21
  103.9 1.0 collective-permute-start.20
  105.0 0.1 copy.18
  105.1 0.1 reshape.151.place_ref
  105.2 0.1 collective-permute-start.9
  105.2 0.1 collective-permute-start.10
  105.3 4.3 %collective-permute-start.11 = (bf16[256,512]{1,0:T(8,128)(2,1)}, bf16[256,512]{1,0:T(8,128)(2,1)S(1)}, u32[]{:S(2)}, u32[]{:S(2)}) collective-permute-start(bf16[256,512]{1,0:T(8,128)(2,1)} %copy-done.10), channel_id=1, source_target_pairs={{0,12},{4,8},{8,4},{12,0},{1,13},{5,9},{9,5},{13,1},{2,14},{6,10},... | collective-permute-start | bytes 786440 | tf_op jit(solution)/shard_map/ppermute | solution.py:451
  109.6 4.6 %collective-permute-done.21.over1.refs_13_.refs_5_ = bf16[2,512,256]{2,1,0:T(8,128)(2,1)} collective-permute-done((bf16[2,512,256]{2,1,0:T(8,128)(2,1)S(1)}, bf16[2,512,256]{2,1,0:T(8,128)(2,1)}, u32[]{:S(2)}, u32[]{:S(2)}) %collective-permute-start.21) | collective-permute-done | bytes 524320 | tf_op jit(solution)/shard_map/ppermute | solution.py:451
  114.2 1.3 join.1
  115.4 1.8 collective-permute-start.22
  117.3 4.9 %weight_parts.2 = (f32[4,512,512]{2,1,0:T(8,128)S(1)}, bf16[4,512,512]{2,1,0:T(8,128)(2,1)S(1)}) custom-call(s32[16]{0:T(128)S(1)} %reshape.151.place_ref, bf16[512,512]{1,0:T(8,128)(2,1)S(1)} %bitcast.25, bf16[2,512,256]{2,1,0:T(8,128)(2,1)S(1)} %copy-done.4, bf16[2,512,256]{2,1,0:T(8,128)(2,1)S(1)} %hold.3.refs_9_.refs_1_, ...), custom_call_target="tpu_custom_call" | custom-call | flops 6442450944 | bytes 6291456 | tf_op jit(solution)/shard_map/weight_parts/pallas_call | solution.py:370
  122.3 1.8 collective-permute-done.10.refs_2_.refs_5_
  124.1 0.7 collective-permute-done.22.refs_14_.refs_0_
  124.8 1.6 collective-permute-done.23.refs_15_.refs_1_
  126.4 2.3 %weight_parts.3 = (f32[4,512,512]{2,1,0:T(8,128)S(1)}, bf16[4,512,512]{2,1,0:T(8,128)(2,1)S(1)}) custom-call(s32[16]{0:T(128)S(1)} %reshape.151.place_ref, bf16[512,512]{1,0:T(8,128)(2,1)S(1)} %bitcast.26, bf16[2,512,256]{2,1,0:T(8,128)(2,1)S(1)} %collective-permute-done.22.refs_14_.refs_0_, ...), custom_call_target="tpu_custom_call", output_to_operand_aliasing={{0}: (4, {}), {1}: (5, {})} | custom-call | flops 2147483648 | bytes 6291456 | tf_op jit(solution)/shard_map/weight_parts/pallas_call | solution.py:370
  128.8 0.1 collective-permute-start.24
  128.8 0.5 collective-permute-start.14
  129.3 0.1 collective-permute-start.15
  129.6 0.5 collective-permute-start.12
  130.1 0.1 collective-permute-start.16
  130.1 2.8 %collective-permute-done.24.got_ref = bf16[4,512,512]{2,1,0:T(8,128)(2,1)S(1)} collective-permute-done((bf16[4,512,512]{2,1,0:T(8,128)(2,1)S(1)}, bf16[4,512,512]{2,1,0:T(8,128)(2,1)S(1)}, u32[]{:S(2)}, u32[]{:S(2)}) %collective-permute-start.24) | collective-permute-done | bytes 2097184 | tf_op jit(solution)/shard_map/ppermute | solution.py:451
  133.0 0.1 collective-permute-start.17
  133.1 0.3 combine.1
  133.5 0.3 collective-permute-done.14.refs_4_
  133.7 0.1 collective-permute-start.25
  133.8 0.6 collective-permute-done.15.refs_5_
  134.5 2.5 %collective-permute-start.26 = (bf16[512,512]{1,0:T(8,128)(2,1)S(1)}, bf16[512,512]{1,0:T(8,128)(2,1)S(1)}, u32[]{:S(2)}, u32[]{:S(2)}) collective-permute-start(bf16[512,512]{1,0:T(8,128)(2,1)S(1)} %get-tuple-element.61), channel_id=1, source_target_pairs={{0,8},{4,12},{8,0},{12,4},{1,9},{5,13},{9,1},{13,5},{2,10},{6,14},... | collective-permute-start | bytes 1572872 | tf_op jit(solution)/shard_map/ppermute | solution.py:451
  137.0 1.1 collective-permute-start.27
  138.1 3.4 %unpack_query_grads.1 = bf16[64,8,512]{2,1,0:T(8,128)(2,1)} custom-call(s32[128]{0:T(128)S(1)} %get-tuple-element.33.table_ref, bf16[256,512]{1,0:T(8,128)(2,1)S(1)} %get-tuple-element.47.refs_0_, bf16[256,512]{1,0:T(8,128)(2,1)S(1)} %collective-permute-done.9.refs_1_.refs_4_, bf16[256,512]{1,0:T(8,128)(2,1)S(1)} %collective-permute-done.10.refs_2_.refs_5_, ...), custom_call_target="tpu_custom_call" | custom-call | bytes 3145728 | tf_op jit(solution)/shard_map/unpack_query_grads/pallas_call | solution.py:208
  141.6 5.4 %state_grads.1 = bf16[512,512]{1,0:T(8,128)(2,1)} custom-call(s32[8]{0:T(128)S(1)} %fusion.2.order_ref, bf16[2,256,512]{2,1,0:T(8,128)(2,1)S(1)} %bitcast.24, bf16[2,256,512]{2,1,0:T(8,128)(2,1)S(1)} %collective-permute-done.4.refs_8_.refs_0_.refs_1_, bf16[2,256,512]{2,1,0:T(8,128)(2,1)S(1)} %copy-done.2, ...), custom_call_target="tpu_custom_call" | custom-call | flops 2147483648 | bytes 8388608 | tf_op jit(solution)/shard_map/state_grads/pallas_call | solution.py:433
  147.0 3.4 %collective-permute-done.25 = bf16[512,512]{1,0:T(8,128)(2,1)S(1)} collective-permute-done((bf16[512,512]{1,0:T(8,128)(2,1)S(1)}, bf16[512,512]{1,0:T(8,128)(2,1)S(1)}, u32[]{:S(2)}, u32[]{:S(2)}) %collective-permute-start.25) | collective-permute-done | bytes 524320 | tf_op jit(solution)/shard_map/ppermute | solution.py:451
  150.4 32.2 %collective-permute-done.26 = bf16[512,512]{1,0:T(8,128)(2,1)S(1)} collective-permute-done((bf16[512,512]{1,0:T(8,128)(2,1)S(1)}, bf16[512,512]{1,0:T(8,128)(2,1)S(1)}, u32[]{:S(2)}, u32[]{:S(2)}) %collective-permute-start.26) | collective-permute-done | bytes 524320 | tf_op jit(solution)/shard_map/ppermute | solution.py:451
  182.7 0.3 add_add_fusion
  183.0 1.8 copy.19
  (44 shorter events, 0.4 us)
Async XLA Ops:
  1.7 17.0 %collective-permute-start.4 = (bf16[2,256,512]{2,1,0:T(8,128)(2,1)S(1)}, bf16[2,256,512]{2,1,0:T(8,128)(2,1)S(1)}, u32[]{:S(2)}, u32[]{:S(2)}) collective-permute-start(bf16[2,256,512]{2,1,0:T(8,128)(2,1)S(1)} %bitcast.22), channel_id=1, source_target_pairs={{0,4},{4,8},{8,12},{12,0},{1,5},{5,9},{9,13},{13,1},{2,6},{6,10},{... | collective-permute-start | bytes 1572872 | tf_op jit(solution)/shard_map/ppermute | solution.py:456
  4.8 1.0 copy-start.5
  5.8 1.0 copy-start.6
  6.9 0.7 copy-start.7
  9.5 1.6 collective-permute-start
  9.5 1.9 %collective-permute-start.1 = (bf16[16,16,512]{2,1,0:T(8,128)(2,1)S(1)}, bf16[16,16,512]{2,1,0:T(8,128)(2,1)S(1)}, u32[]{:S(2)}, u32[]{:S(2)}) collective-permute-start(bf16[16,16,512]{2,1,0:T(8,128)(2,1)S(1)} %get-tuple-element.39), channel_id=1, source_target_pairs={{0,16},{16,0},{1,17},{17,1},{2,18},{18,2},{3,19},{19,3},{4,20},{20... | collective-permute-start | bytes 786440 | tf_op jit(solution)/shard_map/ppermute | solution.py:451
  10.0 1.8 collective-permute-start.2
  10.1 2.1 %collective-permute-start.3 = (bf16[16,16,512]{2,1,0:T(8,128)(2,1)S(1)}, bf16[16,16,512]{2,1,0:T(8,128)(2,1)S(1)}, u32[]{:S(2)}, u32[]{:S(2)}) collective-permute-start(bf16[16,16,512]{2,1,0:T(8,128)(2,1)S(1)} %get-tuple-element.41), channel_id=1, source_target_pairs={{0,16},{16,0},{1,17},{17,1},{2,18},{18,2},{3,19},{19,3},{4,20},{20... | collective-permute-start | bytes 786440 | tf_op jit(solution)/shard_map/ppermute | solution.py:451
  18.8 60.6 %copy-start.8 = (bf16[1,512,512]{2,1,0:T(8,128)(2,1)S(1)}, bf16[1,512,512]{2,1,0:T(8,128)(2,1)}, u32[]{:S(2)}) copy-start(bf16[1,512,512]{2,1,0:T(8,128)(2,1)} %param.11) | copy-start | bytes 1572868
  18.8 60.6 %copy-start.9 = (bf16[1,512,512]{2,1,0:T(8,128)(2,1)S(1)}, bf16[1,512,512]{2,1,0:T(8,128)(2,1)}, u32[]{:S(2)}) copy-start(bf16[1,512,512]{2,1,0:T(8,128)(2,1)} %param.12) | copy-start | bytes 1572868
  18.9 23.7 %collective-permute-start.5 = (bf16[2,16,16,512]{3,2,1,0:T(8,128)(2,1)S(1)}, bf16[2,16,16,512]{3,2,1,0:T(8,128)(2,1)S(1)}, u32[]{:S(2)}, u32[]{:S(2)}) collective-permute-start(bf16[2,16,16,512]{3,2,1,0:T(8,128)(2,1)S(1)} %get-tuple-element.43), channel_id=1, source_target_pairs={{0,4},{4,0},{8,12},{12,8},{1,5},{5,1},{9,13},{13,9},{2,6},{6,2},{1... | collective-permute-start | bytes 1572872 | tf_op jit(solution)/shard_map/ppermute | solution.py:451
  19.0 43.9 %collective-permute-start.6 = (bf16[2,16,16,512]{3,2,1,0:T(8,128)(2,1)S(1)}, bf16[2,16,16,512]{3,2,1,0:T(8,128)(2,1)S(1)}, u32[]{:S(2)}, u32[]{:S(2)}) collective-permute-start(bf16[2,16,16,512]{3,2,1,0:T(8,128)(2,1)S(1)} %get-tuple-element.44), channel_id=1, source_target_pairs={{0,8},{4,12},{8,0},{12,4},{1,9},{5,13},{9,1},{13,5},{2,10},{6,14},... | collective-permute-start | bytes 1572872 | tf_op jit(solution)/shard_map/ppermute | solution.py:451
  21.3 41.6 %collective-permute-start.7 = (bf16[2,16,16,512]{3,2,1,0:T(8,128)(2,1)S(1)}, bf16[2,16,16,512]{3,2,1,0:T(8,128)(2,1)S(1)}, u32[]{:S(2)}, u32[]{:S(2)}) collective-permute-start(bf16[2,16,16,512]{3,2,1,0:T(8,128)(2,1)S(1)} %get-tuple-element.45), channel_id=1, source_target_pairs={{0,12},{4,8},{8,4},{12,0},{1,13},{5,9},{9,5},{13,1},{2,14},{6,10},... | collective-permute-start | bytes 1572872 | tf_op jit(solution)/shard_map/ppermute | solution.py:451
  62.9 27.4 %collective-permute-start.8 = (bf16[2,256,512]{2,1,0:T(8,128)(2,1)S(1)}, bf16[2,256,512]{2,1,0:T(8,128)(2,1)S(1)}, u32[]{:S(2)}, u32[]{:S(2)}) collective-permute-start(bf16[2,256,512]{2,1,0:T(8,128)(2,1)S(1)} %hold.2), channel_id=1, source_target_pairs={{0,4},{4,8},{8,12},{12,0},{1,5},{5,9},{9,13},{13,1},{2,6},{6,10},{... | collective-permute-start | bytes 1572872 | tf_op jit(solution)/shard_map/ppermute | solution.py:456
  87.5 11.7 %copy-start.3 = (bf16[2,512,256]{2,1,0:T(8,128)(2,1)}, bf16[2,512,256]{2,1,0:T(8,128)(2,1)S(1)}, u32[]{:S(2)}) copy-start(bf16[2,512,256]{2,1,0:T(8,128)(2,1)S(1)} %get-tuple-element.51.refs_8_.refs_0_) | copy-start | bytes 1572868
  87.5 12.0 %collective-permute-start.19 = (bf16[2,512,256]{2,1,0:T(8,128)(2,1)S(1)}, bf16[2,512,256]{2,1,0:T(8,128)(2,1)S(1)}, u32[]{:S(2)}, u32[]{:S(2)}) collective-permute-start(bf16[2,512,256]{2,1,0:T(8,128)(2,1)S(1)} %get-tuple-element.51.refs_8_.refs_0_), channel_id=1, source_target_pairs={{0,2},{1,3},{2,0},{3,1},{4,6},{5,7},{6,4},{7,5},{8,10},{9,11},{10,... | collective-permute-start | bytes 1572872 | tf_op jit(solution)/shard_map/ppermute | solution.py:451
  88.9 11.4 %collective-permute-start.18 = (bf16[2,512,256]{2,1,0:T(8,128)(2,1)S(1)}, bf16[2,512,256]{2,1,0:T(8,128)(2,1)S(1)}, u32[]{:S(2)}, u32[]{:S(2)}) collective-permute-start(bf16[2,512,256]{2,1,0:T(8,128)(2,1)S(1)} %get-tuple-element.51.refs_8_.refs_0_), channel_id=1, source_target_pairs={{0,1},{1,0},{2,3},{3,2},{4,5},{5,4},{6,7},{7,6},{8,9},{9,8},{10,11... | collective-permute-start | bytes 1572872 | tf_op jit(solution)/shard_map/ppermute | solution.py:451
  90.3 8.9 %copy-start.1 = (bf16[2,256,512]{2,1,0:T(8,128)(2,1)}, bf16[2,256,512]{2,1,0:T(8,128)(2,1)S(1)}, u32[]{:S(2)}) copy-start(bf16[2,256,512]{2,1,0:T(8,128)(2,1)S(1)} %collective-permute-done.8.refs_2_) | copy-start | bytes 1572868
  90.3 13.0 %collective-permute-start.13 = (bf16[2,256,512]{2,1,0:T(8,128)(2,1)S(1)}, bf16[2,256,512]{2,1,0:T(8,128)(2,1)S(1)}, u32[]{:S(2)}, u32[]{:S(2)}) collective-permute-start(bf16[2,256,512]{2,1,0:T(8,128)(2,1)S(1)} %collective-permute-done.8.refs_2_), channel_id=1, source_target_pairs={{0,4},{4,8},{8,12},{12,0},{1,5},{5,9},{9,13},{13,1},{2,6},{6,10},{... | collective-permute-start | bytes 1572872 | tf_op jit(solution)/shard_map/ppermute | solution.py:456
  99.2 4.1 %copy-start.10 = (bf16[256,512]{1,0:T(8,128)(2,1)}, bf16[256,512]{1,0:T(8,128)(2,1)S(1)}, u32[]{:S(2)}) copy-start(bf16[256,512]{1,0:T(8,128)(2,1)S(1)} %get-tuple-element.50) | copy-start | bytes 786436
  99.2 4.7 %copy-start.11 = (bf16[256,512]{1,0:T(8,128)(2,1)}, bf16[256,512]{1,0:T(8,128)(2,1)S(1)}, u32[]{:S(2)}) copy-start(bf16[256,512]{1,0:T(8,128)(2,1)S(1)} %get-tuple-element.49) | copy-start | bytes 786436
  99.2 4.7 %copy-start.12 = (bf16[256,512]{1,0:T(8,128)(2,1)}, bf16[256,512]{1,0:T(8,128)(2,1)S(1)}, u32[]{:S(2)}) copy-start(bf16[256,512]{1,0:T(8,128)(2,1)S(1)} %get-tuple-element.48) | copy-start | bytes 786436
  103.4 10.8 %collective-permute-start.21 = (bf16[2,512,256]{2,1,0:T(8,128)(2,1)S(1)}, bf16[2,512,256]{2,1,0:T(8,128)(2,1)}, u32[]{:S(2)}, u32[]{:S(2)}) collective-permute-start(bf16[2,512,256]{2,1,0:T(8,128)(2,1)S(1)} %hold.3.refs_9_.refs_1_), channel_id=1, source_target_pairs={{0,2},{1,3},{2,0},{3,1},{4,6},{5,7},{6,4},{7,5},{8,10},{9,11},{10,... | collective-permute-start | bytes 1572872 | tf_op jit(solution)/shard_map/ppermute | solution.py:451
  103.9 10.2 %collective-permute-start.20 = (bf16[2,512,256]{2,1,0:T(8,128)(2,1)S(1)}, bf16[2,512,256]{2,1,0:T(8,128)(2,1)}, u32[]{:S(2)}, u32[]{:S(2)}) collective-permute-start(bf16[2,512,256]{2,1,0:T(8,128)(2,1)S(1)} %hold.3.refs_9_.refs_1_), channel_id=1, source_target_pairs={{0,1},{1,0},{2,3},{3,2},{4,5},{5,4},{6,7},{7,6},{8,9},{9,8},{10,11... | collective-permute-start | bytes 1572872 | tf_op jit(solution)/shard_map/ppermute | solution.py:451
  105.2 12.2 %copy-start = (bf16[1,512,512]{2,1,0:T(8,128)(2,1)S(1)}, bf16[1,512,512]{2,1,0:T(8,128)(2,1)}, u32[]{:S(2)}) copy-start(bf16[1,512,512]{2,1,0:T(8,128)(2,1)} %param.13) | copy-start | bytes 1572868
  105.2 12.2 %copy-start.4 = (bf16[2,512,256]{2,1,0:T(8,128)(2,1)S(1)}, bf16[2,512,256]{2,1,0:T(8,128)(2,1)}, u32[]{:S(2)}) copy-start(bf16[2,512,256]{2,1,0:T(8,128)(2,1)} %copy-done.3) | copy-start | bytes 1572868
  105.2 17.1 %collective-permute-start.9 = (bf16[256,512]{1,0:T(8,128)(2,1)}, bf16[256,512]{1,0:T(8,128)(2,1)S(1)}, u32[]{:S(2)}, u32[]{:S(2)}) collective-permute-start(bf16[256,512]{1,0:T(8,128)(2,1)} %copy-done.12), channel_id=1, source_target_pairs={{0,4},{4,0},{8,12},{12,8},{1,5},{5,1},{9,13},{13,9},{2,6},{6,2},{1... | collective-permute-start | bytes 786440 | tf_op jit(solution)/shard_map/ppermute | solution.py:451
  105.2 18.9 %collective-permute-start.10 = (bf16[256,512]{1,0:T(8,128)(2,1)}, bf16[256,512]{1,0:T(8,128)(2,1)S(1)}, u32[]{:S(2)}, u32[]{:S(2)}) collective-permute-start(bf16[256,512]{1,0:T(8,128)(2,1)} %copy-done.11), channel_id=1, source_target_pairs={{0,8},{4,12},{8,0},{12,4},{1,9},{5,13},{9,1},{13,5},{2,10},{6,14},... | collective-permute-start | bytes 786440 | tf_op jit(solution)/shard_map/ppermute | solution.py:451
  105.3 18.8 %collective-permute-start.11 = (bf16[256,512]{1,0:T(8,128)(2,1)}, bf16[256,512]{1,0:T(8,128)(2,1)S(1)}, u32[]{:S(2)}, u32[]{:S(2)}) collective-permute-start(bf16[256,512]{1,0:T(8,128)(2,1)} %copy-done.10), channel_id=1, source_target_pairs={{0,12},{4,8},{8,4},{12,0},{1,13},{5,9},{9,5},{13,1},{2,14},{6,10},... | collective-permute-start | bytes 786440 | tf_op jit(solution)/shard_map/ppermute | solution.py:451
  115.4 9.4 %collective-permute-start.22 = (bf16[2,512,256]{2,1,0:T(8,128)(2,1)S(1)}, bf16[2,512,256]{2,1,0:T(8,128)(2,1)S(1)}, u32[]{:S(2)}, u32[]{:S(2)}) collective-permute-start(bf16[2,512,256]{2,1,0:T(8,128)(2,1)S(1)} %get-tuple-element.53), channel_id=1, source_target_pairs={{0,2},{1,3},{2,0},{3,1},{4,6},{5,7},{6,4},{7,5},{8,10},{9,11},{10,... | collective-permute-start | bytes 1572872 | tf_op jit(solution)/shard_map/ppermute | solution.py:451
  117.3 9.2 %collective-permute-start.23 = (bf16[2,512,256]{2,1,0:T(8,128)(2,1)S(1)}, bf16[2,512,256]{2,1,0:T(8,128)(2,1)S(1)}, u32[]{:S(2)}, u32[]{:S(2)}) collective-permute-start(bf16[2,512,256]{2,1,0:T(8,128)(2,1)S(1)} %get-tuple-element.54), channel_id=1, source_target_pairs={{0,1},{1,0},{2,3},{3,2},{4,5},{5,4},{6,7},{7,6},{8,9},{9,8},{10,11... | collective-permute-start | bytes 1572872 | tf_op jit(solution)/shard_map/ppermute | solution.py:451
  128.7 1.3 copy-start.2
  128.8 4.2 %collective-permute-start.24 = (bf16[4,512,512]{2,1,0:T(8,128)(2,1)S(1)}, bf16[4,512,512]{2,1,0:T(8,128)(2,1)S(1)}, u32[]{:S(2)}, u32[]{:S(2)}) collective-permute-start(bf16[4,512,512]{2,1,0:T(8,128)(2,1)S(1)} %get-tuple-element.58), channel_id=1, source_target_pairs={{0,16},{16,0},{1,17},{17,1},{2,18},{18,2},{3,19},{19,3},{4,20},{20... | collective-permute-start | bytes 6291464 | tf_op jit(solution)/shard_map/ppermute | solution.py:451
  128.8 4.9 %collective-permute-start.14 = (bf16[2,256,512]{2,1,0:T(8,128)(2,1)S(1)}, bf16[2,256,512]{2,1,0:T(8,128)(2,1)S(1)}, u32[]{:S(2)}, u32[]{:S(2)}) collective-permute-start(bf16[2,256,512]{2,1,0:T(8,128)(2,1)S(1)} %bitcast.23), channel_id=1, source_target_pairs={{0,16},{16,0},{1,17},{17,1},{2,18},{18,2},{3,19},{19,3},{4,20},{20... | collective-permute-start | bytes 1572872 | tf_op jit(solution)/shard_map/ppermute | solution.py:451
  129.3 5.1 %collective-permute-start.15 = (bf16[2,256,512]{2,1,0:T(8,128)(2,1)S(1)}, bf16[2,256,512]{2,1,0:T(8,128)(2,1)S(1)}, u32[]{:S(2)}, u32[]{:S(2)}) collective-permute-start(bf16[2,256,512]{2,1,0:T(8,128)(2,1)S(1)} %collective-permute-done.4.refs_8_.refs_0_.refs_1_), channel_id=1, source_target_pairs={{0,16},{16,0},{1,17},{17,1},{2,18},{18,2},{3,19},{19,3},{4,20},{20... | collective-permute-start | bytes 1572872 | tf_op jit(solution)/shard_map/ppermute | solution.py:451
  129.6 7.4 %collective-permute-start.12 = (bf16[4,128,512]{2,1,0:T(8,128)(2,1)S(1)}, bf16[4,128,512]{2,1,0:T(8,128)(2,1)S(1)}, u32[]{:S(2)}, u32[]{:S(2)}) collective-permute-start(bf16[4,128,512]{2,1,0:T(8,128)(2,1)S(1)} %pad_maximum_fusion), channel_id=1, source_target_pairs={{0,16},{16,0},{1,17},{17,1},{2,18},{18,2},{3,19},{19,3},{4,20},{20... | collective-permute-start | bytes 1572872 | tf_op jit(solution)/shard_map/ppermute | solution.py:451
  130.1 11.5 %collective-permute-start.16 = (bf16[2,256,512]{2,1,0:T(8,128)(2,1)S(1)}, bf16[2,256,512]{2,1,0:T(8,128)(2,1)S(1)}, u32[]{:S(2)}, u32[]{:S(2)}) collective-permute-start(bf16[2,256,512]{2,1,0:T(8,128)(2,1)S(1)} %copy-done.2), channel_id=1, source_target_pairs={{0,16},{16,0},{1,17},{17,1},{2,18},{18,2},{3,19},{19,3},{4,20},{20... | collective-permute-start | bytes 1572872 | tf_op jit(solution)/shard_map/ppermute | solution.py:451
  133.0 8.6 %collective-permute-start.17 = (bf16[2,256,512]{2,1,0:T(8,128)(2,1)S(1)}, bf16[2,256,512]{2,1,0:T(8,128)(2,1)S(1)}, u32[]{:S(2)}, u32[]{:S(2)}) collective-permute-start(bf16[2,256,512]{2,1,0:T(8,128)(2,1)S(1)} %collective-permute-done.13.refs_3_), channel_id=1, source_target_pairs={{0,16},{16,0},{1,17},{17,1},{2,18},{18,2},{3,19},{19,3},{4,20},{20... | collective-permute-start | bytes 1572872 | tf_op jit(solution)/shard_map/ppermute | solution.py:451
  133.7 16.7 %collective-permute-start.25 = (bf16[512,512]{1,0:T(8,128)(2,1)S(1)}, bf16[512,512]{1,0:T(8,128)(2,1)S(1)}, u32[]{:S(2)}, u32[]{:S(2)}) collective-permute-start(bf16[512,512]{1,0:T(8,128)(2,1)S(1)} %get-tuple-element.60), channel_id=1, source_target_pairs={{0,12},{4,8},{8,4},{12,0},{1,13},{5,9},{9,5},{13,1},{2,14},{6,10},... | collective-permute-start | bytes 1572872 | tf_op jit(solution)/shard_map/ppermute | solution.py:451
  134.5 48.2 %collective-permute-start.26 = (bf16[512,512]{1,0:T(8,128)(2,1)S(1)}, bf16[512,512]{1,0:T(8,128)(2,1)S(1)}, u32[]{:S(2)}, u32[]{:S(2)}) collective-permute-start(bf16[512,512]{1,0:T(8,128)(2,1)S(1)} %get-tuple-element.61), channel_id=1, source_target_pairs={{0,8},{4,12},{8,0},{12,4},{1,9},{5,13},{9,1},{13,5},{2,10},{6,14},... | collective-permute-start | bytes 1572872 | tf_op jit(solution)/shard_map/ppermute | solution.py:451
  137.0 45.7 %collective-permute-start.27 = (bf16[512,512]{1,0:T(8,128)(2,1)S(1)}, bf16[512,512]{1,0:T(8,128)(2,1)S(1)}, u32[]{:S(2)}, u32[]{:S(2)}) collective-permute-start(bf16[512,512]{1,0:T(8,128)(2,1)S(1)} %get-tuple-element.62), channel_id=1, source_target_pairs={{0,4},{4,0},{8,12},{12,8},{1,5},{5,1},{9,13},{13,9},{2,6},{6,2},{1... | collective-permute-start | bytes 1572872 | tf_op jit(solution)/shard_map/ppermute | solution.py:451
